TPU v7x, 256 devices: a whole 4x4x8 slice. The times are simulated.
256 devices in a mesh: dp: 4 (over y), mp: 64 (over z, x, core).
Axes of the slice: x: 4, y: 4, z: 8, core: 2. Of those that a mesh axis runs over, the one named last changes fastest.
Arguments:
- queries: bfloat16 [3, 2048, 4096], P(None, 'dp', 'mp'), may hold values from -15 to 15
- memory: bfloat16 [1024, 4096], P('mp'), may hold values from -6 to 6
- w_key: bfloat16 [3, 4096, 4096], P(None, 'mp'), may hold values from -0.09375 to 0.09375
- w_value: bfloat16 [3, 4096, 4096], P(None, 'mp'), may hold values from -0.09375 to 0.09375
- grad_out: bfloat16 [3, 2048, 4096], P(None, 'dp', 'mp'), may hold values from -6 to 6
Outputs:
- attended: bfloat16 [3, 2048, 4096], P(None, 'dp', 'mp')
- grad_queries: bfloat16 [3, 2048, 4096], P(None, 'dp', 'mp')
- grad_memory: float32 [1024, 4096], P('mp')
- grad_w_key: float32 [3, 4096, 4096], P(None, 'mp')
- grad_w_value: float32 [3, 4096, 4096], P(None, 'mp')
All inputs are finite; a program needn't handle non-finite values.
Results may differ from a plain program's by a relative error of at most 0.025.
Values may be sent and summed in bfloat16 or wider, within the bound.
No kernel may reach another device: no remote copies, remote signals or barrier semaphores. Data moves between devices by JAX's collectives and lax.ppermute only.
A program may use at most 128 MiB of HBM per device.

v0:
```python
import jax
import jax.numpy as jnp
from jax import lax
from jax.sharding import PartitionSpec as P

HEAD_WIDTH = 64


def shards(queries, memory, w_key, w_value, grad_out):
    layers, rows, width = queries.shape
    heads_dev = width // HEAD_WIDTH
    mem_all = lax.all_gather(memory, "mp", axis=0, tiled=True)
    mem_total = mem_all.shape[0]
    keys = jnp.einsum("md,lcd->lmc", mem_all, w_key, preferred_element_type=jnp.float32).astype(
        jnp.bfloat16
    )
    values = jnp.einsum("md,lcd->lmc", mem_all, w_value, preferred_element_type=jnp.float32).astype(
        jnp.bfloat16
    )
    per_head_queries = queries.reshape(layers, rows, heads_dev, HEAD_WIDTH)
    per_head_keys = keys.reshape(layers, mem_total, heads_dev, HEAD_WIDTH)
    per_head_values = values.reshape(layers, mem_total, heads_dev, HEAD_WIDTH)
    head_output_gradient = grad_out.reshape(layers, rows, heads_dev, HEAD_WIDTH)
    attention_logits = jnp.einsum(
        "lrhd,lmhd->lhrm", per_head_queries, per_head_keys, preferred_element_type=jnp.float32
    )
    row_max = jnp.max(attention_logits, axis=-1, keepdims=True)
    exp_scores = jnp.exp(attention_logits - row_max)
    attn_probs = exp_scores / jnp.sum(exp_scores, axis=-1, keepdims=True)
    batch_probabilities = attn_probs.astype(jnp.bfloat16)
    attended = (
        jnp.einsum(
            "lhrm,lmhd->lrhd",
            batch_probabilities,
            per_head_values,
            preferred_element_type=jnp.float32,
        )
        .reshape(layers, rows, width)
        .astype(jnp.bfloat16)
    )
    probability_gradient = jnp.einsum(
        "lrhd,lmhd->lhrm", head_output_gradient, per_head_values, preferred_element_type=jnp.float32
    )
    row_delta = jnp.sum(attn_probs * probability_gradient, axis=-1, keepdims=True)
    logit_gradient = (attn_probs * (probability_gradient - row_delta)).astype(jnp.bfloat16)
    grad_queries = (
        jnp.einsum(
            "lhrm,lmhd->lrhd", logit_gradient, per_head_keys, preferred_element_type=jnp.float32
        )
        .reshape(layers, rows, width)
        .astype(jnp.bfloat16)
    )
    key_part = jnp.einsum(
        "lhrm,lrhd->lmhd", logit_gradient, per_head_queries, preferred_element_type=jnp.float32
    ).reshape(layers, mem_total, width)
    value_part = jnp.einsum(
        "lhrm,lrhd->lmhd",
        batch_probabilities,
        head_output_gradient,
        preferred_element_type=jnp.float32,
    ).reshape(layers, mem_total, width)
    key_sum, value_sum = lax.psum((key_part, value_part), "dp")
    key_gradient = key_sum.astype(jnp.bfloat16)
    value_gradient = value_sum.astype(jnp.bfloat16)
    grad_w_key = jnp.einsum(
        "lmc,md->lcd", key_gradient, mem_all, preferred_element_type=jnp.float32
    )
    grad_w_value = jnp.einsum(
        "lmc,md->lcd", value_gradient, mem_all, preferred_element_type=jnp.float32
    )
    grad_memory = lax.psum_scatter(
        jnp.einsum("lmc,lcd->md", key_gradient, w_key, preferred_element_type=jnp.float32)
        + jnp.einsum("lmc,lcd->md", value_gradient, w_value, preferred_element_type=jnp.float32),
        "mp",
        scatter_dimension=0,
        tiled=True,
    )
    return (attended, grad_queries, grad_memory, grad_w_key, grad_w_value)


def solution(mesh):
    return jax.shard_map(
        shards,
        mesh=mesh,
        in_specs=(
            P(None, "dp", "mp"),
            P("mp", None),
            P(None, "mp", None),
            P(None, "mp", None),
            P(None, "dp", "mp"),
        ),
        out_specs=(
            P(None, "dp", "mp"),
            P(None, "dp", "mp"),
            P("mp", None),
            P(None, "mp", None),
            P(None, "mp", None),
        ),
        check_vma=False,
    )
```

profile of v0, /device:TPU:32, one launch (start us, length us, event | category | flops | bytes accessed | tf_op | source)
XLA Modules:
  0.0 364.1 jit_solution(14707447586563638420)
XLA Ops:
  7.2 0.0 copy-start
  7.2 0.0 all-gather.2.cloned.1.call-start
  7.2 0.7 all-gather.2.cloned.1.call-update
  7.9 0.0 copy-start.5
  7.9 0.0 reduce-scatter.2.cloned.1.call-start
  8.0 88.5 %all-gather.2.cloned.1.call-done = bf16[1024,4096]{1,0:T(8,128)(2,1)} async-done(((bf16[16,4096]{1,0:T(8,128)(2,1)}), bf16[1024,4096]{1,0:T(8,128)(2,1)}) %all-gather.2.cloned.1.call-update) | async-done | bytes 8388624 | tf_op jit(solution)/shard_map/all_gather | solution.py:12
  96.5 0.0 copy-done
  96.5 6.3 %fusion.23 = bf16[3,64,1024]{2,1,0:T(8,128)(2,1)S(1)} fusion(bf16[3,64,4096]{2,1,0:T(8,128)(2,1)S(1)} %copy-done, bf16[1024,4096]{1,0:T(8,128)(2,1)} %all-gather.2.cloned.1.call-done), kind=kOutput, calls=%fused_computation.25 | convolution fusion | flops 1610809344 | bytes 10354688 | tf_op jit(solution)/shard_map/md,lcd->lmc/dot_general | solution.py:14
  102.7 0.0 copy-done.5
  102.7 4.7 %fusion.56 = (f32[3,512]{1,0:T(4,128)S(1)}, f32[3,512,1024]{1,2,0:T(8,128)}) fusion(bf16[3,64,1024]{2,1,0:T(8,128)(2,1)S(1)} %fusion.23, bf16[3,512,64]{1,2,0:T(8,128)(2,1)S(1)} %copy-done.5), kind=kOutput, calls=%fused_computation.36 | convolution fusion | flops 204473344 | bytes 6887424 | tf_op jit(solution)/shard_map/sub | solution.py:28
  107.5 4.7 %fusion.16 = f32[3,1024,64]{1,2,0:T(8,128)} fusion(bf16[3,512,64]{1,2,0:T(8,128)(2,1)} %param.9, f32[3,512]{1,0:T(4,128)S(1)} %get-tuple-element.7, bf16[3,64,1024]{2,1,0:T(8,128)(2,1)S(1)} %fusion.23, bf16[3,512,64]{1,2,0:T(8,128)(2,1)} %param.5), kind=kOutput, calls=%fused_computation.20 | convolution fusion | flops 407374336 | bytes 1579008 | tf_op jit(solution)/shard_map/lhrm,lrhd->lmhd/dot_general | solution.py:56
  112.2 6.4 %fusion.20 = bf16[3,64,1024]{2,1,0:T(8,128)(2,1)S(1)} fusion(bf16[3,64,4096]{2,1,0:T(8,128)(2,1)S(1)} %copy-done.4, bf16[1024,4096]{1,0:T(8,128)(2,1)} %all-gather.2.cloned.1.call-done), kind=kOutput, calls=%fused_computation.24 | convolution fusion | flops 1610809344 | bytes 10354688 | tf_op jit(solution)/shard_map/md,lcd->lmc/dot_general | solution.py:17
  118.7 1.0 fusion.9
  119.7 0.0 copy-done.9
  119.7 0.0 copy-start.6
  119.7 1.8 fusion.11
  121.5 0.0 copy-start.2
  121.5 1.7 copy-done.2
  123.2 1.1 fusion.57
  124.2 36.7 %all-reduce.2 = (bf16[3,1024,64]{1,2,0:T(8,128)(2,1)S(1)}, bf16[3,1024,64]{1,2,0:T(8,128)(2,1)S(1)}) all-reduce(f32[3,1024,64]{1,2,0:T(8,128)S(1)} %fusion.57, f32[3,1024,64]{1,2,0:T(8,128)} %fusion.16), channel_id=1, replica_groups=mesh['dp'=4,'mp'=64] {'dp'}, use_global_device_ids=true, to_apply=%region_3.0 | all-reduce | flops 393216 | bytes 2359296 | tf_op jit(solution)/shard_map/psum | solution.py:62
  161.0 2.4 fusion.58
  163.4 9.6 %bitcast_add_fusion = f32[1024,4096]{1,0:T(8,128)} fusion(f32[1024,4096,1]{1,0,2:T(8,128)S(1)} %fusion.58, bf16[3,64,4096]{2,1,0:T(8,128)(2,1)} %param.8, bf16[3,1024,64]{1,2,0:T(8,128)(2,1)S(1)} %get-tuple-element.6), kind=kOutput, calls=%fused_computation.1 | convolution fusion | flops 1614807040 | bytes 35520512 | tf_op jit(solution)/shard_map/lmc,lcd->md/dot_general | solution.py:73
  172.9 0.0 reduce-scatter.2.cloned.1.call-update
  172.9 0.9 copy-done.7
  173.8 0.2 copy-done.10
  174.0 3.1 fusion.29
  177.2 3.4 fusion.32
  180.5 7.4 %fusion.3 = f32[3,64,4096]{2,1,0:T(8,128)} fusion(bf16[1024,4096]{1,0:T(8,128)(2,1)} %all-gather.2.cloned.1.call-done, bf16[3,1024,64]{1,2,0:T(8,128)(2,1)S(1)} %get-tuple-element.5), kind=kOutput, calls=%fused_computation.4 | convolution fusion | flops 1610612736 | bytes 11927552 | tf_op jit(solution)/shard_map/lmc,md->lcd/dot_general | solution.py:65
  187.9 0.0 slice-done
  188.0 3.5 fusion.1
  191.5 165.7 %reduce-scatter.2.cloned.1.call-done = f32[16,4096]{1,0:T(8,128)} async-done(((f32[1024,4096]{1,0:T(8,128)}), f32[16,4096]{1,0:T(8,128)}) %reduce-scatter.2.cloned.1.call-update) | async-done | bytes 262160 | tf_op jit(solution)/shard_map/reduce_scatter | solution.py:71
  357.2 0.0 copy-done.1
  (15 shorter events, 0.0 us)
Async XLA Ops:
  7.2 89.3 %copy-start = (bf16[3,64,4096]{2,1,0:T(8,128)(2,1)S(1)}, bf16[3,64,4096]{2,1,0:T(8,128)(2,1)}, u32[]{:S(2)}) copy-start(bf16[3,64,4096]{2,1,0:T(8,128)(2,1)} %param.7) | copy-start | bytes 4718596
  7.2 89.3 %all-gather.2.cloned.1.call-start = ((), (), s32[]{:S(2)}) async-start(), calls=%async_computation.1 | async-start | bytes 8519680 | tf_op jit(solution)/shard_map/all_gather | solution.py:12
  7.9 94.8 %copy-start.5 = (bf16[3,512,64]{1,2,0:T(8,128)(2,1)S(1)}, bf16[3,512,64]{1,2,0:T(8,128)(2,1)}, u32[]{:S(2)}) copy-start(bf16[3,512,64]{1,2,0:T(8,128)(2,1)} %param.5) | copy-start | bytes 589828
  7.9 349.3 %reduce-scatter.2.cloned.1.call-start = ((), (), s32[]{:S(2)}) async-start(), calls=%async_computation.2 | async-start | bytes 17039360 | tf_op jit(solution)/shard_map/reduce_scatter | solution.py:71
  107.5 4.7 %copy-start.4 = (bf16[3,64,4096]{2,1,0:T(8,128)(2,1)S(1)}, bf16[3,64,4096]{2,1,0:T(8,128)(2,1)}, u32[]{:S(2)}) copy-start(bf16[3,64,4096]{2,1,0:T(8,128)(2,1)} %param.8) | copy-start | bytes 4718596
  112.2 6.5 %copy-start.3 = (f32[3,512,1024]{1,2,0:T(8,128)S(1)}, f32[3,512,1024]{1,2,0:T(8,128)}, u32[]{:S(2)}) copy-start(f32[3,512,1024]{1,2,0:T(8,128)} %get-tuple-element.8) | copy-start | bytes 18874372
  112.2 6.5 %copy-start.8 = (bf16[3,512,64]{1,2,0:T(8,128)(2,1)S(1)}, bf16[3,512,64]{1,2,0:T(8,128)(2,1)}, u32[]{:S(2)}) copy-start(bf16[3,512,64]{1,2,0:T(8,128)(2,1)} %param.9) | copy-start | bytes 589828
  118.6 1.1 copy-start.9
  119.7 3.4 copy-start.6
  121.5 1.7 copy-start.2
  172.9 0.9 copy-start.7
  172.9 1.1 copy-start.10
  177.2 10.8 %slice-start = ((s8[8388608]{0:T(1024)(128)(4,1)}), s8[4194304]{0:T(1024)(128)(4,1)S(1)}, s32[]{:S(2)}) async-start(s8[8388608]{0:T(1024)(128)(4,1)} %bitcast.93), calls=%async_computation.3 | async-start | bytes 8388608
  180.5 7.4 %slice-start.1 = ((s8[8388608]{0:T(1024)(128)(4,1)}), s8[4194304]{0:T(1024)(128)(4,1)S(1)}, s32[]{:S(2)}) async-start(s8[8388608]{0:T(1024)(128)(4,1)} %bitcast.93), calls=%async_computation.4 | async-start | bytes 8388608
  180.5 176.7 %copy-start.1 = (bf16[3,64,4096]{2,1,0:T(8,128)(2,1)S(1)}, bf16[3,64,4096]{2,1,0:T(8,128)(2,1)}, u32[]{:S(2)}) copy-start(bf16[3,64,4096]{2,1,0:T(8,128)(2,1)} %param.7) | copy-start | bytes 4718596
Sparse Core Ops, SparseCore 0:
  10.8 85.6 all-gather.1
  173.1 184.0 reduce-scatter.1
where the time goes:
time: 365 us; the launch traced here: 364 us
  waiting for transfers between devices  255 us (70%)
  matrix products  53.6 us (15%)
  blocking collectives  36.7 us (10%)
  between operations  14.2 us (4%)
    reduce_scatter x1, waiting for transfers between devices, shards(): lax.psum_scatter(jnp.einsum('lmc,lcd->md', key_gradient, w_key, preferred...  166 us
    all_gather x1, waiting for transfers between devices, shards(): mem_all = lax.all_gather(memory, 'mp', axis=0, tiled=True)  88.5 us
    psum x1, blocking collectives, shards(): key_sum, value_sum = lax.psum((key_part, value_part), 'dp')  36.7 us
    dot_general x1, matrix products, shards(): jnp.einsum('lmc,lcd->md', value_gradient, w_value, preferred_element_type...  9.57 us
    dot_general x1, matrix products, shards(): jnp.einsum('lmc,md->lcd', key_gradient, mem_all, preferred_element_type=j...  7.42 us
  transfers between devices with their start and end apart: 2, of which 2 were waited for; matrix products, arithmetic and copies ran while one was open for 5% of the time, Pallas kernels for 0%

commit v1 on v0

v1 whole, which is shorter than its diff:
```python
import jax
import jax.numpy as jnp
from jax import lax
from jax.experimental import pallas as pl
from jax.experimental.pallas import tpu as pltpu
from jax.sharding import Mesh
from jax.sharding import PartitionSpec as P

HEAD_WIDTH = 64
BF16 = jnp.bfloat16
F32 = jnp.float32
NT = (((1,), (1,)), ((), ()))
TN = (((0,), (0,)), ((), ()))
SWAP = [(0, 1), (1, 0)]


def mm(a, b, dims=(((1,), (0,)), ((), ()))):
    return lax.dot_general(a, b, dims, preferred_element_type=F32)


def split_heads(own_ref, other_ref, layer):
    lanes = slice(layer * 2 * HEAD_WIDTH, (layer + 1) * 2 * HEAD_WIDTH)
    both = jnp.concatenate([own_ref[:, lanes], other_ref[:, lanes]], axis=0).astype(F32)
    left = lax.broadcasted_iota(jnp.int32, both.shape, 1) < HEAD_WIDTH
    keys = jnp.where(left, both, 0.0).astype(BF16)
    values = jnp.where(left, 0.0, both).astype(BF16)
    return keys, values


def stats_kernel(own_ref, other_ref, qdo_ref, stats_ref):
    parts, layers, rows, _ = qdo_ref.shape
    stats_ref[...] = jnp.zeros_like(stats_ref)
    for layer in range(layers):
        keys, values = split_heads(own_ref, other_ref, layer)
        for part in range(parts):
            q = qdo_ref[part, layer]
            scores = mm(keys, q, NT)
            grads = mm(values, q, NT)
            top = jnp.max(scores, axis=0, keepdims=True)
            e = jnp.exp(scores - top)
            total = jnp.sum(e, axis=0, keepdims=True)
            delta = jnp.sum(e * grads, axis=0, keepdims=True) / total
            at = slice(part * rows, (part + 1) * rows)
            stats_ref[layer : layer + 1, at] = top + jnp.log(total)
            stats_ref[layers + layer : layers + layer + 1, at] = delta


def grads_kernel(own_ref, other_ref, qdo_ref, s0, s1, s2, s3, g_ref, qa_ref):
    parts, layers, rows, width = qdo_ref.shape
    tokens = 2 * own_ref.shape[0]
    left = lax.broadcasted_iota(jnp.int32, (tokens, width), 1) < HEAD_WIDTH
    stats = [s[...] for s in (s0, s1, s2, s3)]
    lses = [s[0:layers] for s in stats]
    top = jnp.maximum(jnp.maximum(lses[0], lses[1]), jnp.maximum(lses[2], lses[3]))
    total = sum(jnp.exp(a - top) for a in lses)
    lse = top + jnp.log(total)
    delta = sum(jnp.exp(s[0:layers] - lse) * s[layers : 2 * layers] for s in stats)
    for layer in range(layers):
        keys, values = split_heads(own_ref, other_ref, layer)
        flipped = jnp.concatenate([keys, values], axis=0).astype(F32).T.astype(BF16)
        acc = jnp.zeros((2 * tokens, width), F32)
        for part in range(parts):
            at = slice(part * rows, (part + 1) * rows)
            q = qdo_ref[part, layer]
            scores = mm(keys, q, NT)
            grads = mm(values, q, NT)
            probs = jnp.exp(scores - lse[layer : layer + 1, at])
            dscores = (probs * (grads - delta[layer : layer + 1, at])).astype(BF16)
            both = jnp.concatenate([dscores, probs.astype(BF16)], axis=0)
            acc += mm(both, q)
            qa_ref[part, layer] = mm(flipped, both).T.astype(BF16)
        g_ref[:, layer * width : (layer + 1) * width] = jnp.where(left, acc[:tokens], acc[tokens:]).astype(BF16)


def weights_kernel(g_ref, own_ref, other_ref, key_ref, value_ref):
    half = own_ref.shape[0]
    layers, width, _ = key_ref.shape
    out = mm(g_ref[:, :half], own_ref[...]) + mm(g_ref[:, half:], other_ref[...])
    for layer in range(layers):
        at = 2 * layer * width
        key_ref[layer] = out[at : at + width]
        value_ref[layer] = out[at + width : at + 2 * width]


def cost(flops, moved, exps=0):
    return pl.CostEstimate(flops=flops, bytes_accessed=moved, transcendentals=exps)


def shards(queries, memory, w_key, w_value, grad_out):
    layers, rows, width = queries.shape
    dp, nz, nx = lax.axis_size("dp"), lax.axis_size("z"), lax.axis_size("x")
    mine, d = memory.shape
    few = mine // dp
    here = lax.axis_index("dp")
    cols = 2 * width * layers
    half = few * nz * nx
    params = pltpu.CompilerParams(vmem_limit_bytes=48 * 1024 * 1024)

    full_own = lax.all_gather(memory, ("z", "x"), axis=0, tiled=True)
    full_other = lax.ppermute(full_own, "core", SWAP)

    quarter = lax.dynamic_slice(memory, (here * few, 0), (few, d))
    along_z = lax.all_to_all(jnp.broadcast_to(quarter, (nz, few, d)), "z", 0, 0).reshape(nz * few, d)
    mem_own = lax.all_to_all(jnp.broadcast_to(along_z, (nx, nz * few, d)), "x", 0, 0).reshape(half, d)
    mem_other = lax.ppermute(mem_own, "core", SWAP)

    qdo_own = jnp.concatenate([queries, grad_out], axis=-1)
    qdo = lax.all_to_all(jnp.broadcast_to(qdo_own, (dp,) + qdo_own.shape), "dp", 0, 0)

    w = jnp.concatenate([w_key, w_value], axis=1).reshape(cols, d)
    kv_own = mm(mem_own, w, NT).astype(BF16)
    kv_other = mm(mem_other, w, NT).astype(BF16)

    all_rows = dp * rows
    work = layers * all_rows * 2 * half * 256
    stats = pl.pallas_call(
        stats_kernel,
        out_shape=jax.ShapeDtypeStruct((8, all_rows), F32),
        compiler_params=params,
        cost_estimate=cost(4 * work, 4 * qdo.size, layers * all_rows * 2 * half),
    )(kv_own, kv_other, qdo)
    others = [lax.ppermute(stats, "dp", [(a, (a + s) % dp) for a in range(dp)]) for s in range(1, dp)]
    g, qa = pl.pallas_call(
        grads_kernel,
        out_shape=(
            jax.ShapeDtypeStruct((2 * half, cols), BF16),
            jax.ShapeDtypeStruct(qdo.shape, BF16),
        ),
        compiler_params=params,
        cost_estimate=cost(12 * work, 8 * qdo.size, layers * all_rows * 2 * half),
    )(kv_own, kv_other, qdo, stats, *others)

    to_other = mm(g[half:], w).astype(BF16)
    from_other = lax.ppermute(to_other, "core", SWAP)
    part = (mm(g[:half], w) + from_other.astype(F32)).astype(BF16)
    part = lax.all_to_all(part.reshape(nx, nz * few, d), "x", 0, 0)
    part = jnp.sum(part.astype(F32), axis=0).astype(BF16)
    part = lax.all_to_all(part.reshape(nz, few, d), "z", 0, 0)
    part = jnp.sum(part.astype(F32), axis=0)
    grad_memory = lax.all_to_all(jnp.broadcast_to(part, (dp, few, d)), "dp", 0, 0).reshape(mine, d)

    qa = lax.all_to_all(qa, "dp", 0, 0)
    qa = jnp.sum(qa.astype(F32), axis=0).astype(BF16)
    grad_queries, attended = qa[..., :width], qa[..., width:]

    g_all = lax.all_to_all(jnp.broadcast_to(g, (dp,) + g.shape), "dp", 0, 0)
    g_all = g_all.reshape(dp, 2, nx, nz, few, cols).transpose(5, 1, 3, 2, 0, 4).reshape(cols, 2 * nz * nx * mine)
    block = 512
    gw_shape = jax.ShapeDtypeStruct((layers, width, d), F32)
    gw_spec = pl.BlockSpec((layers, width, block), lambda n: (0, 0, n))
    mem_spec = pl.BlockSpec((nz * nx * mine, block), lambda n: (0, n))
    grad_w_key, grad_w_value = pl.pallas_call(
        weights_kernel,
        grid=(d // block,),
        in_specs=[pl.BlockSpec(g_all.shape, lambda n: (0, 0)), mem_spec, mem_spec],
        out_specs=(gw_spec, gw_spec),
        out_shape=(gw_shape, gw_shape),
        compiler_params=params,
        cost_estimate=cost(2 * cols * 2 * nz * nx * mine * d, 4 * nz * nx * mine * d + 4 * cols * d),
    )(g_all, full_own, full_other)
    return (attended, grad_queries, grad_memory, grad_w_key, grad_w_value)


def solution(mesh):
    dp = mesh.shape["dp"]
    split = Mesh(mesh.devices.reshape(dp, -1, 4, 2), ("dp", "z", "x", "core"))
    mp = ("z", "x", "core")
    by_rows, by_heads = P(None, "dp", mp), P(None, mp, None)
    return jax.shard_map(
        shards,
        mesh=split,
        in_specs=(by_rows, P(mp, None), by_heads, by_heads, by_rows),
        out_specs=(by_rows, by_rows, P(mp, None), by_heads, by_heads),
        check_vma=False,
    )
```

time: 365 us -> 200 us (0.55)
  waiting for transfers between devices: 255 us -> 64.4 us
  matrix products: 53.6 us -> 7.05 us
  starting transfers between devices: 0.08 us -> 23.4 us
  Pallas kernels: 0 us -> 17.2 us
  blocking collectives: 36.7 us -> 53.8 us
  local copies, waits for them, and re-layouts: 2.78 us -> 13.9 us
    reduce_scatter x1 -> x0, waiting for transfers between devices: 166 us -> none  [shards(): lax.psum_scatter(jnp.einsum('lmc,lcd->md', key_gradient, w_key, preferred...]
    all_gather x1, waiting for transfers between devices: 88.5 us -> 5.02 us  [shards(): full_own = lax.all_gather(memory, ('z', 'x'), axis=0, tiled=True)]
    all_to_all x0 -> x3, blocking collectives: none -> 53.8 us  [the longest x1 18.8 us: shards(): lax.all_to_all(jnp.broadcast_to(quarter, (nz, few, d)), 'z', 0, 0)]
    all_to_all x0 -> x5, waiting for transfers between devices: none -> 53.2 us  [the longest x1 16.5 us: shards(): qa = lax.all_to_all(qa, 'dp', 0, 0)]
    dot_general x11 -> x4, matrix products: 48.9 us -> 7.05 us  [mm(): return lax.dot_general(a, b, dims, preferred_element_type=F32)]
    psum x1 -> x0, blocking collectives: 36.7 us -> none  [shards(): key_sum, value_sum = lax.psum((key_part, value_part), 'dp')]
    all_to_all x0 -> x5, starting transfers between devices: none -> 20.5 us  [the longest x1 4.8 us: shards(): part = lax.all_to_all(part.reshape(nz, few, d), 'z', 0, 0)]
    pallas_call x0 -> x3, Pallas kernels: none -> 17.2 us  [the longest x1 8.89 us: shards(): pl.pallas_call(weights_kernel, grid=(d // block,), in_specs=[pl.BlockSpec...]
  transfers between devices with their start and end apart: 2 -> 12, of which waited for: 2 -> 9; matrix products, arithmetic and copies ran while one was open for 5% -> 11% of each run, Pallas kernels for 0% -> 4%
where the time goes in v1:
time: 200 us; the launch traced here: 198 us
  waiting for transfers between devices  64.4 us (32%)
  blocking collectives  53.8 us (27%)
  starting transfers between devices  23.4 us (12%)
  Pallas kernels  17.2 us (9%)
  between operations  14.2 us (7%)
  local copies, waits for them, and re-layouts  13.9 us (7%)
  matrix products  7.05 us (4%)
  other arithmetic  3.9 us (2%)
    all_to_all x1, blocking collectives, shards(): lax.all_to_all(jnp.broadcast_to(quarter, (nz, few, d)), 'z', 0, 0)  18.8 us
    all_to_all x1, blocking collectives, shards(): lax.all_to_all(jnp.broadcast_to(along_z, (nx, nz * few, d)), 'x', 0, 0)  17.6 us
    all_to_all x1, blocking collectives, shards(): part = lax.all_to_all(part.reshape(nx, nz * few, d), 'x', 0, 0)  17.4 us
    all_to_all x1, waiting for transfers between devices, shards(): qa = lax.all_to_all(qa, 'dp', 0, 0)  16.5 us
    all_to_all x1, waiting for transfers between devices, shards(): lax.all_to_all(jnp.broadcast_to(qdo_own, (dp,) + qdo_own.shape), 'dp', 0, 0)  15.1 us
    all_to_all x1, waiting for transfers between devices, shards(): g_all = lax.all_to_all(jnp.broadcast_to(g, (dp,) + g.shape), 'dp', 0, 0)  10.1 us
    pallas_call x1, Pallas kernels, shards(): pl.pallas_call(weights_kernel, grid=(d // block,), in_specs=[pl.BlockSpec...  8.89 us
    dot_general x4, matrix products, mm(): return lax.dot_general(a, b, dims, preferred_element_type=F32)  7.05 us
  transfers between devices with their start and end apart: 12, of which 9 were waited for; matrix products, arithmetic and copies ran while one was open for 11% of the time, Pallas kernels for 4%

profile of v1, /device:TPU:32, one launch (start us, length us, event | category | flops | bytes accessed | tf_op | source)
XLA Modules:
  0.0 197.8 jit_solution(12727334005319498271)
XLA Ops:
  8.9 18.8 %all_to_all.40 = bf16[8,4,4096]{2,1,0:T(4,128)(2,1)S(1)} all-to-all(bf16[8,4,4096]{2,1,0:T(4,128)(2,1)S(1)} %broadcast_in_dim.15), channel_id=1, replica_groups=mesh['dp'=4,'z'=8,'x'=4,'core'=2] {'z'}, dimensions={0} | all-to-all | bytes 524288 | tf_op jit(solution)/shard_map/all_to_all | solution.py:103
  27.8 17.6 %all_to_all.41 = bf16[4,32,4096]{2,1,0:T(8,128)(2,1)S(1)} all-to-all(bf16[4,32,4096]{2,1,0:T(8,128)(2,1)S(1)} %broadcast_in_dim.16), channel_id=1, replica_groups=mesh['dp'=4,'z'=8,'x'=4,'core'=2] {'x'}, dimensions={0} | all-to-all | bytes 2097152 | tf_op jit(solution)/shard_map/all_to_all | solution.py:104
  45.7 1.4 broadcast_in_dim.17
  47.1 4.4 %all-to-all-start.2 = ((bf16[4,3,512,128]{3,2,1,0:T(8,128)(2,1)}), bf16[4,3,512,128]{3,2,1,0:T(8,128)(2,1)S(1)}, u32[]{:S(2)}, u32[]{:S(2)}) async-start(bf16[4,3,512,128]{3,2,1,0:T(8,128)(2,1)} %broadcast_in_dim.17), calls=%async_computation.2 | async-start | bytes 3145728 | tf_op jit(solution)/shard_map/all_to_all | solution.py:108
  51.6 2.2 %pad_maximum_fusion = bf16[3,128,4096]{2,1,0:T(8,128)(2,1)S(1)} fusion(bf16[3,64,4096]{2,1,0:T(8,128)(2,1)} %param.8, bf16[3,64,4096]{2,1,0:T(8,128)(2,1)} %param.7), kind=kLoop, calls=%fused_computation.3 | loop fusion | flops 6291456 | bytes 6291456 | tf_op jit(solution)/shard_map/concatenate | solution.py:110
  53.8 1.1 convolution_convert_fusion.2.own_ref
  55.5 2.3 %convolution_convert_fusion.1.other_ref = bf16[128,384]{1,0:T(8,128)(2,1)S(1)} fusion(bf16[128,4096]{1,0:T(8,128)(2,1)} %collective-permute-done, bf16[384,4096]{1,0:T(8,128)(2,1)S(1)} %bitcast.15), kind=kOutput, calls=%fused_computation.4 | convolution fusion | flops 402702336 | bytes 4292608 | tf_op jit(solution)/shard_map/dot_general | solution.py:18
  57.8 15.1 %all-to-all-done.2.qdo_ref = bf16[4,3,512,128]{3,2,1,0:T(8,128)(2,1)S(1)} async-done(((bf16[4,3,512,128]{3,2,1,0:T(8,128)(2,1)}), bf16[4,3,512,128]{3,2,1,0:T(8,128)(2,1)S(1)}, u32[]{:S(2)}, u32[]{:S(2)}) %all-to-all-start.2) | async-done | bytes 1572896 | tf_op jit(solution)/shard_map/all_to_all | solution.py:108
  72.9 1.9 shard_map.92.s0
  74.9 1.2 collective-permute-start.3
  76.2 1.5 collective-permute-start.2
  77.6 1.6 collective-permute-done.3.s3
  79.3 2.7 %collective-permute-done.2.s2 = f32[8,2048]{1,0:T(8,128)S(1)} collective-permute-done((f32[8,2048]{1,0:T(8,128)S(1)}, f32[8,2048]{1,0:T(8,128)S(1)}, u32[]{:S(2)}, u32[]{:S(2)}) %collective-permute-start.2) | collective-permute-done | bytes 65568 | tf_op jit(solution)/shard_map/ppermute | solution.py:122
  82.0 1.1 collective-permute-done.1.s1
  83.1 6.3 %shard_map.93 = (bf16[256,384]{1,0:T(8,128)(2,1)S(1)}, bf16[4,3,512,128]{3,2,1,0:T(8,128)(2,1)}) custom-call(bf16[128,384]{1,0:T(8,128)(2,1)S(1)} %convolution_convert_fusion.2.own_ref, bf16[128,384]{1,0:T(8,128)(2,1)S(1)} %convolution_convert_fusion.1.other_ref, bf16[4,3,512,128]{3,2,1,0:T(8,128)(2,1)S(1)} %all-to-all-done.2.qdo_ref, ...), custom_call_target="tpu_custom_call" | custom-call | flops 4831838208 | bytes 6291456 | tf_op jit(solution)/shard_map/pallas_call | solution.py:123
  90.3 5.0 %all-gather.2.cloned.1.call-done.own_ref = bf16[512,4096]{1,0:T(8,128)(2,1)} async-done(((bf16[16,4096]{1,0:T(8,128)(2,1)}), bf16[512,4096]{1,0:T(8,128)(2,1)}) %all-gather.2.cloned.1.call-update) | async-done | bytes 4194320 | tf_op jit(solution)/shard_map/all_gather | solution.py:99
  95.3 0.9 broadcast_in_dim.19
  96.2 4.2 %all-to-all-start.7 = ((bf16[4,256,384]{2,1,0:T(8,128)(2,1)}), bf16[4,256,384]{2,1,0:T(8,128)(2,1)S(1)}, u32[]{:S(2)}, u32[]{:S(2)}) async-start(bf16[4,256,384]{2,1,0:T(8,128)(2,1)} %broadcast_in_dim.19), calls=%async_computation.7 | async-start | bytes 1572864 | tf_op jit(solution)/shard_map/all_to_all | solution.py:146
  100.5 2.9 %fusion = bf16[128,4096]{1,0:T(8,128)(2,1)S(1)} fusion(bf16[384,4096]{1,0:T(8,128)(2,1)} %bitcast.16, bf16[128,4096]{1,0:T(8,128)(2,1)} %collective-permute-done.4, bf16[256,384]{1,0:T(8,128)(2,1)S(1)} %get-tuple-element.10), kind=kOutput, calls=%fused_computation.1 | convolution fusion | flops 404226048 | bytes 5341184 | tf_op jit(solution)/shard_map/dot_general | solution.py:18
  103.4 10.1 %all-to-all-done.7 = bf16[4,256,384]{2,1,0:T(8,128)(2,1)S(1)} async-done(((bf16[4,256,384]{2,1,0:T(8,128)(2,1)}), bf16[4,256,384]{2,1,0:T(8,128)(2,1)S(1)}, u32[]{:S(2)}, u32[]{:S(2)}) %all-to-all-start.7) | async-done | bytes 786464 | tf_op jit(solution)/shard_map/all_to_all | solution.py:146
  113.4 0.9 copy-done.3
  114.3 17.4 %all_to_all.42 = bf16[4,32,4096]{2,1,0:T(8,128)(2,1)S(1)} all-to-all(bf16[4,32,4096]{2,1,0:T(8,128)(2,1)S(1)} %bitcast.20), channel_id=1, replica_groups=mesh['dp'=4,'z'=8,'x'=4,'core'=2] {'x'}, dimensions={0} | all-to-all | bytes 2097152 | tf_op jit(solution)/shard_map/all_to_all | solution.py:136
  131.7 3.7 %all-to-all-start.3 = ((bf16[4,3,512,128]{3,2,1,0:T(8,128)(2,1)}), bf16[4,3,512,128]{3,2,1,0:T(8,128)(2,1)S(1)}, u32[]{:S(2)}, u32[]{:S(2)}) async-start(bf16[4,3,512,128]{3,2,1,0:T(8,128)(2,1)} %get-tuple-element.9), calls=%async_computation.3 | async-start | bytes 3145728 | tf_op jit(solution)/shard_map/all_to_all | solution.py:142
  135.4 0.9 reduce_sum.34
  136.3 1.8 reshape.38
  138.0 16.5 %all-to-all-done.3 = bf16[4,3,512,128]{3,2,1,0:T(8,128)(2,1)S(1)} async-done(((bf16[4,3,512,128]{3,2,1,0:T(8,128)(2,1)}), bf16[4,3,512,128]{3,2,1,0:T(8,128)(2,1)S(1)}, u32[]{:S(2)}, u32[]{:S(2)}) %all-to-all-start.3) | async-done | bytes 1572896 | tf_op jit(solution)/shard_map/all_to_all | solution.py:142
  154.5 4.8 %all-to-all-start.5 = ((bf16[8,4,4096]{2,1,0:T(4,128)(2,1)}), bf16[8,4,4096]{2,1,0:T(4,128)(2,1)S(1)}, u32[]{:S(2)}, u32[]{:S(2)}) async-start(bf16[8,4,4096]{2,1,0:T(4,128)(2,1)} %reshape.38), calls=%async_computation.5 | async-start | bytes 524288 | tf_op jit(solution)/shard_map/all_to_all | solution.py:138
  161.2 6.8 %all-to-all-done.5 = bf16[8,4,4096]{2,1,0:T(4,128)(2,1)S(1)} async-done(((bf16[8,4,4096]{2,1,0:T(4,128)(2,1)}), bf16[8,4,4096]{2,1,0:T(4,128)(2,1)S(1)}, u32[]{:S(2)}, u32[]{:S(2)}) %all-to-all-start.5) | async-done | bytes 262176 | tf_op jit(solution)/shard_map/all_to_all | solution.py:138
  169.1 3.4 %all-to-all-start.6 = ((f32[4,4,4096]{2,1,0:T(4,128)}), f32[4,4,4096]{2,1,0:T(4,128)S(1)}, u32[]{:S(2)}, u32[]{:S(2)}) async-start(f32[4,4,4096]{2,1,0:T(4,128)} %broadcast_in_dim.18), calls=%async_computation.6 | async-start | bytes 524288 | tf_op jit(solution)/shard_map/all_to_all | solution.py:140
  174.3 4.8 %all-to-all-done.6 = f32[4,4,4096]{2,1,0:T(4,128)S(1)} async-done(((f32[4,4,4096]{2,1,0:T(4,128)}), f32[4,4,4096]{2,1,0:T(4,128)S(1)}, u32[]{:S(2)}, u32[]{:S(2)}) %all-to-all-start.6) | async-done | bytes 262176 | tf_op jit(solution)/shard_map/all_to_all | solution.py:140
  179.9 2.2 %copy-done = bf16[512,4096]{1,0:T(8,128)(2,1)S(1)} copy-done((bf16[512,4096]{1,0:T(8,128)(2,1)S(1)}, bf16[512,4096]{1,0:T(8,128)(2,1)}, u32[]{:S(2)}) %copy-start) | copy-done | bytes 4194328
  182.1 8.9 %shard_map.94 = (f32[3,64,4096]{2,1,0:T(8,128)}, f32[3,64,4096]{2,1,0:T(8,128)}) custom-call(bf16[384,1024]{1,0:T(8,128)(2,1)S(1)} %copy.44.g_ref, bf16[512,4096]{1,0:T(8,128)(2,1)S(1)} %copy-done, bf16[512,4096]{1,0:T(8,128)(2,1)} %collective-permute-done.5.other_ref), custom_call_target="tpu_custom_call" | custom-call | flops 3221225472 | bytes 14680064 | tf_op jit(solution)/shard_map/pallas_call | solution.py:152
  (39 shorter events, 9.0 us)
Async XLA Ops:
  7.2 38.3 %copy-start.5 = (bf16[3,512,64]{1,2,0:T(8,128)(2,1)S(1)}, bf16[3,512,64]{1,2,0:T(8,128)(2,1)}, u32[]{:S(2)}) copy-start(bf16[3,512,64]{1,2,0:T(8,128)(2,1)} %param.9) | copy-start | bytes 589828
  7.2 38.3 %copy-start.6 = (bf16[3,512,64]{1,2,0:T(8,128)(2,1)S(1)}, bf16[3,512,64]{1,2,0:T(8,128)(2,1)}, u32[]{:S(2)}) copy-start(bf16[3,512,64]{1,2,0:T(8,128)(2,1)} %param.5) | copy-start | bytes 589828
  7.2 88.1 %all-gather.2.cloned.1.call-start = ((), (), s32[]{:S(2)}) async-start(), calls=%async_computation.8 | async-start | bytes 4325376 | tf_op jit(solution)/shard_map/all_gather | solution.py:99
  45.5 9.5 %collective-permute-start = (bf16[128,4096]{1,0:T(8,128)(2,1)S(1)}, bf16[128,4096]{1,0:T(8,128)(2,1)}, u32[]{:S(2)}, u32[]{:S(2)}) collective-permute-start(bf16[128,4096]{1,0:T(8,128)(2,1)S(1)} %bitcast.18), channel_id=1, source_target_pairs={{0,1},{1,0},{2,3},{3,2},{4,5},{5,4},{6,7},{7,6},{8,9},{9,8},{10,11... | collective-permute-start | bytes 3145736 | tf_op jit(solution)/shard_map/ppermute | solution.py:105
  47.1 25.8 %all-to-all-start.2 = ((bf16[4,3,512,128]{3,2,1,0:T(8,128)(2,1)}), bf16[4,3,512,128]{3,2,1,0:T(8,128)(2,1)S(1)}, u32[]{:S(2)}, u32[]{:S(2)}) async-start(bf16[4,3,512,128]{3,2,1,0:T(8,128)(2,1)} %broadcast_in_dim.17), calls=%async_computation.2 | async-start | bytes 3145728 | tf_op jit(solution)/shard_map/all_to_all | solution.py:108
  53.8 1.7 copy-start.1
  74.9 14.5 %copy-start.2 = (bf16[3,128,4096]{2,1,0:T(8,128)(2,1)S(1)}, bf16[3,128,4096]{2,1,0:T(8,128)(2,1)}, u32[]{:S(2)}) copy-start(bf16[3,128,4096]{2,1,0:T(8,128)(2,1)} %copy-done.1) | copy-start | bytes 9437188
  74.9 4.3 %collective-permute-start.3 = (f32[8,2048]{1,0:T(8,128)S(1)}, f32[8,2048]{1,0:T(8,128)S(1)}, u32[]{:S(2)}, u32[]{:S(2)}) collective-permute-start(f32[8,2048]{1,0:T(8,128)S(1)} %shard_map.92.s0), channel_id=1, source_target_pairs={{0,192},{64,0},{128,64},{192,128},{1,193},{65,1},{129,65},{193,129... | collective-permute-start | bytes 196616 | tf_op jit(solution)/shard_map/ppermute | solution.py:122
  76.2 5.8 %collective-permute-start.2 = (f32[8,2048]{1,0:T(8,128)S(1)}, f32[8,2048]{1,0:T(8,128)S(1)}, u32[]{:S(2)}, u32[]{:S(2)}) collective-permute-start(f32[8,2048]{1,0:T(8,128)S(1)} %shard_map.92.s0), channel_id=1, source_target_pairs={{0,128},{64,192},{128,0},{192,64},{1,129},{65,193},{129,1},{193,65... | collective-permute-start | bytes 196616 | tf_op jit(solution)/shard_map/ppermute | solution.py:122
  77.6 5.5 %collective-permute-start.1 = (f32[8,2048]{1,0:T(8,128)S(1)}, f32[8,2048]{1,0:T(8,128)S(1)}, u32[]{:S(2)}, u32[]{:S(2)}) collective-permute-start(f32[8,2048]{1,0:T(8,128)S(1)} %shard_map.92.s0), channel_id=1, source_target_pairs={{0,64},{64,128},{128,192},{192,0},{1,65},{65,129},{129,193},{193,1... | collective-permute-start | bytes 196616 | tf_op jit(solution)/shard_map/ppermute | solution.py:122
  90.2 10.3 %collective-permute-start.4 = (bf16[128,4096]{1,0:T(8,128)(2,1)S(1)}, bf16[128,4096]{1,0:T(8,128)(2,1)}, u32[]{:S(2)}, u32[]{:S(2)}) collective-permute-start(bf16[128,4096]{1,0:T(8,128)(2,1)S(1)} %convolution_convert_fusion), channel_id=1, source_target_pairs={{0,1},{1,0},{2,3},{3,2},{4,5},{5,4},{6,7},{7,6},{8,9},{9,8},{10,11... | collective-permute-start | bytes 3145736 | tf_op jit(solution)/shard_map/ppermute | solution.py:134
  95.3 84.6 %collective-permute-start.5 = (bf16[512,4096]{1,0:T(8,128)(2,1)}, bf16[512,4096]{1,0:T(8,128)(2,1)}, u32[]{:S(2)}, u32[]{:S(2)}) collective-permute-start(bf16[512,4096]{1,0:T(8,128)(2,1)} %all-gather.2.cloned.1.call-done.own_ref), channel_id=1, source_target_pairs={{0,1},{1,0},{2,3},{3,2},{4,5},{5,4},{6,7},{7,6},{8,9},{9,8},{10,11... | collective-permute-start | bytes 12582920 | tf_op jit(solution)/shard_map/ppermute | solution.py:100
  96.2 17.2 %all-to-all-start.7 = ((bf16[4,256,384]{2,1,0:T(8,128)(2,1)}), bf16[4,256,384]{2,1,0:T(8,128)(2,1)S(1)}, u32[]{:S(2)}, u32[]{:S(2)}) async-start(bf16[4,256,384]{2,1,0:T(8,128)(2,1)} %broadcast_in_dim.19), calls=%async_computation.7 | async-start | bytes 1572864 | tf_op jit(solution)/shard_map/all_to_all | solution.py:146
  113.4 0.9 copy-start.3
  131.7 27.7 %copy-start.4 = (bf16[4,256,384]{2,1,0:T(8,128)(2,1)S(1)}, bf16[4,256,384]{2,1,0:T(8,128)(2,1)}, u32[]{:S(2)}) copy-start(bf16[4,256,384]{2,1,0:T(8,128)(2,1)} %copy-done.3) | copy-start | bytes 2359300
  131.7 22.9 %all-to-all-start.3 = ((bf16[4,3,512,128]{3,2,1,0:T(8,128)(2,1)}), bf16[4,3,512,128]{3,2,1,0:T(8,128)(2,1)S(1)}, u32[]{:S(2)}, u32[]{:S(2)}) async-start(bf16[4,3,512,128]{3,2,1,0:T(8,128)(2,1)} %get-tuple-element.9), calls=%async_computation.3 | async-start | bytes 3145728 | tf_op jit(solution)/shard_map/all_to_all | solution.py:142
  154.5 13.5 %all-to-all-start.5 = ((bf16[8,4,4096]{2,1,0:T(4,128)(2,1)}), bf16[8,4,4096]{2,1,0:T(4,128)(2,1)S(1)}, u32[]{:S(2)}, u32[]{:S(2)}) async-start(bf16[8,4,4096]{2,1,0:T(4,128)(2,1)} %reshape.38), calls=%async_computation.5 | async-start | bytes 524288 | tf_op jit(solution)/shard_map/all_to_all | solution.py:138
  169.1 10.1 %all-to-all-start.6 = ((f32[4,4,4096]{2,1,0:T(4,128)}), f32[4,4,4096]{2,1,0:T(4,128)S(1)}, u32[]{:S(2)}, u32[]{:S(2)}) async-start(f32[4,4,4096]{2,1,0:T(4,128)} %broadcast_in_dim.18), calls=%async_computation.6 | async-start | bytes 524288 | tf_op jit(solution)/shard_map/all_to_all | solution.py:140
  179.9 2.2 %copy-start = (bf16[512,4096]{1,0:T(8,128)(2,1)S(1)}, bf16[512,4096]{1,0:T(8,128)(2,1)}, u32[]{:S(2)}) copy-start(bf16[512,4096]{1,0:T(8,128)(2,1)} %all-gather.2.cloned.1.call-done.own_ref) | copy-start | bytes 12582916
Sparse Core Ops, SparseCore 0:
  10.6 84.6 all-gather.1

commit v2 on v1

v2 whole, which is shorter than its diff:
```python
import jax
import jax.numpy as jnp
from jax import lax
from jax.experimental import pallas as pl
from jax.experimental.pallas import tpu as pltpu
from jax.sharding import Mesh
from jax.sharding import PartitionSpec as P

HEAD_WIDTH = 64
BF16 = jnp.bfloat16
F32 = jnp.float32
NT = (((1,), (1,)), ((), ()))


def mm(a, b, dims=(((1,), (0,)), ((), ()))):
    return lax.dot_general(a, b, dims, preferred_element_type=F32)


def shift(x, axis, by):
    n = lax.axis_size(axis)
    return lax.ppermute(x, axis, [(a, (a + by) % n) for a in range(n)])


def after(x, *others):
    return lax.optimization_barrier((x, *others))[0]


def split_heads(own_ref, other_ref, layer):
    lanes = slice(layer * 2 * HEAD_WIDTH, (layer + 1) * 2 * HEAD_WIDTH)
    both = jnp.concatenate([own_ref[:, lanes], other_ref[:, lanes]], axis=0).astype(F32)
    left = lax.broadcasted_iota(jnp.int32, both.shape, 1) < HEAD_WIDTH
    keys = jnp.where(left, both, 0.0).astype(BF16)
    values = jnp.where(left, 0.0, both).astype(BF16)
    return keys, values


def project_kernel(own_key, own_value, other_key, other_value, *refs):
    *mem_refs, own_ref, other_ref = refs
    mem = jnp.concatenate([m[...] for m in mem_refs], axis=0)
    layers, width, _ = own_key.shape
    for key, value, out_ref in ((other_key, other_value, other_ref), (own_key, own_value, own_ref)):
        for layer in range(layers):
            w = jnp.concatenate([key[layer], value[layer]], axis=0)
            at = 2 * layer * width
            out_ref[:, at : at + 2 * width] = mm(w, mem, NT).T.astype(BF16)


def memory_kernel(own_ref, other_ref, own_key, own_value, other_key, other_value, out_ref):
    layers, width, d = own_key.shape
    blocks, rows, _ = out_ref.shape
    g = jnp.concatenate([own_ref[: blocks * rows], other_ref[...]], axis=1)
    step = 512
    for at in range(0, d, step):
        w = [r[layer, :, at : at + step] for k, v in ((own_key, own_value), (other_key, other_value)) for layer in range(layers) for r in (k, v)]
        out = mm(g, jnp.concatenate(w, axis=0)).astype(BF16)
        out_ref[:, :, at : at + step] = out.reshape(blocks, rows, step)


def stats_kernel(own_ref, other_ref, *refs):
    *qdo_refs, stats_ref = refs
    layers, _, rows = qdo_refs[0].shape
    stats_ref[...] = jnp.zeros_like(stats_ref)
    for layer in range(layers):
        keys, values = split_heads(own_ref, other_ref, layer)
        for part, qdo_ref in enumerate(qdo_refs):
            q = qdo_ref[layer]
            scores = mm(keys, q)
            grads = mm(values, q)
            top = jnp.max(scores, axis=0, keepdims=True)
            e = jnp.exp(scores - top)
            total = jnp.sum(e, axis=0, keepdims=True)
            delta = jnp.sum(e * grads, axis=0, keepdims=True) / total
            at = slice(part * rows, (part + 1) * rows)
            stats_ref[layer : layer + 1, at] = top + jnp.log(total)
            stats_ref[layers + layer : layers + layer + 1, at] = delta


def combine(stats_refs, rows, layers):
    parts = len(stats_refs)
    for part in range(parts):
        stats = []
        for k, s in enumerate(stats_refs):
            at = (part - k) % parts * rows
            stats.append(s[:, at : at + rows])
        lses = [s[0:layers] for s in stats]
        top = jnp.maximum(jnp.maximum(lses[0], lses[1]), jnp.maximum(lses[2], lses[3]))
        lse = top + jnp.log(sum(jnp.exp(a - top) for a in lses))
        yield lse, sum(jnp.exp(s[0:layers] - lse) * s[layers : 2 * layers] for s in stats)


def probs_and_scores(keys, values, q, lse, delta):
    probs = jnp.exp(mm(keys, q) - lse)
    dscores = probs * (mm(values, q) - delta)
    return jnp.concatenate([dscores.astype(BF16), probs.astype(BF16)], axis=0)


def token_grads_kernel(own_ref, other_ref, *refs):
    *qdo_refs, s0, s1, s2, s3, g_ref = refs
    layers, width, rows = qdo_refs[0].shape
    tokens = 2 * own_ref.shape[0]
    left = lax.broadcasted_iota(jnp.int32, (tokens, width), 1) < HEAD_WIDTH
    stats = list(combine((s0, s1, s2, s3), rows, layers))
    for layer in range(layers):
        keys, values = split_heads(own_ref, other_ref, layer)
        acc = 0.0
        for qdo_ref, (lse, delta) in zip(qdo_refs, stats):
            q = qdo_ref[layer]
            acc += mm(probs_and_scores(keys, values, q, lse[layer : layer + 1], delta[layer : layer + 1]), q, NT)
        g_ref[:, layer * width : (layer + 1) * width] = jnp.where(left, acc[:tokens], acc[tokens:]).astype(BF16)


def row_grads_kernel(own_ref, other_ref, *refs):
    *qdo_refs, s0, s1, s2, s3, qa_ref = refs
    layers, _, rows = qdo_refs[0].shape
    stats = list(combine((s0, s1, s2, s3), rows, layers))
    for layer in range(layers):
        keys, values = split_heads(own_ref, other_ref, layer)
        flipped = jnp.concatenate([keys, values], axis=0).astype(F32).T.astype(BF16)
        for part, (qdo_ref, (lse, delta)) in enumerate(zip(qdo_refs, stats)):
            both = probs_and_scores(keys, values, qdo_ref[layer], lse[layer : layer + 1], delta[layer : layer + 1])
            qa_ref[part, layer] = mm(flipped, both).astype(BF16)


def weights_kernel(at_ref, *refs):
    *g_refs, mem_ref, key_ref, value_ref, stack, order, flipped = refs
    ndp, nx, nz, few = len(g_refs), 4, 8, 4
    layers, width, _ = key_ref.shape

    @pl.when(pl.program_id(0) == 0)
    def _():
        for part, g_ref in enumerate(g_refs):
            stack[part] = g_ref[...].astype(F32)
        parts = [lax.rem(at_ref[0] + ndp - dp, ndp) for dp in range(ndp)]
        for half in range(2):
            core = at_ref[2] if half == 0 else 1 - at_ref[2]
            for back in range(nx):
                x = lax.rem(at_ref[1] + nx - back, nx)
                first = (half * nx + back) * nz * few
                blocks = [stack[part, first : first + nz * few] for part in parts]
                for z in range(nz):
                    to = pl.multiple_of(((z * nx + x) * 2 + core) * ndp * few, ndp * few)
                    order[pl.ds(to, ndp * few)] = jnp.concatenate([b[z * few : (z + 1) * few] for b in blocks], axis=0)
        flipped[...] = order[...].T.astype(BF16)

    out = mm(flipped[...], mem_ref[...])
    for layer in range(layers):
        at = 2 * layer * width
        key_ref[layer] = out[at : at + width]
        value_ref[layer] = out[at + width : at + 2 * width]


def cost(flops, moved, exps=0):
    return pl.CostEstimate(flops=flops, bytes_accessed=moved, transcendentals=exps)


def shards(queries, memory, w_key, w_value, grad_out):
    layers, rows, width = queries.shape
    dp, nz, nx = lax.axis_size("dp"), lax.axis_size("z"), lax.axis_size("x")
    mine, d = memory.shape
    few = mine // dp
    here = lax.axis_index("dp")
    cols = 2 * width * layers
    half = few * nz * nx
    params = pltpu.CompilerParams(vmem_limit_bytes=28 * 1024 * 1024)

    at = jnp.stack([here, lax.axis_index("x"), lax.axis_index("core")])

    full = lax.all_gather(memory, ("z", "x", "core"), axis=0, tiled=True)

    quarter = lax.dynamic_slice(memory, (here * few, 0), (few, d))
    along_z = lax.all_to_all(jnp.broadcast_to(quarter, (nz, few, d)), "z", 0, 0).reshape(nz * few, d)
    key_other, value_other = shift(w_key, "core", 1), shift(w_value, "core", 1)
    along_z, key_other, value_other = lax.optimization_barrier((along_z, key_other, value_other))
    qdo = jnp.concatenate([queries.swapaxes(1, 2), grad_out.swapaxes(1, 2)], axis=1)
    qdo = after(qdo, along_z)
    qdo = [qdo] + [shift(qdo, "dp", s) for s in range(1, dp)]

    mem_parts = [along_z] + [shift(along_z, "x", s) for s in range(1, nx)]

    weights = (w_key, w_value, key_other, value_other)
    kv_own, kv_other = pl.pallas_call(
        project_kernel,
        out_shape=(jax.ShapeDtypeStruct((half, cols), BF16), jax.ShapeDtypeStruct((half, cols), BF16)),
        compiler_params=params,
        cost_estimate=cost(4 * half * cols * d, 2 * (half + 2 * cols) * d),
    )(*weights, *mem_parts)
    kv_other = shift(kv_other, "core", 1)

    all_rows = dp * rows
    work = layers * all_rows * 2 * half * 256
    stats = pl.pallas_call(
        stats_kernel,
        out_shape=jax.ShapeDtypeStruct((8, all_rows), F32),
        compiler_params=params,
        cost_estimate=cost(4 * work, 4 * dp * qdo[0].size, layers * all_rows * 2 * half),
    )(kv_own, kv_other, *qdo)
    others = [shift(stats, "dp", s) for s in range(1, dp)]
    g = pl.pallas_call(
        token_grads_kernel,
        out_shape=jax.ShapeDtypeStruct((2 * half, cols), BF16),
        compiler_params=params,
        cost_estimate=cost(8 * work, 4 * dp * qdo[0].size, layers * all_rows * 2 * half),
    )(kv_own, kv_other, *qdo, stats, *others)

    g_other = shift(g[half:], "core", 1)
    part = pl.pallas_call(
        memory_kernel,
        out_shape=jax.ShapeDtypeStruct((nx, nz * few, d), BF16),
        compiler_params=params,
        cost_estimate=cost(4 * half * cols * d, 2 * (half + 2 * cols) * d),
    )(g, g_other, *weights)
    g_all = [g] + [shift(g, "dp", s) for s in range(1, dp)]
    stats = after(stats, part, g_all[1], g_all[3])
    part = sum([part[0].astype(F32)] + [shift(part[s], "x", -s).astype(F32) for s in range(1, nx)]).astype(BF16)

    qa = pl.pallas_call(
        row_grads_kernel,
        out_shape=jax.ShapeDtypeStruct((dp,) + qdo[0].shape, BF16),
        compiler_params=params,
        cost_estimate=cost(8 * work, 8 * dp * qdo[0].size, layers * all_rows * 2 * half),
    )(kv_own, kv_other, *qdo, stats, *others)
    qa = [qa[0]] + [shift(qa[s], "dp", -s) for s in range(1, dp)]

    block = 512
    gw_shape = jax.ShapeDtypeStruct((layers, width, d), F32)
    gw_spec = pl.BlockSpec((layers, width, block), lambda n, at: (0, 0, n))
    grad_w = pl.pallas_call(
        weights_kernel,
        grid_spec=pltpu.PrefetchScalarGridSpec(
            num_scalar_prefetch=1,
            grid=(d // block,),
            in_specs=[pl.BlockSpec(g.shape, lambda n, at: (0, 0))] * dp + [pl.BlockSpec((full.shape[0], block), lambda n, at: (0, n))],
            out_specs=(gw_spec, gw_spec),
            scratch_shapes=[pltpu.VMEM((dp,) + g.shape, F32), pltpu.VMEM((full.shape[0], cols), F32), pltpu.VMEM((cols, full.shape[0]), BF16)],
        ),
        out_shape=(gw_shape, gw_shape),
        compiler_params=pltpu.CompilerParams(vmem_limit_bytes=56 * 1024 * 1024),
        cost_estimate=cost(2 * cols * full.size, 2 * full.size + 4 * cols * d),
    )(at, *g_all, full)

    part = lax.all_to_all(part.reshape(nz, few, d), "z", 0, 0)
    part = jnp.sum(part.astype(F32), axis=0)
    part, grad_w_key, grad_w_value = lax.optimization_barrier((part, *grad_w))
    parts = [part] + [shift(part, "dp", s) for s in range(1, dp)]
    parts = jnp.concatenate([parts[-1 - j % dp] for j in range(2 * dp - 1)], axis=0)
    grad_memory = lax.dynamic_slice(parts, ((dp - 1 - here) * few, 0), (mine, d))
    qa = sum(a.astype(F32) for a in qa).astype(BF16)
    grad_queries, attended = qa[:, :width].swapaxes(1, 2), qa[:, width:].swapaxes(1, 2)
    return (attended, grad_queries, grad_memory, grad_w_key, grad_w_value)


def solution(mesh):
    dp = mesh.shape["dp"]
    split = Mesh(mesh.devices.reshape(dp, -1, 4, 2), ("dp", "z", "x", "core"))
    mp = ("z", "x", "core")
    by_rows, by_heads = P(None, "dp", mp), P(None, mp, None)
    return jax.shard_map(
        shards,
        mesh=split,
        in_specs=(by_rows, P(mp, None), by_heads, by_heads, by_rows),
        out_specs=(by_rows, by_rows, P(mp, None), by_heads, by_heads),
        check_vma=False,
    )
```

time: 200 us -> 143 us (0.71)
  waiting for transfers between devices: 64.4 us -> 25.5 us
  blocking collectives: 53.8 us -> 19.2 us
  starting transfers between devices: 23.4 us -> 45.4 us
  Pallas kernels: 17.2 us -> 27.2 us
  matrix products: 7.05 us -> 0 us
  local copies, waits for them, and re-layouts: 13.9 us -> 7.45 us
    all_to_all x4 -> x0, waiting for transfers between devices: 46.5 us -> none  [the longest x1 16.5 us: shards(): qa = lax.all_to_all(qa, 'dp', 0, 0)]
    all_to_all x2 -> x0, blocking collectives: 35 us -> none  [the longest x1 17.6 us: shards(): lax.all_to_all(jnp.broadcast_to(along_z, (nx, nz * few, d)), 'x', 0, 0)]
    ppermute x6 -> x25, starting transfers between devices: 2.81 us -> 37.6 us  [shift(): return lax.ppermute(x, axis, [(a, (a + by) % n) for a in range(n)])]
    all_to_all x4 -> x0, starting transfers between devices: 15.8 us -> none  [the longest x1 4.42 us: shards(): lax.all_to_all(jnp.broadcast_to(qdo_own, (dp,) + qdo_own.shape), 'dp', 0, 0)]
    ppermute x6 -> x25, waiting for transfers between devices: 5.48 us -> 19.4 us  [shift(): return lax.ppermute(x, axis, [(a, (a + by) % n) for a in range(n)])]
    pallas_call x2 -> x5, Pallas kernels: 15.2 us -> 25.3 us  [the longest x1 11.1 us: shards(): pl.pallas_call(weights_kernel, grid_spec=pltpu.PrefetchScalarGridSpec(num...]
    dot_general x4 -> x0, matrix products: 7.05 us -> none  [mm(): return lax.dot_general(a, b, dims, preferred_element_type=F32)]
    all_gather x1, waiting for transfers between devices: 5.02 us -> 0.02 us  [shards(): full = lax.all_gather(memory, ('z', 'x', 'core'), axis=0, tiled=True)]
  transfers between devices with their start and end apart: 12 -> 27, of which waited for: 9 -> 11; matrix products, arithmetic and copies ran while one was open for 11% -> 5% of each run, Pallas kernels for 4% -> 11%
where the time goes in v2:
time: 143 us; the launch traced here: 142 us
  starting transfers between devices  45.4 us (32%)
  Pallas kernels  27.2 us (19%)
  waiting for transfers between devices  25.5 us (18%)
  blocking collectives  19.2 us (13%)
  between operations  14.3 us (10%)
  local copies, waits for them, and re-layouts  7.45 us (5%)
  other arithmetic  3.31 us (2%)
    ppermute x25, starting transfers between devices, shift(): return lax.ppermute(x, axis, [(a, (a + by) % n) for a in range(n)])  37.6 us
    ppermute x25, waiting for transfers between devices, shift(): return lax.ppermute(x, axis, [(a, (a + by) % n) for a in range(n)])  19.4 us
    all_to_all x1, blocking collectives, shards(): lax.all_to_all(jnp.broadcast_to(quarter, (nz, few, d)), 'z', 0, 0)  19.2 us
    pallas_call x1, Pallas kernels, shards(): pl.pallas_call(weights_kernel, grid_spec=pltpu.PrefetchScalarGridSpec(num...  11.1 us
    all_to_all x1, starting transfers between devices, shards(): part = lax.all_to_all(part.reshape(nz, few, d), 'z', 0, 0)  7.72 us
    all_to_all x1, waiting for transfers between devices, shards(): part = lax.all_to_all(part.reshape(nz, few, d), 'z', 0, 0)  5.33 us
    pallas_call x1, Pallas kernels, shards(): pl.pallas_call(row_grads_kernel, out_shape=jax.ShapeDtypeStruct((dp,) + q...  4.34 us
    pallas_call x1, Pallas kernels, shards(): pl.pallas_call(token_grads_kernel, out_shape=jax.ShapeDtypeStruct((2 * ha...  4.03 us
  transfers between devices with their start and end apart: 27, of which 11 were waited for; matrix products, arithmetic and copies ran while one was open for 5% of the time, Pallas kernels for 11%

profile of v2, /device:TPU:32, one launch (start us, length us, event | category | flops | bytes accessed | tf_op | source)
XLA Modules:
  0.0 142.3 jit_solution(2611187179287997962)
XLA Ops:
  9.4 19.2 %all_to_all.10 = bf16[8,4,4096]{2,1,0:T(4,128)(2,1)} all-to-all(bf16[8,4,4096]{2,1,0:T(4,128)(2,1)S(1)} %broadcast_in_dim.3), channel_id=1, replica_groups=mesh['dp'=4,'z'=8,'x'=4,'core'=2] {'z'}, dimensions={0} | all-to-all | bytes 524288 | tf_op jit(solution)/shard_map/all_to_all | solution.py:171
  29.6 1.6 %collective-permute-start.2 = (bf16[32,4096]{1,0:T(8,128)(2,1)S(1)}, bf16[32,4096]{1,0:T(8,128)(2,1)S(1)}, u32[]{:S(2)}, u32[]{:S(2)}) collective-permute-start(bf16[32,4096]{1,0:T(8,128)(2,1)S(1)} %reshape.20.refs_0_), channel_id=1, source_target_pairs={{0,2},{2,4},{4,6},{6,0},{1,3},{3,5},{5,7},{7,1},{8,10},{10,12},{12... | collective-permute-start | bytes 786440 | tf_op jit(solution)/shard_map/ppermute | solution.py:21
  31.2 2.7 %collective-permute-start.3 = (bf16[32,4096]{1,0:T(8,128)(2,1)S(1)}, bf16[32,4096]{1,0:T(8,128)(2,1)S(1)}, u32[]{:S(2)}, u32[]{:S(2)}) collective-permute-start(bf16[32,4096]{1,0:T(8,128)(2,1)S(1)} %reshape.20.refs_0_), channel_id=1, source_target_pairs={{0,4},{2,6},{4,0},{6,2},{1,5},{3,7},{5,1},{7,3},{8,12},{10,14},{12... | collective-permute-start | bytes 786440 | tf_op jit(solution)/shard_map/ppermute | solution.py:21
  33.9 1.4 %collective-permute-start.4 = (bf16[32,4096]{1,0:T(8,128)(2,1)S(1)}, bf16[32,4096]{1,0:T(8,128)(2,1)S(1)}, u32[]{:S(2)}, u32[]{:S(2)}) collective-permute-start(bf16[32,4096]{1,0:T(8,128)(2,1)S(1)} %reshape.20.refs_0_), channel_id=1, source_target_pairs={{0,6},{2,0},{4,2},{6,4},{1,7},{3,1},{5,3},{7,5},{8,14},{10,8},{12,... | collective-permute-start | bytes 786440 | tf_op jit(solution)/shard_map/ppermute | solution.py:21
  36.4 1.7 %collective-permute-start.6 = (bf16[3,128,512]{2,1,0:T(8,128)(2,1)S(1)}, bf16[3,128,512]{2,1,0:T(8,128)(2,1)S(1)}, u32[]{:S(2)}, u32[]{:S(2)}) collective-permute-start(bf16[3,128,512]{2,1,0:T(8,128)(2,1)S(1)} %pad_maximum_fusion.refs_0_), channel_id=1, source_target_pairs={{0,64},{64,128},{128,192},{192,0},{1,65},{65,129},{129,193},{193,1... | collective-permute-start | bytes 1179656 | tf_op jit(solution)/shard_map/ppermute | solution.py:21
  38.1 2.9 %collective-permute-start.7 = (bf16[3,128,512]{2,1,0:T(8,128)(2,1)S(1)}, bf16[3,128,512]{2,1,0:T(8,128)(2,1)S(1)}, u32[]{:S(2)}, u32[]{:S(2)}) collective-permute-start(bf16[3,128,512]{2,1,0:T(8,128)(2,1)S(1)} %pad_maximum_fusion.refs_0_), channel_id=1, source_target_pairs={{0,128},{64,192},{128,0},{192,64},{1,129},{65,193},{129,1},{193,65... | collective-permute-start | bytes 1179656 | tf_op jit(solution)/shard_map/ppermute | solution.py:21
  41.0 2.0 %collective-permute-start.8 = (bf16[3,128,512]{2,1,0:T(8,128)(2,1)S(1)}, bf16[3,128,512]{2,1,0:T(8,128)(2,1)S(1)}, u32[]{:S(2)}, u32[]{:S(2)}) collective-permute-start(bf16[3,128,512]{2,1,0:T(8,128)(2,1)S(1)} %pad_maximum_fusion.refs_0_), channel_id=1, source_target_pairs={{0,192},{64,0},{128,64},{192,128},{1,193},{65,1},{129,65},{193,129... | collective-permute-start | bytes 1179656 | tf_op jit(solution)/shard_map/ppermute | solution.py:21
  43.0 1.5 %collective-permute-done.3.refs_2_ = bf16[32,4096]{1,0:T(8,128)(2,1)S(1)} collective-permute-done((bf16[32,4096]{1,0:T(8,128)(2,1)S(1)}, bf16[32,4096]{1,0:T(8,128)(2,1)S(1)}, u32[]{:S(2)}, u32[]{:S(2)}) %collective-permute-start.3) | collective-permute-done | bytes 262176 | tf_op jit(solution)/shard_map/ppermute | solution.py:21
  44.5 1.4 copy-done.1
  45.9 3.3 %shard_map.92 = (bf16[128,384]{1,0:T(8,128)(2,1)S(1)}, bf16[128,384]{1,0:T(8,128)(2,1)S(1)}) custom-call(bf16[3,64,4096]{2,1,0:T(8,128)(2,1)S(1)} %copy-done, bf16[3,64,4096]{2,1,0:T(8,128)(2,1)S(1)} %copy-done.1, bf16[3,64,4096]{2,1,0:T(8,128)(2,1)S(1)} %collective-permute-done.other_key, bf16[3,64,4096]{2,1,0:T(8,128)(2,1)} %collective-permute-done.1.other_value, ...), custom_call_target="tpu_custom_call" | custom-call | flops 805306368 | bytes 7340032 | tf_op jit(solution)/shard_map/pallas_call | solution.py:181
  50.6 4.3 %collective-permute-done.7.refs_2_ = bf16[3,128,512]{2,1,0:T(8,128)(2,1)S(1)} collective-permute-done((bf16[3,128,512]{2,1,0:T(8,128)(2,1)S(1)}, bf16[3,128,512]{2,1,0:T(8,128)(2,1)S(1)}, u32[]{:S(2)}, u32[]{:S(2)}) %collective-permute-start.7) | collective-permute-done | bytes 393248 | tf_op jit(solution)/shard_map/ppermute | solution.py:21
  54.9 1.9 %shard_map.93.refs_4_ = f32[8,2048]{1,0:T(8,128)S(1)} custom-call(bf16[128,384]{1,0:T(8,128)(2,1)S(1)} %get-tuple-element.20.own_ref, bf16[128,384]{1,0:T(8,128)(2,1)S(1)} %collective-permute-done.5.other_ref, bf16[3,128,512]{2,1,0:T(8,128)(2,1)S(1)} %pad_maximum_fusion.refs_0_, bf16[3,128,512]{2,1,0:T(8,128)(2,1)S(1)} %collective-permute-done.6.refs_1_, ...), custom_call_target="tpu_custom_call" | custom-call | flops 1610612736 | bytes 3145728 | tf_op jit(solution)/shard_map/pallas_call | solution.py:191
  56.9 1.3 collective-permute-start.9
  58.2 2.4 %collective-permute-start.10 = (f32[8,2048]{1,0:T(8,128)S(1)}, f32[8,2048]{1,0:T(8,128)S(1)}, u32[]{:S(2)}, u32[]{:S(2)}) collective-permute-start(f32[8,2048]{1,0:T(8,128)S(1)} %shard_map.93.refs_4_), channel_id=1, source_target_pairs={{0,128},{64,192},{128,0},{192,64},{1,129},{65,193},{129,1},{193,65... | collective-permute-start | bytes 196616 | tf_op jit(solution)/shard_map/ppermute | solution.py:21
  60.6 1.6 %collective-permute-start.11 = (f32[8,2048]{1,0:T(8,128)S(1)}, f32[8,2048]{1,0:T(8,128)S(1)}, u32[]{:S(2)}, u32[]{:S(2)}) collective-permute-start(f32[8,2048]{1,0:T(8,128)S(1)} %shard_map.93.refs_4_), channel_id=1, source_target_pairs={{0,192},{64,0},{128,64},{192,128},{1,193},{65,1},{129,65},{193,129... | collective-permute-start | bytes 196616 | tf_op jit(solution)/shard_map/ppermute | solution.py:21
  62.4 1.5 %collective-permute-done.10.refs_6_ = f32[8,2048]{1,0:T(8,128)S(1)} collective-permute-done((f32[8,2048]{1,0:T(8,128)S(1)}, f32[8,2048]{1,0:T(8,128)S(1)}, u32[]{:S(2)}, u32[]{:S(2)}) %collective-permute-start.10) | collective-permute-done | bytes 65568 | tf_op jit(solution)/shard_map/ppermute | solution.py:21
  64.9 4.0 %shard_map.94.own_ref.refs_0_ = bf16[256,384]{1,0:T(8,128)(2,1)S(1)} custom-call(bf16[128,384]{1,0:T(8,128)(2,1)S(1)} %get-tuple-element.20.own_ref, bf16[128,384]{1,0:T(8,128)(2,1)S(1)} %collective-permute-done.5.other_ref, bf16[3,128,512]{2,1,0:T(8,128)(2,1)S(1)} %pad_maximum_fusion.refs_0_, bf16[3,128,512]{2,1,0:T(8,128)(2,1)S(1)} %collective-permute-done.6.refs_1_, ...), custom_call_target="tpu_custom_call" | custom-call | flops 3221225472 | bytes 3145728 | tf_op jit(solution)/shard_map/pallas_call | solution.py:198
  70.2 2.1 %collective-permute-start.14 = (bf16[256,384]{1,0:T(8,128)(2,1)S(1)}, bf16[256,384]{1,0:T(8,128)(2,1)S(1)}, u32[]{:S(2)}, u32[]{:S(2)}) collective-permute-start(bf16[256,384]{1,0:T(8,128)(2,1)S(1)} %shard_map.94.own_ref.refs_0_), channel_id=1, source_target_pairs={{0,192},{64,0},{128,64},{192,128},{1,193},{65,1},{129,65},{193,129... | collective-permute-start | bytes 589832 | tf_op jit(solution)/shard_map/ppermute | solution.py:21
  72.4 2.6 %shard_map.95 = bf16[4,32,4096]{2,1,0:T(8,128)(2,1)S(1)} custom-call(bf16[256,384]{1,0:T(8,128)(2,1)S(1)} %shard_map.94.own_ref.refs_0_, bf16[128,384]{1,0:T(8,128)(2,1)S(1)} %collective-permute-done.12.other_ref, bf16[3,64,4096]{2,1,0:T(8,128)(2,1)S(1)} %copy-done, bf16[3,64,4096]{2,1,0:T(8,128)(2,1)S(1)} %copy-done.2, ...), custom_call_target="tpu_custom_call" | custom-call | flops 805306368 | bytes 7340032 | tf_op jit(solution)/shard_map/pallas_call | solution.py:206
  76.6 1.7 %collective-permute-start.18 = (bf16[32,4096]{1,0:T(8,128)(2,1)S(1)}, bf16[32,4096]{1,0:T(8,128)(2,1)S(1)}, u32[]{:S(2)}, u32[]{:S(2)}) collective-permute-start(bf16[32,4096]{1,0:T(8,128)(2,1)S(1)} %get-tuple-element.32), channel_id=1, source_target_pairs={{0,6},{2,0},{4,2},{6,4},{1,7},{3,1},{5,3},{7,5},{8,14},{10,8},{12,... | collective-permute-start | bytes 786440 | tf_op jit(solution)/shard_map/ppermute | solution.py:21
  78.4 4.3 %shard_map.96 = bf16[4,3,128,512]{3,2,1,0:T(8,128)(2,1)S(1)} custom-call(bf16[128,384]{1,0:T(8,128)(2,1)S(1)} %get-tuple-element.20.own_ref, bf16[128,384]{1,0:T(8,128)(2,1)S(1)} %collective-permute-done.5.other_ref, bf16[3,128,512]{2,1,0:T(8,128)(2,1)S(1)} %pad_maximum_fusion.refs_0_, bf16[3,128,512]{2,1,0:T(8,128)(2,1)S(1)} %collective-permute-done.6.refs_1_, ...), custom_call_target="tpu_custom_call" | custom-call | flops 3221225472 | bytes 6291456 | tf_op jit(solution)/shard_map/pallas_call | solution.py:216
  83.8 3.4 %collective-permute-start.16 = (bf16[3,128,512]{2,1,0:T(8,128)(2,1)S(1)}, bf16[3,128,512]{2,1,0:T(8,128)(2,1)}, u32[]{:S(2)}, u32[]{:S(2)}) collective-permute-start(bf16[3,128,512]{2,1,0:T(8,128)(2,1)S(1)} %get-tuple-element.31), channel_id=1, source_target_pairs={{0,128},{64,192},{128,0},{192,64},{1,129},{65,193},{129,1},{193,65... | collective-permute-start | bytes 1179656 | tf_op jit(solution)/shard_map/ppermute | solution.py:21
  87.2 2.8 %collective-permute-done.20 = bf16[32,4096]{1,0:T(8,128)(2,1)S(1)} collective-permute-done((bf16[32,4096]{1,0:T(8,128)(2,1)S(1)}, bf16[32,4096]{1,0:T(8,128)(2,1)S(1)}, u32[]{:S(2)}, u32[]{:S(2)}) %collective-permute-start.20) | collective-permute-done | bytes 262176 | tf_op jit(solution)/shard_map/ppermute | solution.py:21
  90.0 1.7 %collective-permute-start.15 = (bf16[3,128,512]{2,1,0:T(8,128)(2,1)S(1)}, bf16[3,128,512]{2,1,0:T(8,128)(2,1)}, u32[]{:S(2)}, u32[]{:S(2)}) collective-permute-start(bf16[3,128,512]{2,1,0:T(8,128)(2,1)S(1)} %get-tuple-element.29), channel_id=1, source_target_pairs={{0,192},{64,0},{128,64},{192,128},{1,193},{65,1},{129,65},{193,129... | collective-permute-start | bytes 1179656 | tf_op jit(solution)/shard_map/ppermute | solution.py:21
  91.8 2.8 %collective-permute-done.19 = bf16[32,4096]{1,0:T(8,128)(2,1)S(1)} collective-permute-done((bf16[32,4096]{1,0:T(8,128)(2,1)S(1)}, bf16[32,4096]{1,0:T(8,128)(2,1)S(1)}, u32[]{:S(2)}, u32[]{:S(2)}) %collective-permute-start.19) | collective-permute-done | bytes 262176 | tf_op jit(solution)/shard_map/ppermute | solution.py:21
  95.5 7.7 %all-to-all-start.1 = ((bf16[8,4,4096]{2,1,0:T(4,128)(2,1)}), bf16[8,4,4096]{2,1,0:T(4,128)(2,1)S(1)}, u32[]{:S(2)}, u32[]{:S(2)}) async-start(bf16[8,4,4096]{2,1,0:T(4,128)(2,1)} %reshape.21), calls=%async_computation.1 | async-start | bytes 524288 | tf_op jit(solution)/shard_map/all_to_all | solution.py:241
  103.8 2.8 %collective-permute-start.21 = (bf16[256,384]{1,0:T(8,128)(2,1)S(1)}, bf16[256,384]{1,0:T(8,128)(2,1)S(1)}, u32[]{:S(2)}, u32[]{:S(2)}) collective-permute-start(bf16[256,384]{1,0:T(8,128)(2,1)S(1)} %shard_map.94.own_ref.refs_0_), channel_id=1, source_target_pairs={{0,128},{64,192},{128,0},{192,64},{1,129},{65,193},{129,1},{193,65... | collective-permute-start | bytes 589832 | tf_op jit(solution)/shard_map/ppermute | solution.py:21
  106.6 1.4 %fusion.2 = bf16[3,128,512]{2,1,0:T(8,128)(2,1)S(1)} fusion(bf16[3,128,512]{2,1,0:T(8,128)(2,1)} %collective-permute-done.17, bf16[3,128,512]{2,1,0:T(8,128)(2,1)} %collective-permute-done.16, bf16[3,128,512]{2,1,0:T(8,128)(2,1)} %collective-permute-done.15, bf16[4,3,128,512]{3,2,1,0:T(8,128)(2,1)S(1)} %shard_map.96), kind=kLoop, calls=%fused_computation.3 | loop fusion | flops 1572864 | bytes 1966080 | tf_op jit(solution)/shard_map/convert_element_type | solution.py:247
  108.0 5.3 %all-to-all-done.1 = bf16[8,4,4096]{2,1,0:T(4,128)(2,1)S(1)} async-done(((bf16[8,4,4096]{2,1,0:T(4,128)(2,1)}), bf16[8,4,4096]{2,1,0:T(4,128)(2,1)S(1)}, u32[]{:S(2)}, u32[]{:S(2)}) %all-to-all-start.1) | async-done | bytes 262176 | tf_op jit(solution)/shard_map/all_to_all | solution.py:241
  114.2 11.1 %shard_map.97 = (f32[3,64,4096]{2,1,0:T(8,128)}, f32[3,64,4096]{2,1,0:T(8,128)}) custom-call(s32[3]{0:T(128)} %pad_add_fusion.at_ref, bf16[256,384]{1,0:T(8,128)(2,1)} %copy-done.3, bf16[256,384]{1,0:T(8,128)(2,1)} %copy-done.4, bf16[256,384]{1,0:T(8,128)(2,1)} %copy-done.6, bf16[256,384]{1,0:T(8,128)(2,1)} %copy-done.5, ...), custom_call_target="tpu_custom_call" | custom-call | flops 3221225472 | bytes 14680064 | tf_op jit(solution)/shard_map/pallas_call | solution.py:227
  125.2 2.8 %collective-permute-start.22 = (f32[4,4096]{1,0:T(4,128)S(1)}, f32[4,4096]{1,0:T(4,128)S(1)}, u32[]{:S(2)}, u32[]{:S(2)}) collective-permute-start(f32[4,4096]{1,0:T(4,128)S(1)} %convert_reduce_fusion), channel_id=1, source_target_pairs={{0,192},{64,0},{128,64},{192,128},{1,193},{65,1},{129,65},{193,129... | collective-permute-start | bytes 196616 | tf_op jit(solution)/shard_map/ppermute | solution.py:21
  130.5 3.3 %collective-permute-done.23 = f32[4,4096]{1,0:T(4,128)S(1)} collective-permute-done((f32[4,4096]{1,0:T(4,128)S(1)}, f32[4,4096]{1,0:T(4,128)S(1)}, u32[]{:S(2)}, u32[]{:S(2)}) %collective-permute-start.23) | collective-permute-done | bytes 65568 | tf_op jit(solution)/shard_map/ppermute | solution.py:21
  (59 shorter events, 17.3 us)
Async XLA Ops:
  7.2 37.3 %copy-start = (bf16[3,64,4096]{2,1,0:T(8,128)(2,1)S(1)}, bf16[3,64,4096]{2,1,0:T(8,128)(2,1)}, u32[]{:S(2)}) copy-start(bf16[3,64,4096]{2,1,0:T(8,128)(2,1)} %own_key.3) | copy-start | bytes 4718596
  7.2 106.3 %all-gather.2.cloned.1.call-start = ((), (), s32[]{:S(2)}) async-start(), calls=%async_computation.2 | async-start | bytes 8519680 | tf_op jit(solution)/shard_map/all_gather | solution.py:168
  7.9 21.7 %collective-permute-start = (bf16[3,64,4096]{2,1,0:T(8,128)(2,1)}, bf16[3,64,4096]{2,1,0:T(8,128)(2,1)S(1)}, u32[]{:S(2)}, u32[]{:S(2)}) collective-permute-start(bf16[3,64,4096]{2,1,0:T(8,128)(2,1)} %own_key.3), channel_id=1, source_target_pairs={{0,1},{1,0},{2,3},{3,2},{4,5},{5,4},{6,7},{7,6},{8,9},{9,8},{10,11... | collective-permute-start | bytes 4718600 | tf_op jit(solution)/shard_map/ppermute | solution.py:21
  8.0 21.6 %collective-permute-start.1 = (bf16[3,64,4096]{2,1,0:T(8,128)(2,1)}, bf16[3,64,4096]{2,1,0:T(8,128)(2,1)}, u32[]{:S(2)}, u32[]{:S(2)}) collective-permute-start(bf16[3,64,4096]{2,1,0:T(8,128)(2,1)} %own_value.3), channel_id=1, source_target_pairs={{0,1},{1,0},{2,3},{3,2},{4,5},{5,4},{6,7},{7,6},{8,9},{9,8},{10,11... | collective-permute-start | bytes 4718600 | tf_op jit(solution)/shard_map/ppermute | solution.py:21
  29.6 11.4 %collective-permute-start.2 = (bf16[32,4096]{1,0:T(8,128)(2,1)S(1)}, bf16[32,4096]{1,0:T(8,128)(2,1)S(1)}, u32[]{:S(2)}, u32[]{:S(2)}) collective-permute-start(bf16[32,4096]{1,0:T(8,128)(2,1)S(1)} %reshape.20.refs_0_), channel_id=1, source_target_pairs={{0,2},{2,4},{4,6},{6,0},{1,3},{3,5},{5,7},{7,1},{8,10},{10,12},{12... | collective-permute-start | bytes 786440 | tf_op jit(solution)/shard_map/ppermute | solution.py:21
  31.2 13.3 %collective-permute-start.3 = (bf16[32,4096]{1,0:T(8,128)(2,1)S(1)}, bf16[32,4096]{1,0:T(8,128)(2,1)S(1)}, u32[]{:S(2)}, u32[]{:S(2)}) collective-permute-start(bf16[32,4096]{1,0:T(8,128)(2,1)S(1)} %reshape.20.refs_0_), channel_id=1, source_target_pairs={{0,4},{2,6},{4,0},{6,2},{1,5},{3,7},{5,1},{7,3},{8,12},{10,14},{12... | collective-permute-start | bytes 786440 | tf_op jit(solution)/shard_map/ppermute | solution.py:21
  33.9 10.6 %collective-permute-start.4 = (bf16[32,4096]{1,0:T(8,128)(2,1)S(1)}, bf16[32,4096]{1,0:T(8,128)(2,1)S(1)}, u32[]{:S(2)}, u32[]{:S(2)}) collective-permute-start(bf16[32,4096]{1,0:T(8,128)(2,1)S(1)} %reshape.20.refs_0_), channel_id=1, source_target_pairs={{0,6},{2,0},{4,2},{6,4},{1,7},{3,1},{5,3},{7,5},{8,14},{10,8},{12,... | collective-permute-start | bytes 786440 | tf_op jit(solution)/shard_map/ppermute | solution.py:21
  36.4 14.2 %collective-permute-start.6 = (bf16[3,128,512]{2,1,0:T(8,128)(2,1)S(1)}, bf16[3,128,512]{2,1,0:T(8,128)(2,1)S(1)}, u32[]{:S(2)}, u32[]{:S(2)}) collective-permute-start(bf16[3,128,512]{2,1,0:T(8,128)(2,1)S(1)} %pad_maximum_fusion.refs_0_), channel_id=1, source_target_pairs={{0,64},{64,128},{128,192},{192,0},{1,65},{65,129},{129,193},{193,1... | collective-permute-start | bytes 1179656 | tf_op jit(solution)/shard_map/ppermute | solution.py:21
  38.1 16.8 %collective-permute-start.7 = (bf16[3,128,512]{2,1,0:T(8,128)(2,1)S(1)}, bf16[3,128,512]{2,1,0:T(8,128)(2,1)S(1)}, u32[]{:S(2)}, u32[]{:S(2)}) collective-permute-start(bf16[3,128,512]{2,1,0:T(8,128)(2,1)S(1)} %pad_maximum_fusion.refs_0_), channel_id=1, source_target_pairs={{0,128},{64,192},{128,0},{192,64},{1,129},{65,193},{129,1},{193,65... | collective-permute-start | bytes 1179656 | tf_op jit(solution)/shard_map/ppermute | solution.py:21
  41.0 13.9 %collective-permute-start.8 = (bf16[3,128,512]{2,1,0:T(8,128)(2,1)S(1)}, bf16[3,128,512]{2,1,0:T(8,128)(2,1)S(1)}, u32[]{:S(2)}, u32[]{:S(2)}) collective-permute-start(bf16[3,128,512]{2,1,0:T(8,128)(2,1)S(1)} %pad_maximum_fusion.refs_0_), channel_id=1, source_target_pairs={{0,192},{64,0},{128,64},{192,128},{1,193},{65,1},{129,65},{193,129... | collective-permute-start | bytes 1179656 | tf_op jit(solution)/shard_map/ppermute | solution.py:21
  49.2 1.4 collective-permute-start.5
  56.9 15.5 %copy-start.2 = (bf16[3,64,4096]{2,1,0:T(8,128)(2,1)S(1)}, bf16[3,64,4096]{2,1,0:T(8,128)(2,1)}, u32[]{:S(2)}) copy-start(bf16[3,64,4096]{2,1,0:T(8,128)(2,1)} %own_value.3) | copy-start | bytes 4718596
  56.9 5.6 %collective-permute-start.9 = (f32[8,2048]{1,0:T(8,128)S(1)}, f32[8,2048]{1,0:T(8,128)S(1)}, u32[]{:S(2)}, u32[]{:S(2)}) collective-permute-start(f32[8,2048]{1,0:T(8,128)S(1)} %shard_map.93.refs_4_), channel_id=1, source_target_pairs={{0,64},{64,128},{128,192},{192,0},{1,65},{65,129},{129,193},{193,1... | collective-permute-start | bytes 196616 | tf_op jit(solution)/shard_map/ppermute | solution.py:21
  58.2 5.8 %collective-permute-start.10 = (f32[8,2048]{1,0:T(8,128)S(1)}, f32[8,2048]{1,0:T(8,128)S(1)}, u32[]{:S(2)}, u32[]{:S(2)}) collective-permute-start(f32[8,2048]{1,0:T(8,128)S(1)} %shard_map.93.refs_4_), channel_id=1, source_target_pairs={{0,128},{64,192},{128,0},{192,64},{1,129},{65,193},{129,1},{193,65... | collective-permute-start | bytes 196616 | tf_op jit(solution)/shard_map/ppermute | solution.py:21
  60.6 4.3 %collective-permute-start.11 = (f32[8,2048]{1,0:T(8,128)S(1)}, f32[8,2048]{1,0:T(8,128)S(1)}, u32[]{:S(2)}, u32[]{:S(2)}) collective-permute-start(f32[8,2048]{1,0:T(8,128)S(1)} %shard_map.93.refs_4_), channel_id=1, source_target_pairs={{0,192},{64,0},{128,64},{192,128},{1,193},{65,1},{129,65},{193,129... | collective-permute-start | bytes 196616 | tf_op jit(solution)/shard_map/ppermute | solution.py:21
  68.9 34.9 %copy-start.3 = (bf16[256,384]{1,0:T(8,128)(2,1)}, bf16[256,384]{1,0:T(8,128)(2,1)S(1)}, u32[]{:S(2)}) copy-start(bf16[256,384]{1,0:T(8,128)(2,1)S(1)} %shard_map.94.own_ref.refs_0_) | copy-start | bytes 589828
  68.9 3.4 %collective-permute-start.12 = (bf16[128,384]{1,0:T(8,128)(2,1)S(1)}, bf16[128,384]{1,0:T(8,128)(2,1)S(1)}, u32[]{:S(2)}, u32[]{:S(2)}) collective-permute-start(bf16[128,384]{1,0:T(8,128)(2,1)S(1)} %slice.44), channel_id=1, source_target_pairs={{0,1},{1,0},{2,3},{3,2},{4,5},{5,4},{6,7},{7,6},{8,9},{9,8},{10,11... | collective-permute-start | bytes 294920 | tf_op jit(solution)/shard_map/ppermute | solution.py:21
  69.0 9.3 %collective-permute-start.13 = (bf16[256,384]{1,0:T(8,128)(2,1)S(1)}, bf16[256,384]{1,0:T(8,128)(2,1)S(1)}, u32[]{:S(2)}, u32[]{:S(2)}) collective-permute-start(bf16[256,384]{1,0:T(8,128)(2,1)S(1)} %shard_map.94.own_ref.refs_0_), channel_id=1, source_target_pairs={{0,64},{64,128},{128,192},{192,0},{1,65},{65,129},{129,193},{193,1... | collective-permute-start | bytes 589832 | tf_op jit(solution)/shard_map/ppermute | solution.py:21
  70.2 8.1 %collective-permute-start.14 = (bf16[256,384]{1,0:T(8,128)(2,1)S(1)}, bf16[256,384]{1,0:T(8,128)(2,1)S(1)}, u32[]{:S(2)}, u32[]{:S(2)}) collective-permute-start(bf16[256,384]{1,0:T(8,128)(2,1)S(1)} %shard_map.94.own_ref.refs_0_), channel_id=1, source_target_pairs={{0,192},{64,0},{128,64},{192,128},{1,193},{65,1},{129,65},{193,129... | collective-permute-start | bytes 589832 | tf_op jit(solution)/shard_map/ppermute | solution.py:21
  75.0 15.0 %collective-permute-start.20 = (bf16[32,4096]{1,0:T(8,128)(2,1)S(1)}, bf16[32,4096]{1,0:T(8,128)(2,1)S(1)}, u32[]{:S(2)}, u32[]{:S(2)}) collective-permute-start(bf16[32,4096]{1,0:T(8,128)(2,1)S(1)} %get-tuple-element.33), channel_id=1, source_target_pairs={{0,2},{2,4},{4,6},{6,0},{1,3},{3,5},{5,7},{7,1},{8,10},{10,12},{12... | collective-permute-start | bytes 786440 | tf_op jit(solution)/shard_map/ppermute | solution.py:21
  75.6 19.0 %collective-permute-start.19 = (bf16[32,4096]{1,0:T(8,128)(2,1)S(1)}, bf16[32,4096]{1,0:T(8,128)(2,1)S(1)}, u32[]{:S(2)}, u32[]{:S(2)}) collective-permute-start(bf16[32,4096]{1,0:T(8,128)(2,1)S(1)} %get-tuple-element.34), channel_id=1, source_target_pairs={{0,4},{2,6},{4,0},{6,2},{1,5},{3,7},{5,1},{7,3},{8,12},{10,14},{12... | collective-permute-start | bytes 786440 | tf_op jit(solution)/shard_map/ppermute | solution.py:21
  76.6 17.9 %collective-permute-start.18 = (bf16[32,4096]{1,0:T(8,128)(2,1)S(1)}, bf16[32,4096]{1,0:T(8,128)(2,1)S(1)}, u32[]{:S(2)}, u32[]{:S(2)}) collective-permute-start(bf16[32,4096]{1,0:T(8,128)(2,1)S(1)} %get-tuple-element.32), channel_id=1, source_target_pairs={{0,6},{2,0},{4,2},{6,4},{1,7},{3,1},{5,3},{7,5},{8,14},{10,8},{12,... | collective-permute-start | bytes 786440 | tf_op jit(solution)/shard_map/ppermute | solution.py:21
  78.3 4.4 %copy-start.4 = (bf16[256,384]{1,0:T(8,128)(2,1)}, bf16[256,384]{1,0:T(8,128)(2,1)S(1)}, u32[]{:S(2)}) copy-start(bf16[256,384]{1,0:T(8,128)(2,1)S(1)} %collective-permute-done.13.refs_1_) | copy-start | bytes 589828
  78.4 4.4 %copy-start.5 = (bf16[256,384]{1,0:T(8,128)(2,1)}, bf16[256,384]{1,0:T(8,128)(2,1)S(1)}, u32[]{:S(2)}) copy-start(bf16[256,384]{1,0:T(8,128)(2,1)S(1)} %collective-permute-done.14.refs_3_) | copy-start | bytes 589828
  83.6 23.0 %collective-permute-start.17 = (bf16[3,128,512]{2,1,0:T(8,128)(2,1)}, bf16[3,128,512]{2,1,0:T(8,128)(2,1)}, u32[]{:S(2)}, u32[]{:S(2)}) collective-permute-start(bf16[3,128,512]{2,1,0:T(8,128)(2,1)} %get-tuple-element.30), channel_id=1, source_target_pairs={{0,64},{64,128},{128,192},{192,0},{1,65},{65,129},{129,193},{193,1... | collective-permute-start | bytes 1179656 | tf_op jit(solution)/shard_map/ppermute | solution.py:21
  83.8 22.8 %collective-permute-start.16 = (bf16[3,128,512]{2,1,0:T(8,128)(2,1)S(1)}, bf16[3,128,512]{2,1,0:T(8,128)(2,1)}, u32[]{:S(2)}, u32[]{:S(2)}) collective-permute-start(bf16[3,128,512]{2,1,0:T(8,128)(2,1)S(1)} %get-tuple-element.31), channel_id=1, source_target_pairs={{0,128},{64,192},{128,0},{192,64},{1,129},{65,193},{129,1},{193,65... | collective-permute-start | bytes 1179656 | tf_op jit(solution)/shard_map/ppermute | solution.py:21
  90.0 16.6 %collective-permute-start.15 = (bf16[3,128,512]{2,1,0:T(8,128)(2,1)S(1)}, bf16[3,128,512]{2,1,0:T(8,128)(2,1)}, u32[]{:S(2)}, u32[]{:S(2)}) collective-permute-start(bf16[3,128,512]{2,1,0:T(8,128)(2,1)S(1)} %get-tuple-element.29), channel_id=1, source_target_pairs={{0,192},{64,0},{128,64},{192,128},{1,193},{65,1},{129,65},{193,129... | collective-permute-start | bytes 1179656 | tf_op jit(solution)/shard_map/ppermute | solution.py:21
  95.5 17.9 %all-to-all-start.1 = ((bf16[8,4,4096]{2,1,0:T(4,128)(2,1)}), bf16[8,4,4096]{2,1,0:T(4,128)(2,1)S(1)}, u32[]{:S(2)}, u32[]{:S(2)}) async-start(bf16[8,4,4096]{2,1,0:T(4,128)(2,1)} %reshape.21), calls=%async_computation.1 | async-start | bytes 524288 | tf_op jit(solution)/shard_map/all_to_all | solution.py:241
  103.8 9.7 %collective-permute-start.21 = (bf16[256,384]{1,0:T(8,128)(2,1)S(1)}, bf16[256,384]{1,0:T(8,128)(2,1)S(1)}, u32[]{:S(2)}, u32[]{:S(2)}) collective-permute-start(bf16[256,384]{1,0:T(8,128)(2,1)S(1)} %shard_map.94.own_ref.refs_0_), channel_id=1, source_target_pairs={{0,128},{64,192},{128,0},{192,64},{1,129},{65,193},{129,1},{193,65... | collective-permute-start | bytes 589832 | tf_op jit(solution)/shard_map/ppermute | solution.py:21
  125.2 5.3 %collective-permute-start.22 = (f32[4,4096]{1,0:T(4,128)S(1)}, f32[4,4096]{1,0:T(4,128)S(1)}, u32[]{:S(2)}, u32[]{:S(2)}) collective-permute-start(f32[4,4096]{1,0:T(4,128)S(1)} %convert_reduce_fusion), channel_id=1, source_target_pairs={{0,192},{64,0},{128,64},{192,128},{1,193},{65,1},{129,65},{193,129... | collective-permute-start | bytes 196616 | tf_op jit(solution)/shard_map/ppermute | solution.py:21
  128.0 5.8 %collective-permute-start.23 = (f32[4,4096]{1,0:T(4,128)S(1)}, f32[4,4096]{1,0:T(4,128)S(1)}, u32[]{:S(2)}, u32[]{:S(2)}) collective-permute-start(f32[4,4096]{1,0:T(4,128)S(1)} %convert_reduce_fusion), channel_id=1, source_target_pairs={{0,128},{64,192},{128,0},{192,64},{1,129},{65,193},{129,1},{193,65... | collective-permute-start | bytes 196616 | tf_op jit(solution)/shard_map/ppermute | solution.py:21
  128.8 5.7 %collective-permute-start.24 = (f32[4,4096]{1,0:T(4,128)S(1)}, f32[4,4096]{1,0:T(4,128)S(1)}, u32[]{:S(2)}, u32[]{:S(2)}) collective-permute-start(f32[4,4096]{1,0:T(4,128)S(1)} %convert_reduce_fusion), channel_id=1, source_target_pairs={{0,64},{64,128},{128,192},{192,0},{1,65},{65,129},{129,193},{193,1... | collective-permute-start | bytes 196616 | tf_op jit(solution)/shard_map/ppermute | solution.py:21
  (2 other events, 2.1 us)
Sparse Core Ops, SparseCore 0:
  10.8 88.7 all-gather.1

commit v3 on v2

--- a/solution.py
+++ b/solution.py
@@ -45,15 +45,16 @@
             out_ref[:, at : at + 2 * width] = mm(w, mem, NT).T.astype(BF16)
 
 
-def memory_kernel(own_ref, other_ref, own_key, own_value, other_key, other_value, out_ref):
+def memory_kernel(own_ref, other_ref, own_key, own_value, other_key, other_value, *out_refs):
     layers, width, d = own_key.shape
-    blocks, rows, _ = out_ref.shape
+    blocks, rows = len(out_refs), out_refs[0].shape[0]
     g = jnp.concatenate([own_ref[: blocks * rows], other_ref[...]], axis=1)
     step = 512
     for at in range(0, d, step):
         w = [r[layer, :, at : at + step] for k, v in ((own_key, own_value), (other_key, other_value)) for layer in range(layers) for r in (k, v)]
         out = mm(g, jnp.concatenate(w, axis=0)).astype(BF16)
-        out_ref[:, :, at : at + step] = out.reshape(blocks, rows, step)
+        for x, out_ref in enumerate(out_refs):
+            out_ref[:, at : at + step] = out[x * rows : (x + 1) * rows]
 
 
 def stats_kernel(own_ref, other_ref, *refs):
@@ -94,55 +95,47 @@
     return jnp.concatenate([dscores.astype(BF16), probs.astype(BF16)], axis=0)
 
 
-def token_grads_kernel(own_ref, other_ref, *refs):
-    *qdo_refs, s0, s1, s2, s3, g_ref = refs
+def grads_kernel(own_ref, other_ref, *refs):
+    n = len(refs) // 3
+    qdo_refs, stats_refs, g_ref, qa_refs = refs[:n], refs[n : 2 * n], refs[2 * n], refs[2 * n + 1 :]
     layers, width, rows = qdo_refs[0].shape
     tokens = 2 * own_ref.shape[0]
     left = lax.broadcasted_iota(jnp.int32, (tokens, width), 1) < HEAD_WIDTH
-    stats = list(combine((s0, s1, s2, s3), rows, layers))
-    for layer in range(layers):
-        keys, values = split_heads(own_ref, other_ref, layer)
-        acc = 0.0
-        for qdo_ref, (lse, delta) in zip(qdo_refs, stats):
-            q = qdo_ref[layer]
-            acc += mm(probs_and_scores(keys, values, q, lse[layer : layer + 1], delta[layer : layer + 1]), q, NT)
-        g_ref[:, layer * width : (layer + 1) * width] = jnp.where(left, acc[:tokens], acc[tokens:]).astype(BF16)
-
-
-def row_grads_kernel(own_ref, other_ref, *refs):
-    *qdo_refs, s0, s1, s2, s3, qa_ref = refs
-    layers, _, rows = qdo_refs[0].shape
-    stats = list(combine((s0, s1, s2, s3), rows, layers))
+    stats = list(combine(stats_refs, rows, layers))
     for layer in range(layers):
         keys, values = split_heads(own_ref, other_ref, layer)
         flipped = jnp.concatenate([keys, values], axis=0).astype(F32).T.astype(BF16)
+        acc = 0.0
         for part, (qdo_ref, (lse, delta)) in enumerate(zip(qdo_refs, stats)):
-            both = probs_and_scores(keys, values, qdo_ref[layer], lse[layer : layer + 1], delta[layer : layer + 1])
-            qa_ref[part, layer] = mm(flipped, both).astype(BF16)
-
-
-def weights_kernel(at_ref, *refs):
-    *g_refs, mem_ref, key_ref, value_ref, stack, order, flipped = refs
-    ndp, nx, nz, few = len(g_refs), 4, 8, 4
+            q = qdo_ref[layer]
+            both = probs_and_scores(keys, values, q, lse[layer : layer + 1], delta[layer : layer + 1])
+            acc += mm(both, q, NT)
+            qa_refs[part][layer] = mm(flipped, both).astype(BF16)
+        g_ref[:, layer * width : (layer + 1) * width] = jnp.where(left, acc[:tokens], acc[tokens:]).astype(BF16)
+
+
+def order_kernel(at_ref, *refs):
+    *g_refs, out_ref, stack, order = refs
+    ndp, nx, nz, few = 2 * len(g_refs), 4, 8, 4
+    for pair, g_ref in enumerate(g_refs):
+        for part in range(2):
+            stack[2 * pair + part] = g_ref[part].astype(F32)
+    parts = [lax.bitwise_xor(at_ref[0], dp) for dp in range(ndp)]
+    for half in range(2):
+        core = at_ref[2] if half == 0 else 1 - at_ref[2]
+        for back in range(nx):
+            x = lax.rem(at_ref[1] + nx - back, nx)
+            first = (half * nx + back) * nz * few
+            blocks = [stack[part, first : first + nz * few] for part in parts]
+            for z in range(nz):
+                to = pl.multiple_of(((z * nx + x) * 2 + core) * ndp * few, ndp * few)
+                order[pl.ds(to, ndp * few)] = jnp.concatenate([b[z * few : (z + 1) * few] for b in blocks], axis=0)
+    out_ref[...] = order[...].T.astype(BF16)
+
+
+def weights_kernel(g_ref, mem_ref, key_ref, value_ref):
     layers, width, _ = key_ref.shape
-
-    @pl.when(pl.program_id(0) == 0)
-    def _():
-        for part, g_ref in enumerate(g_refs):
-            stack[part] = g_ref[...].astype(F32)
-        parts = [lax.rem(at_ref[0] + ndp - dp, ndp) for dp in range(ndp)]
-        for half in range(2):
-            core = at_ref[2] if half == 0 else 1 - at_ref[2]
-            for back in range(nx):
-                x = lax.rem(at_ref[1] + nx - back, nx)
-                first = (half * nx + back) * nz * few
-                blocks = [stack[part, first : first + nz * few] for part in parts]
-                for z in range(nz):
-                    to = pl.multiple_of(((z * nx + x) * 2 + core) * ndp * few, ndp * few)
-                    order[pl.ds(to, ndp * few)] = jnp.concatenate([b[z * few : (z + 1) * few] for b in blocks], axis=0)
-        flipped[...] = order[...].T.astype(BF16)
-
-    out = mm(flipped[...], mem_ref[...])
+    out = mm(g_ref[...], mem_ref[...])
     for layer in range(layers):
         at = 2 * layer * width
         key_ref[layer] = out[at : at + width]
@@ -195,55 +188,56 @@
         cost_estimate=cost(4 * work, 4 * dp * qdo[0].size, layers * all_rows * 2 * half),
     )(kv_own, kv_other, *qdo)
     others = [shift(stats, "dp", s) for s in range(1, dp)]
-    g = pl.pallas_call(
-        token_grads_kernel,
-        out_shape=jax.ShapeDtypeStruct((2 * half, cols), BF16),
-        compiler_params=params,
-        cost_estimate=cost(8 * work, 4 * dp * qdo[0].size, layers * all_rows * 2 * half),
+    g, *qa = pl.pallas_call(
+        grads_kernel,
+        out_shape=[jax.ShapeDtypeStruct((2 * half, cols), BF16)] + [jax.ShapeDtypeStruct(qdo[0].shape, BF16)] * dp,
+        compiler_params=params,
+        cost_estimate=cost(12 * work, 8 * dp * qdo[0].size, layers * all_rows * 2 * half),
     )(kv_own, kv_other, *qdo, stats, *others)
 
     g_other = shift(g[half:], "core", 1)
     part = pl.pallas_call(
         memory_kernel,
-        out_shape=jax.ShapeDtypeStruct((nx, nz * few, d), BF16),
+        out_shape=[jax.ShapeDtypeStruct((nz * few, d), BF16)] * nx,
         compiler_params=params,
         cost_estimate=cost(4 * half * cols * d, 2 * (half + 2 * cols) * d),
     )(g, g_other, *weights)
-    g_all = [g] + [shift(g, "dp", s) for s in range(1, dp)]
-    stats = after(stats, part, g_all[1], g_all[3])
+    g_all = jnp.stack([g, lax.ppermute(g, "dp", [(a, a ^ 1) for a in range(dp)])])
+    g_all = (g_all, lax.ppermute(g_all, "dp", [(a, a ^ 2) for a in range(dp)]))
     part = sum([part[0].astype(F32)] + [shift(part[s], "x", -s).astype(F32) for s in range(1, nx)]).astype(BF16)
 
-    qa = pl.pallas_call(
-        row_grads_kernel,
-        out_shape=jax.ShapeDtypeStruct((dp,) + qdo[0].shape, BF16),
-        compiler_params=params,
-        cost_estimate=cost(8 * work, 8 * dp * qdo[0].size, layers * all_rows * 2 * half),
-    )(kv_own, kv_other, *qdo, stats, *others)
-    qa = [qa[0]] + [shift(qa[s], "dp", -s) for s in range(1, dp)]
-
-    block = 512
+    flipped = pl.pallas_call(
+        order_kernel,
+        in_specs=[pl.BlockSpec(memory_space=pltpu.SMEM)] + [pl.BlockSpec(memory_space=pltpu.VMEM)] * 2,
+        out_shape=jax.ShapeDtypeStruct((cols, full.shape[0]), BF16),
+        scratch_shapes=[pltpu.VMEM((dp,) + g.shape, F32), pltpu.VMEM((full.shape[0], cols), F32)],
+        compiler_params=params,
+        cost_estimate=cost(0, 8 * cols * full.shape[0]),
+    )(at, *g_all)
+    block = 1024
     gw_shape = jax.ShapeDtypeStruct((layers, width, d), F32)
-    gw_spec = pl.BlockSpec((layers, width, block), lambda n, at: (0, 0, n))
+    gw_spec = pl.BlockSpec((layers, width, block), lambda n: (0, 0, n))
     grad_w = pl.pallas_call(
         weights_kernel,
-        grid_spec=pltpu.PrefetchScalarGridSpec(
-            num_scalar_prefetch=1,
-            grid=(d // block,),
-            in_specs=[pl.BlockSpec(g.shape, lambda n, at: (0, 0))] * dp + [pl.BlockSpec((full.shape[0], block), lambda n, at: (0, n))],
-            out_specs=(gw_spec, gw_spec),
-            scratch_shapes=[pltpu.VMEM((dp,) + g.shape, F32), pltpu.VMEM((full.shape[0], cols), F32), pltpu.VMEM((cols, full.shape[0]), BF16)],
-        ),
+        grid=(d // block,),
+        in_specs=[pl.BlockSpec(flipped.shape, lambda n: (0, 0)), pl.BlockSpec((full.shape[0], block), lambda n: (0, n))],
+        out_specs=(gw_spec, gw_spec),
         out_shape=(gw_shape, gw_shape),
         compiler_params=pltpu.CompilerParams(vmem_limit_bytes=56 * 1024 * 1024),
         cost_estimate=cost(2 * cols * full.size, 2 * full.size + 4 * cols * d),
-    )(at, *g_all, full)
+    )(flipped, full)
+
+    qa[1], qa[3] = shift(qa[1], "dp", -1), shift(qa[3], "dp", -3)
+    part, *qa = lax.optimization_barrier((part, *qa))
+    qa[2] = shift(qa[2], "dp", -2)
 
     part = lax.all_to_all(part.reshape(nz, few, d), "z", 0, 0)
+    part, grad_w_key, grad_w_value = lax.optimization_barrier((part, *grad_w))
     part = jnp.sum(part.astype(F32), axis=0)
-    part, grad_w_key, grad_w_value = lax.optimization_barrier((part, *grad_w))
     parts = [part] + [shift(part, "dp", s) for s in range(1, dp)]
     parts = jnp.concatenate([parts[-1 - j % dp] for j in range(2 * dp - 1)], axis=0)
     grad_memory = lax.dynamic_slice(parts, ((dp - 1 - here) * few, 0), (mine, d))
+    part, *qa = lax.optimization_barrier((part, *qa))
     qa = sum(a.astype(F32) for a in qa).astype(BF16)
     grad_queries, attended = qa[:, :width].swapaxes(1, 2), qa[:, width:].swapaxes(1, 2)
     return (attended, grad_queries, grad_memory, grad_w_key, grad_w_value)

time: 143 us -> 134 us (0.937); the launches traced: 142 us -> 132 us
  starting transfers between devices: 45.4 us -> 37.8 us
  Pallas kernels: 27.2 us -> 22.4 us
  waiting for transfers between devices: 25.5 us -> 29.7 us
  other arithmetic: 3.31 us -> 1.62 us
    ppermute x25 -> x22, starting transfers between devices: 37.6 us -> 25.5 us  [shift(): return lax.ppermute(x, axis, [(a, (a + by) % n) for a in range(n)])]
    ppermute x25 -> x22, waiting for transfers between devices: 19.4 us -> 29 us  [shift(): return lax.ppermute(x, axis, [(a, (a + by) % n) for a in range(n)])]
    all_to_all x1, waiting for transfers between devices: 5.33 us -> 0.01 us  [shards(): part = lax.all_to_all(part.reshape(nz, few, d), 'z', 0, 0)]
    pallas_call x4, Pallas kernels: 22 us -> 17.2 us  [the longest x1 8.55 us: shards(): pl.pallas_call(weights_kernel, grid=(d // block,), in_specs=[pl.BlockSpec...]
    ppermute x0 -> x2, starting transfers between devices: none -> 3.09 us  [the longest x1 2.29 us: shards(): g_all = (g_all, lax.ppermute(g_all, 'dp', [(a, a ^ 2) for a in range(dp)]))]
    all_to_all x1, starting transfers between devices: 7.72 us -> 9.2 us  [shards(): part = lax.all_to_all(part.reshape(nz, few, d), 'z', 0, 0)]
  transfers between devices with their start and end apart: 27 -> 26, of which waited for: 11 -> 12; matrix products, arithmetic and copies ran while one was open for 5% -> 4% of each run, Pallas kernels for 11% -> 17%
where the time goes in v3:
time: 134 us; the launch traced here: 132 us
  starting transfers between devices  37.8 us (28%)
  waiting for transfers between devices  29.7 us (22%)
  Pallas kernels  22.4 us (17%)
  blocking collectives  19.2 us (14%)
  between operations  14.2 us (11%)
  local copies, waits for them, and re-layouts  6.84 us (5%)
  other arithmetic  1.62 us (1%)
    ppermute x22, waiting for transfers between devices, shift(): return lax.ppermute(x, axis, [(a, (a + by) % n) for a in range(n)])  29 us
    ppermute x22, starting transfers between devices, shift(): return lax.ppermute(x, axis, [(a, (a + by) % n) for a in range(n)])  25.5 us
    all_to_all x1, blocking collectives, shards(): lax.all_to_all(jnp.broadcast_to(quarter, (nz, few, d)), 'z', 0, 0)  19.2 us
    all_to_all x1, starting transfers between devices, shards(): part = lax.all_to_all(part.reshape(nz, few, d), 'z', 0, 0)  9.2 us
    pallas_call x1, Pallas kernels, shards(): pl.pallas_call(weights_kernel, grid=(d // block,), in_specs=[pl.BlockSpec...  8.55 us
    pallas_call x1, Pallas kernels, shards(): pl.pallas_call(grads_kernel, out_shape=[jax.ShapeDtypeStruct((2 * half, c...  5.15 us
    pallas_call x1, Pallas kernels, shards(): pl.pallas_call(project_kernel, out_shape=(jax.ShapeDtypeStruct((half, col...  3.26 us
  transfers between devices with their start and end apart: 26, of which 12 were waited for; matrix products, arithmetic and copies ran while one was open for 4% of the time, Pallas kernels for 17%

profile of v3, /device:TPU:32, one launch (start us, length us, event | category | flops | bytes accessed | tf_op | source)
XLA Modules:
  0.0 131.8 jit_solution(13566126663914346041)
XLA Ops:
  8.5 0.9 constant_dynamic-slice_fusion.1
  9.4 19.2 %all_to_all.10 = bf16[8,4,4096]{2,1,0:T(4,128)(2,1)} all-to-all(bf16[8,4,4096]{2,1,0:T(4,128)(2,1)S(1)} %broadcast_in_dim.3), channel_id=1, replica_groups=mesh['dp'=4,'z'=8,'x'=4,'core'=2] {'z'}, dimensions={0} | all-to-all | bytes 524288 | tf_op jit(solution)/shard_map/all_to_all | solution.py:164
  28.6 1.0 reshape.16.refs_0_
  29.6 2.8 %collective-permute-start.4 = (bf16[32,4096]{1,0:T(8,128)(2,1)S(1)}, bf16[32,4096]{1,0:T(8,128)(2,1)S(1)}, u32[]{:S(2)}, u32[]{:S(2)}) collective-permute-start(bf16[32,4096]{1,0:T(8,128)(2,1)S(1)} %reshape.16.refs_0_), channel_id=1, source_target_pairs={{0,6},{2,0},{4,2},{6,4},{1,7},{3,1},{5,3},{7,5},{8,14},{10,8},{12,... | collective-permute-start | bytes 786440 | tf_op jit(solution)/shard_map/ppermute | solution.py:21
  33.3 0.9 collective-permute-start.2
  34.2 1.1 pad_maximum_fusion.refs_0_
  35.2 3.1 %collective-permute-start.8 = (bf16[3,128,512]{2,1,0:T(8,128)(2,1)S(1)}, bf16[3,128,512]{2,1,0:T(8,128)(2,1)S(1)}, u32[]{:S(2)}, u32[]{:S(2)}) collective-permute-start(bf16[3,128,512]{2,1,0:T(8,128)(2,1)S(1)} %pad_maximum_fusion.refs_0_), channel_id=1, source_target_pairs={{0,192},{64,0},{128,64},{192,128},{1,193},{65,1},{129,65},{193,129... | collective-permute-start | bytes 1179656 | tf_op jit(solution)/shard_map/ppermute | solution.py:21
  38.9 3.6 %collective-permute-done.4.refs_3_ = bf16[32,4096]{1,0:T(8,128)(2,1)S(1)} collective-permute-done((bf16[32,4096]{1,0:T(8,128)(2,1)S(1)}, bf16[32,4096]{1,0:T(8,128)(2,1)S(1)}, u32[]{:S(2)}, u32[]{:S(2)}) %collective-permute-start.4) | collective-permute-done | bytes 262176 | tf_op jit(solution)/shard_map/ppermute | solution.py:21
  42.6 1.6 %collective-permute-start.6 = (bf16[3,128,512]{2,1,0:T(8,128)(2,1)S(1)}, bf16[3,128,512]{2,1,0:T(8,128)(2,1)S(1)}, u32[]{:S(2)}, u32[]{:S(2)}) collective-permute-start(bf16[3,128,512]{2,1,0:T(8,128)(2,1)S(1)} %pad_maximum_fusion.refs_0_), channel_id=1, source_target_pairs={{0,64},{64,128},{128,192},{192,0},{1,65},{65,129},{129,193},{193,1... | collective-permute-start | bytes 1179656 | tf_op jit(solution)/shard_map/ppermute | solution.py:21
  44.2 1.7 %collective-permute-done.2.refs_1_ = bf16[32,4096]{1,0:T(8,128)(2,1)S(1)} collective-permute-done((bf16[32,4096]{1,0:T(8,128)(2,1)S(1)}, bf16[32,4096]{1,0:T(8,128)(2,1)S(1)}, u32[]{:S(2)}, u32[]{:S(2)}) %collective-permute-start.2) | collective-permute-done | bytes 262176 | tf_op jit(solution)/shard_map/ppermute | solution.py:21
  45.9 1.4 %copy-done.1 = bf16[3,64,4096]{2,1,0:T(8,128)(2,1)S(1)} copy-done((bf16[3,64,4096]{2,1,0:T(8,128)(2,1)S(1)}, bf16[3,64,4096]{2,1,0:T(8,128)(2,1)}, u32[]{:S(2)}) %copy-start.1) | copy-done | bytes 1572888
  47.3 3.3 %shard_map.92 = (bf16[128,384]{1,0:T(8,128)(2,1)S(1)}, bf16[128,384]{1,0:T(8,128)(2,1)S(1)}) custom-call(bf16[3,64,4096]{2,1,0:T(8,128)(2,1)S(1)} %copy-done, bf16[3,64,4096]{2,1,0:T(8,128)(2,1)S(1)} %copy-done.1, bf16[3,64,4096]{2,1,0:T(8,128)(2,1)S(1)} %collective-permute-done.other_key, bf16[3,64,4096]{2,1,0:T(8,128)(2,1)} %collective-permute-done.1.other_value, ...), custom_call_target="tpu_custom_call" | custom-call | flops 805306368 | bytes 7340032 | tf_op jit(solution)/shard_map/pallas_call | solution.py:174
  50.6 1.3 collective-permute-done.5.other_ref
  51.9 3.6 %collective-permute-done.6.refs_1_ = bf16[3,128,512]{2,1,0:T(8,128)(2,1)S(1)} collective-permute-done((bf16[3,128,512]{2,1,0:T(8,128)(2,1)S(1)}, bf16[3,128,512]{2,1,0:T(8,128)(2,1)S(1)}, u32[]{:S(2)}, u32[]{:S(2)}) %collective-permute-start.6) | collective-permute-done | bytes 393248 | tf_op jit(solution)/shard_map/ppermute | solution.py:21
  55.5 1.9 %shard_map.93.refs_4_ = f32[8,2048]{1,0:T(8,128)S(1)} custom-call(bf16[128,384]{1,0:T(8,128)(2,1)S(1)} %get-tuple-element.37.own_ref, bf16[128,384]{1,0:T(8,128)(2,1)S(1)} %collective-permute-done.5.other_ref, bf16[3,128,512]{2,1,0:T(8,128)(2,1)S(1)} %pad_maximum_fusion.refs_0_, bf16[3,128,512]{2,1,0:T(8,128)(2,1)S(1)} %collective-permute-done.6.refs_1_, ...), custom_call_target="tpu_custom_call" | custom-call | flops 1610612736 | bytes 3145728 | tf_op jit(solution)/shard_map/pallas_call | solution.py:184
  59.6 2.2 %collective-permute-done.11.refs_7_ = f32[8,2048]{1,0:T(8,128)S(1)} collective-permute-done((f32[8,2048]{1,0:T(8,128)S(1)}, f32[8,2048]{1,0:T(8,128)S(1)}, u32[]{:S(2)}, u32[]{:S(2)}) %collective-permute-start.11) | collective-permute-done | bytes 65568 | tf_op jit(solution)/shard_map/ppermute | solution.py:21
  61.8 2.1 %collective-permute-done.10.refs_6_ = f32[8,2048]{1,0:T(8,128)S(1)} collective-permute-done((f32[8,2048]{1,0:T(8,128)S(1)}, f32[8,2048]{1,0:T(8,128)S(1)}, u32[]{:S(2)}, u32[]{:S(2)}) %collective-permute-start.10) | collective-permute-done | bytes 65568 | tf_op jit(solution)/shard_map/ppermute | solution.py:21
  64.6 5.2 %shard_map.94 = (bf16[256,384]{1,0:T(8,128)(2,1)S(1)}, bf16[3,128,512]{2,1,0:T(8,128)(2,1)S(1)}, bf16[3,128,512]{2,1,0:T(8,128)(2,1)S(1)}, bf16[3,128,512]{2,1,0:T(8,128)(2,1)S(1)}, bf16[3,128,512]{2,1,0:T(8,128)(2,1)S(1)}) custom-call(bf16[128,384]{1,0:T(8,128)(2,1)S(1)} %get-tuple-element.37.own_ref, ...), custom_call_target="tpu_custom_call" | custom-call | flops 4831838208 | bytes 6291456 | tf_op jit(solution)/shard_map/pallas_call | solution.py:191
  71.2 2.5 %shard_map.95 = (bf16[32,4096]{1,0:T(8,128)(2,1)S(1)}, bf16[32,4096]{1,0:T(8,128)(2,1)S(1)}, bf16[32,4096]{1,0:T(8,128)(2,1)S(1)}, bf16[32,4096]{1,0:T(8,128)(2,1)S(1)}) custom-call(bf16[256,384]{1,0:T(8,128)(2,1)S(1)} %get-tuple-element.40.own_ref, bf16[128,384]{1,0:T(8,128)(2,1)S(1)} %collective-permute-done.12.other_ref, ...), custom_call_target="tpu_custom_call" | custom-call | flops 805306368 | bytes 7340032 | tf_op jit(solution)/shard_map/pallas_call | solution.py:199
  73.7 2.4 %collective-permute-start.13 = (bf16[32,4096]{1,0:T(8,128)(2,1)S(1)}, bf16[32,4096]{1,0:T(8,128)(2,1)S(1)}, u32[]{:S(2)}, u32[]{:S(2)}) collective-permute-start(bf16[32,4096]{1,0:T(8,128)(2,1)S(1)} %get-tuple-element.42), channel_id=1, source_target_pairs={{0,6},{2,0},{4,2},{6,4},{1,7},{3,1},{5,3},{7,5},{8,14},{10,8},{12,... | collective-permute-start | bytes 786440 | tf_op jit(solution)/shard_map/ppermute | solution.py:21
  76.1 1.9 %collective-permute-start.14 = (bf16[32,4096]{1,0:T(8,128)(2,1)S(1)}, bf16[32,4096]{1,0:T(8,128)(2,1)S(1)}, u32[]{:S(2)}, u32[]{:S(2)}) collective-permute-start(bf16[32,4096]{1,0:T(8,128)(2,1)S(1)} %get-tuple-element.43), channel_id=1, source_target_pairs={{0,4},{2,6},{4,0},{6,2},{1,5},{3,7},{5,1},{7,3},{8,12},{10,14},{12... | collective-permute-start | bytes 786440 | tf_op jit(solution)/shard_map/ppermute | solution.py:21
  78.0 1.5 %collective-permute-start.16 = (bf16[3,128,512]{2,1,0:T(8,128)(2,1)S(1)}, bf16[3,128,512]{2,1,0:T(8,128)(2,1)S(1)}, u32[]{:S(2)}, u32[]{:S(2)}) collective-permute-start(bf16[3,128,512]{2,1,0:T(8,128)(2,1)S(1)} %get-tuple-element.46), channel_id=1, source_target_pairs={{0,192},{64,0},{128,64},{192,128},{1,193},{65,1},{129,65},{193,129... | collective-permute-start | bytes 1179656 | tf_op jit(solution)/shard_map/ppermute | solution.py:21
  80.1 7.6 %collective-permute-done.13 = bf16[32,4096]{1,0:T(8,128)(2,1)S(1)} collective-permute-done((bf16[32,4096]{1,0:T(8,128)(2,1)S(1)}, bf16[32,4096]{1,0:T(8,128)(2,1)S(1)}, u32[]{:S(2)}, u32[]{:S(2)}) %collective-permute-start.13) | collective-permute-done | bytes 262176 | tf_op jit(solution)/shard_map/ppermute | solution.py:21
  87.7 2.3 %collective-permute-start.19 = (bf16[2,256,384]{2,1,0:T(8,128)(2,1)S(1)}, bf16[2,256,384]{2,1,0:T(8,128)(2,1)S(1)}, u32[]{:S(2)}, u32[]{:S(2)}) collective-permute-start(bf16[2,256,384]{2,1,0:T(8,128)(2,1)S(1)} %pad_maximum_fusion.1.refs_0_), channel_id=1, source_target_pairs={{0,128},{64,192},{128,0},{192,64},{1,129},{65,193},{129,1},{193,65... | collective-permute-start | bytes 1179656 | tf_op jit(solution)/shard_map/ppermute | solution.py:206
  90.0 4.7 %collective-permute-done.15 = bf16[32,4096]{1,0:T(8,128)(2,1)S(1)} collective-permute-done((bf16[32,4096]{1,0:T(8,128)(2,1)S(1)}, bf16[32,4096]{1,0:T(8,128)(2,1)S(1)}, u32[]{:S(2)}, u32[]{:S(2)}) %collective-permute-start.15) | collective-permute-done | bytes 262176 | tf_op jit(solution)/shard_map/ppermute | solution.py:21
  95.7 9.2 %all-to-all-start.1 = ((bf16[8,4,4096]{2,1,0:T(4,128)(2,1)}), bf16[8,4,4096]{2,1,0:T(4,128)(2,1)S(1)}, u32[]{:S(2)}, u32[]{:S(2)}) async-start(bf16[8,4,4096]{2,1,0:T(4,128)(2,1)} %reshape.17), calls=%async_computation.1 | async-start | bytes 524288 | tf_op jit(solution)/shard_map/all_to_all | solution.py:234
  105.0 1.2 collective-permute-start.20
  106.1 1.0 shard_map.96.g_ref
  107.2 0.9 copy-done.3
  108.1 8.6 %shard_map.97 = (f32[3,64,4096]{2,1,0:T(8,128)}, f32[3,64,4096]{2,1,0:T(8,128)}) custom-call(bf16[384,1024]{1,0:T(8,128)(2,1)} %copy-done.3, bf16[1024,4096]{1,0:T(8,128)(2,1)} %all-gather.2.cloned.1.call-done.mem_ref), custom_call_target="tpu_custom_call" | custom-call | flops 3221225472 | bytes 14680064 | tf_op jit(solution)/shard_map/pallas_call | solution.py:220
  117.5 2.1 %collective-permute-start.22 = (f32[4,4096]{1,0:T(4,128)S(1)}, f32[4,4096]{1,0:T(4,128)S(1)}, u32[]{:S(2)}, u32[]{:S(2)}) collective-permute-start(f32[4,4096]{1,0:T(4,128)S(1)} %convert_reduce_fusion), channel_id=1, source_target_pairs={{0,128},{64,192},{128,0},{192,64},{1,129},{65,193},{129,1},{193,65... | collective-permute-start | bytes 196616 | tf_op jit(solution)/shard_map/ppermute | solution.py:21
  119.6 2.5 %collective-permute-start.21 = (f32[4,4096]{1,0:T(4,128)S(1)}, f32[4,4096]{1,0:T(4,128)S(1)}, u32[]{:S(2)}, u32[]{:S(2)}) collective-permute-start(f32[4,4096]{1,0:T(4,128)S(1)} %convert_reduce_fusion), channel_id=1, source_target_pairs={{0,192},{64,0},{128,64},{192,128},{1,193},{65,1},{129,65},{193,129... | collective-permute-start | bytes 196616 | tf_op jit(solution)/shard_map/ppermute | solution.py:21
  (54 shorter events, 12.4 us)
Async XLA Ops:
  7.2 38.7 %copy-start = (bf16[3,64,4096]{2,1,0:T(8,128)(2,1)S(1)}, bf16[3,64,4096]{2,1,0:T(8,128)(2,1)}, u32[]{:S(2)}) copy-start(bf16[3,64,4096]{2,1,0:T(8,128)(2,1)} %own_key.3) | copy-start | bytes 4718596
  7.2 100.9 %all-gather.2.cloned.1.call-start = ((), (), s32[]{:S(2)}) async-start(), calls=%async_computation.2 | async-start | bytes 8519680 | tf_op jit(solution)/shard_map/all_gather | solution.py:161
  7.9 21.7 %collective-permute-start = (bf16[3,64,4096]{2,1,0:T(8,128)(2,1)}, bf16[3,64,4096]{2,1,0:T(8,128)(2,1)S(1)}, u32[]{:S(2)}, u32[]{:S(2)}) collective-permute-start(bf16[3,64,4096]{2,1,0:T(8,128)(2,1)} %own_key.3), channel_id=1, source_target_pairs={{0,1},{1,0},{2,3},{3,2},{4,5},{5,4},{6,7},{7,6},{8,9},{9,8},{10,11... | collective-permute-start | bytes 4718600 | tf_op jit(solution)/shard_map/ppermute | solution.py:21
  8.0 21.6 %collective-permute-start.1 = (bf16[3,64,4096]{2,1,0:T(8,128)(2,1)}, bf16[3,64,4096]{2,1,0:T(8,128)(2,1)}, u32[]{:S(2)}, u32[]{:S(2)}) collective-permute-start(bf16[3,64,4096]{2,1,0:T(8,128)(2,1)} %own_value.3), channel_id=1, source_target_pairs={{0,1},{1,0},{2,3},{3,2},{4,5},{5,4},{6,7},{7,6},{8,9},{9,8},{10,11... | collective-permute-start | bytes 4718600 | tf_op jit(solution)/shard_map/ppermute | solution.py:21
  29.6 12.9 %collective-permute-start.4 = (bf16[32,4096]{1,0:T(8,128)(2,1)S(1)}, bf16[32,4096]{1,0:T(8,128)(2,1)S(1)}, u32[]{:S(2)}, u32[]{:S(2)}) collective-permute-start(bf16[32,4096]{1,0:T(8,128)(2,1)S(1)} %reshape.16.refs_0_), channel_id=1, source_target_pairs={{0,6},{2,0},{4,2},{6,4},{1,7},{3,1},{5,3},{7,5},{8,14},{10,8},{12,... | collective-permute-start | bytes 786440 | tf_op jit(solution)/shard_map/ppermute | solution.py:21
  32.5 11.7 %collective-permute-start.3 = (bf16[32,4096]{1,0:T(8,128)(2,1)S(1)}, bf16[32,4096]{1,0:T(8,128)(2,1)S(1)}, u32[]{:S(2)}, u32[]{:S(2)}) collective-permute-start(bf16[32,4096]{1,0:T(8,128)(2,1)S(1)} %reshape.16.refs_0_), channel_id=1, source_target_pairs={{0,4},{2,6},{4,0},{6,2},{1,5},{3,7},{5,1},{7,3},{8,12},{10,14},{12... | collective-permute-start | bytes 786440 | tf_op jit(solution)/shard_map/ppermute | solution.py:21
  33.3 12.6 %collective-permute-start.2 = (bf16[32,4096]{1,0:T(8,128)(2,1)S(1)}, bf16[32,4096]{1,0:T(8,128)(2,1)S(1)}, u32[]{:S(2)}, u32[]{:S(2)}) collective-permute-start(bf16[32,4096]{1,0:T(8,128)(2,1)S(1)} %reshape.16.refs_0_), channel_id=1, source_target_pairs={{0,2},{2,4},{4,6},{6,0},{1,3},{3,5},{5,7},{7,1},{8,10},{10,12},{12... | collective-permute-start | bytes 786440 | tf_op jit(solution)/shard_map/ppermute | solution.py:21
  35.2 16.7 %collective-permute-start.8 = (bf16[3,128,512]{2,1,0:T(8,128)(2,1)S(1)}, bf16[3,128,512]{2,1,0:T(8,128)(2,1)S(1)}, u32[]{:S(2)}, u32[]{:S(2)}) collective-permute-start(bf16[3,128,512]{2,1,0:T(8,128)(2,1)S(1)} %pad_maximum_fusion.refs_0_), channel_id=1, source_target_pairs={{0,192},{64,0},{128,64},{192,128},{1,193},{65,1},{129,65},{193,129... | collective-permute-start | bytes 1179656 | tf_op jit(solution)/shard_map/ppermute | solution.py:21
  38.3 13.6 %collective-permute-start.7 = (bf16[3,128,512]{2,1,0:T(8,128)(2,1)S(1)}, bf16[3,128,512]{2,1,0:T(8,128)(2,1)S(1)}, u32[]{:S(2)}, u32[]{:S(2)}) collective-permute-start(bf16[3,128,512]{2,1,0:T(8,128)(2,1)S(1)} %pad_maximum_fusion.refs_0_), channel_id=1, source_target_pairs={{0,128},{64,192},{128,0},{192,64},{1,129},{65,193},{129,1},{193,65... | collective-permute-start | bytes 1179656 | tf_op jit(solution)/shard_map/ppermute | solution.py:21
  42.6 12.9 %collective-permute-start.6 = (bf16[3,128,512]{2,1,0:T(8,128)(2,1)S(1)}, bf16[3,128,512]{2,1,0:T(8,128)(2,1)S(1)}, u32[]{:S(2)}, u32[]{:S(2)}) collective-permute-start(bf16[3,128,512]{2,1,0:T(8,128)(2,1)S(1)} %pad_maximum_fusion.refs_0_), channel_id=1, source_target_pairs={{0,64},{64,128},{128,192},{192,0},{1,65},{65,129},{129,193},{193,1... | collective-permute-start | bytes 1179656 | tf_op jit(solution)/shard_map/ppermute | solution.py:21
  45.9 1.4 %copy-start.1 = (bf16[3,64,4096]{2,1,0:T(8,128)(2,1)S(1)}, bf16[3,64,4096]{2,1,0:T(8,128)(2,1)}, u32[]{:S(2)}) copy-start(bf16[3,64,4096]{2,1,0:T(8,128)(2,1)} %own_value.3) | copy-start | bytes 4718596
  50.5 1.4 %collective-permute-start.5 = (bf16[128,384]{1,0:T(8,128)(2,1)S(1)}, bf16[128,384]{1,0:T(8,128)(2,1)S(1)}, u32[]{:S(2)}, u32[]{:S(2)}) collective-permute-start(bf16[128,384]{1,0:T(8,128)(2,1)S(1)} %get-tuple-element.38), channel_id=1, source_target_pairs={{0,1},{1,0},{2,3},{3,2},{4,5},{5,4},{6,7},{7,6},{8,9},{9,8},{10,11... | collective-permute-start | bytes 294920 | tf_op jit(solution)/shard_map/ppermute | solution.py:21
  57.4 13.8 %copy-start.2 = (bf16[3,64,4096]{2,1,0:T(8,128)(2,1)S(1)}, bf16[3,64,4096]{2,1,0:T(8,128)(2,1)}, u32[]{:S(2)}) copy-start(bf16[3,64,4096]{2,1,0:T(8,128)(2,1)} %own_value.3) | copy-start | bytes 4718596
  57.5 4.3 %collective-permute-start.11 = (f32[8,2048]{1,0:T(8,128)S(1)}, f32[8,2048]{1,0:T(8,128)S(1)}, u32[]{:S(2)}, u32[]{:S(2)}) collective-permute-start(f32[8,2048]{1,0:T(8,128)S(1)} %shard_map.93.refs_4_), channel_id=1, source_target_pairs={{0,192},{64,0},{128,64},{192,128},{1,193},{65,1},{129,65},{193,129... | collective-permute-start | bytes 196616 | tf_op jit(solution)/shard_map/ppermute | solution.py:21
  58.1 5.8 %collective-permute-start.10 = (f32[8,2048]{1,0:T(8,128)S(1)}, f32[8,2048]{1,0:T(8,128)S(1)}, u32[]{:S(2)}, u32[]{:S(2)}) collective-permute-start(f32[8,2048]{1,0:T(8,128)S(1)} %shard_map.93.refs_4_), channel_id=1, source_target_pairs={{0,128},{64,192},{128,0},{192,64},{1,129},{65,193},{129,1},{193,65... | collective-permute-start | bytes 196616 | tf_op jit(solution)/shard_map/ppermute | solution.py:21
  58.8 5.9 %collective-permute-start.9 = (f32[8,2048]{1,0:T(8,128)S(1)}, f32[8,2048]{1,0:T(8,128)S(1)}, u32[]{:S(2)}, u32[]{:S(2)}) collective-permute-start(f32[8,2048]{1,0:T(8,128)S(1)} %shard_map.93.refs_4_), channel_id=1, source_target_pairs={{0,64},{64,128},{128,192},{192,0},{1,65},{65,129},{129,193},{193,1... | collective-permute-start | bytes 196616 | tf_op jit(solution)/shard_map/ppermute | solution.py:21
  69.8 3.9 %copy-start.4 = (bf16[3,128,512]{2,1,0:T(8,128)(2,1)}, bf16[3,128,512]{2,1,0:T(8,128)(2,1)S(1)}, u32[]{:S(2)}) copy-start(bf16[3,128,512]{2,1,0:T(8,128)(2,1)S(1)} %get-tuple-element.55) | copy-start | bytes 1179652
  69.8 1.4 %collective-permute-start.12 = (bf16[128,384]{1,0:T(8,128)(2,1)S(1)}, bf16[128,384]{1,0:T(8,128)(2,1)S(1)}, u32[]{:S(2)}, u32[]{:S(2)}) collective-permute-start(bf16[128,384]{1,0:T(8,128)(2,1)S(1)} %slice.9), channel_id=1, source_target_pairs={{0,1},{1,0},{2,3},{3,2},{4,5},{5,4},{6,7},{7,6},{8,9},{9,8},{10,11... | collective-permute-start | bytes 294920 | tf_op jit(solution)/shard_map/ppermute | solution.py:21
  69.9 9.6 %collective-permute-start.18 = (bf16[256,384]{1,0:T(8,128)(2,1)S(1)}, bf16[256,384]{1,0:T(8,128)(2,1)S(1)}, u32[]{:S(2)}, u32[]{:S(2)}) collective-permute-start(bf16[256,384]{1,0:T(8,128)(2,1)S(1)} %get-tuple-element.40.own_ref), channel_id=1, source_target_pairs={{0,64},{64,0},{128,192},{192,128},{1,65},{65,1},{129,193},{193,129... | collective-permute-start | bytes 589832 | tf_op jit(solution)/shard_map/ppermute | solution.py:205
  73.7 14.0 %collective-permute-start.13 = (bf16[32,4096]{1,0:T(8,128)(2,1)S(1)}, bf16[32,4096]{1,0:T(8,128)(2,1)S(1)}, u32[]{:S(2)}, u32[]{:S(2)}) collective-permute-start(bf16[32,4096]{1,0:T(8,128)(2,1)S(1)} %get-tuple-element.42), channel_id=1, source_target_pairs={{0,6},{2,0},{4,2},{6,4},{1,7},{3,1},{5,3},{7,5},{8,14},{10,8},{12,... | collective-permute-start | bytes 786440 | tf_op jit(solution)/shard_map/ppermute | solution.py:21
  76.1 13.9 %collective-permute-start.14 = (bf16[32,4096]{1,0:T(8,128)(2,1)S(1)}, bf16[32,4096]{1,0:T(8,128)(2,1)S(1)}, u32[]{:S(2)}, u32[]{:S(2)}) collective-permute-start(bf16[32,4096]{1,0:T(8,128)(2,1)S(1)} %get-tuple-element.43), channel_id=1, source_target_pairs={{0,4},{2,6},{4,0},{6,2},{1,5},{3,7},{5,1},{7,3},{8,12},{10,14},{12... | collective-permute-start | bytes 786440 | tf_op jit(solution)/shard_map/ppermute | solution.py:21
  78.0 16.7 %collective-permute-start.15 = (bf16[32,4096]{1,0:T(8,128)(2,1)S(1)}, bf16[32,4096]{1,0:T(8,128)(2,1)S(1)}, u32[]{:S(2)}, u32[]{:S(2)}) collective-permute-start(bf16[32,4096]{1,0:T(8,128)(2,1)S(1)} %get-tuple-element.44), channel_id=1, source_target_pairs={{0,2},{2,4},{4,6},{6,0},{1,3},{3,5},{5,7},{7,1},{8,10},{10,12},{12... | collective-permute-start | bytes 786440 | tf_op jit(solution)/shard_map/ppermute | solution.py:21
  78.0 16.9 %collective-permute-start.16 = (bf16[3,128,512]{2,1,0:T(8,128)(2,1)S(1)}, bf16[3,128,512]{2,1,0:T(8,128)(2,1)S(1)}, u32[]{:S(2)}, u32[]{:S(2)}) collective-permute-start(bf16[3,128,512]{2,1,0:T(8,128)(2,1)S(1)} %get-tuple-element.46), channel_id=1, source_target_pairs={{0,192},{64,0},{128,64},{192,128},{1,193},{65,1},{129,65},{193,129... | collective-permute-start | bytes 1179656 | tf_op jit(solution)/shard_map/ppermute | solution.py:21
  79.5 15.4 %collective-permute-start.17 = (bf16[3,128,512]{2,1,0:T(8,128)(2,1)S(1)}, bf16[3,128,512]{2,1,0:T(8,128)(2,1)S(1)}, u32[]{:S(2)}, u32[]{:S(2)}) collective-permute-start(bf16[3,128,512]{2,1,0:T(8,128)(2,1)S(1)} %get-tuple-element.48), channel_id=1, source_target_pairs={{0,64},{64,128},{128,192},{192,0},{1,65},{65,129},{129,193},{193,1... | collective-permute-start | bytes 1179656 | tf_op jit(solution)/shard_map/ppermute | solution.py:21
  80.0 24.9 %copy-start.5 = (bf16[3,128,512]{2,1,0:T(8,128)(2,1)S(1)}, bf16[3,128,512]{2,1,0:T(8,128)(2,1)}, u32[]{:S(2)}) copy-start(bf16[3,128,512]{2,1,0:T(8,128)(2,1)} %copy-done.4) | copy-start | bytes 1179652
  87.7 18.4 %collective-permute-start.19 = (bf16[2,256,384]{2,1,0:T(8,128)(2,1)S(1)}, bf16[2,256,384]{2,1,0:T(8,128)(2,1)S(1)}, u32[]{:S(2)}, u32[]{:S(2)}) collective-permute-start(bf16[2,256,384]{2,1,0:T(8,128)(2,1)S(1)} %pad_maximum_fusion.1.refs_0_), channel_id=1, source_target_pairs={{0,128},{64,192},{128,0},{192,64},{1,129},{65,193},{129,1},{193,65... | collective-permute-start | bytes 1179656 | tf_op jit(solution)/shard_map/ppermute | solution.py:206
  95.7 21.0 %all-to-all-start.1 = ((bf16[8,4,4096]{2,1,0:T(4,128)(2,1)}), bf16[8,4,4096]{2,1,0:T(4,128)(2,1)S(1)}, u32[]{:S(2)}, u32[]{:S(2)}) async-start(bf16[8,4,4096]{2,1,0:T(4,128)(2,1)} %reshape.17), calls=%async_computation.1 | async-start | bytes 524288 | tf_op jit(solution)/shard_map/all_to_all | solution.py:234
  105.0 17.2 %collective-permute-start.20 = (bf16[3,128,512]{2,1,0:T(8,128)(2,1)S(1)}, bf16[3,128,512]{2,1,0:T(8,128)(2,1)S(1)}, u32[]{:S(2)}, u32[]{:S(2)}) collective-permute-start(bf16[3,128,512]{2,1,0:T(8,128)(2,1)S(1)} %copy-done.5), channel_id=1, source_target_pairs={{0,128},{64,192},{128,0},{192,64},{1,129},{65,193},{129,1},{193,65... | collective-permute-start | bytes 1179656 | tf_op jit(solution)/shard_map/ppermute | solution.py:21
  107.2 0.9 copy-start.3
  116.8 6.3 %collective-permute-start.23 = (f32[4,4096]{1,0:T(4,128)S(1)}, f32[4,4096]{1,0:T(4,128)S(1)}, u32[]{:S(2)}, u32[]{:S(2)}) collective-permute-start(f32[4,4096]{1,0:T(4,128)S(1)} %convert_reduce_fusion), channel_id=1, source_target_pairs={{0,64},{64,128},{128,192},{192,0},{1,65},{65,129},{129,193},{193,1... | collective-permute-start | bytes 196616 | tf_op jit(solution)/shard_map/ppermute | solution.py:21
  117.5 5.8 %collective-permute-start.22 = (f32[4,4096]{1,0:T(4,128)S(1)}, f32[4,4096]{1,0:T(4,128)S(1)}, u32[]{:S(2)}, u32[]{:S(2)}) collective-permute-start(f32[4,4096]{1,0:T(4,128)S(1)} %convert_reduce_fusion), channel_id=1, source_target_pairs={{0,128},{64,192},{128,0},{192,64},{1,129},{65,193},{129,1},{193,65... | collective-permute-start | bytes 196616 | tf_op jit(solution)/shard_map/ppermute | solution.py:21
  119.6 4.4 %collective-permute-start.21 = (f32[4,4096]{1,0:T(4,128)S(1)}, f32[4,4096]{1,0:T(4,128)S(1)}, u32[]{:S(2)}, u32[]{:S(2)}) collective-permute-start(f32[4,4096]{1,0:T(4,128)S(1)} %convert_reduce_fusion), channel_id=1, source_target_pairs={{0,192},{64,0},{128,64},{192,128},{1,193},{65,1},{129,65},{193,129... | collective-permute-start | bytes 196616 | tf_op jit(solution)/shard_map/ppermute | solution.py:21
Sparse Core Ops, SparseCore 0:
  10.8 91.5 all-gather.1

commit v4 on v3

--- a/solution.py
+++ b/solution.py
@@ -114,28 +114,29 @@
         g_ref[:, layer * width : (layer + 1) * width] = jnp.where(left, acc[:tokens], acc[tokens:]).astype(BF16)
 
 
-def order_kernel(at_ref, *refs):
-    *g_refs, out_ref, stack, order = refs
+def weights_kernel(at_ref, *refs):
+    *g_refs, mem_ref, key_ref, value_ref, stack, order, flipped = refs
     ndp, nx, nz, few = 2 * len(g_refs), 4, 8, 4
-    for pair, g_ref in enumerate(g_refs):
-        for part in range(2):
-            stack[2 * pair + part] = g_ref[part].astype(F32)
-    parts = [lax.bitwise_xor(at_ref[0], dp) for dp in range(ndp)]
-    for half in range(2):
-        core = at_ref[2] if half == 0 else 1 - at_ref[2]
-        for back in range(nx):
-            x = lax.rem(at_ref[1] + nx - back, nx)
-            first = (half * nx + back) * nz * few
-            blocks = [stack[part, first : first + nz * few] for part in parts]
-            for z in range(nz):
-                to = pl.multiple_of(((z * nx + x) * 2 + core) * ndp * few, ndp * few)
-                order[pl.ds(to, ndp * few)] = jnp.concatenate([b[z * few : (z + 1) * few] for b in blocks], axis=0)
-    out_ref[...] = order[...].T.astype(BF16)
-
-
-def weights_kernel(g_ref, mem_ref, key_ref, value_ref):
     layers, width, _ = key_ref.shape
-    out = mm(g_ref[...], mem_ref[...])
+
+    @pl.when(pl.program_id(0) == 0)
+    def _():
+        for pair, g_ref in enumerate(g_refs):
+            for part in range(2):
+                stack[2 * pair + part] = g_ref[part].astype(F32)
+        parts = [lax.bitwise_xor(at_ref[0], dp) for dp in range(ndp)]
+        for half in range(2):
+            core = at_ref[2] if half == 0 else 1 - at_ref[2]
+            for back in range(nx):
+                x = lax.rem(at_ref[1] + nx - back, nx)
+                first = (half * nx + back) * nz * few
+                blocks = [stack[part, first : first + nz * few] for part in parts]
+                for z in range(nz):
+                    to = pl.multiple_of(((z * nx + x) * 2 + core) * ndp * few, ndp * few)
+                    order[pl.ds(to, ndp * few)] = jnp.concatenate([b[z * few : (z + 1) * few] for b in blocks], axis=0)
+        flipped[...] = order[...].T.astype(BF16)
+
+    out = mm(flipped[...], mem_ref[...])
     for layer in range(layers):
         at = 2 * layer * width
         key_ref[layer] = out[at : at + width]
@@ -163,7 +164,7 @@
     quarter = lax.dynamic_slice(memory, (here * few, 0), (few, d))
     along_z = lax.all_to_all(jnp.broadcast_to(quarter, (nz, few, d)), "z", 0, 0).reshape(nz * few, d)
     key_other, value_other = shift(w_key, "core", 1), shift(w_value, "core", 1)
-    along_z, key_other, value_other = lax.optimization_barrier((along_z, key_other, value_other))
+    along_z, key_other, value_other, at = lax.optimization_barrier((along_z, key_other, value_other, at))
     qdo = jnp.concatenate([queries.swapaxes(1, 2), grad_out.swapaxes(1, 2)], axis=1)
     qdo = after(qdo, along_z)
     qdo = [qdo] + [shift(qdo, "dp", s) for s in range(1, dp)]
@@ -206,37 +207,34 @@
     g_all = (g_all, lax.ppermute(g_all, "dp", [(a, a ^ 2) for a in range(dp)]))
     part = sum([part[0].astype(F32)] + [shift(part[s], "x", -s).astype(F32) for s in range(1, nx)]).astype(BF16)
 
-    flipped = pl.pallas_call(
-        order_kernel,
-        in_specs=[pl.BlockSpec(memory_space=pltpu.SMEM)] + [pl.BlockSpec(memory_space=pltpu.VMEM)] * 2,
-        out_shape=jax.ShapeDtypeStruct((cols, full.shape[0]), BF16),
-        scratch_shapes=[pltpu.VMEM((dp,) + g.shape, F32), pltpu.VMEM((full.shape[0], cols), F32)],
-        compiler_params=params,
-        cost_estimate=cost(0, 8 * cols * full.shape[0]),
-    )(at, *g_all)
     block = 1024
     gw_shape = jax.ShapeDtypeStruct((layers, width, d), F32)
-    gw_spec = pl.BlockSpec((layers, width, block), lambda n: (0, 0, n))
+    gw_spec = pl.BlockSpec((layers, width, block), lambda n, at: (0, 0, n))
     grad_w = pl.pallas_call(
         weights_kernel,
-        grid=(d // block,),
-        in_specs=[pl.BlockSpec(flipped.shape, lambda n: (0, 0)), pl.BlockSpec((full.shape[0], block), lambda n: (0, n))],
-        out_specs=(gw_spec, gw_spec),
+        grid_spec=pltpu.PrefetchScalarGridSpec(
+            num_scalar_prefetch=1,
+            grid=(d // block,),
+            in_specs=[pl.BlockSpec((2,) + g.shape, lambda n, at: (0, 0, 0))] * 2 + [pl.BlockSpec((full.shape[0], block), lambda n, at: (0, n))],
+            out_specs=(gw_spec, gw_spec),
+            scratch_shapes=[pltpu.VMEM((dp,) + g.shape, F32), pltpu.VMEM((full.shape[0], cols), F32), pltpu.VMEM((cols, full.shape[0]), BF16)],
+        ),
         out_shape=(gw_shape, gw_shape),
         compiler_params=pltpu.CompilerParams(vmem_limit_bytes=56 * 1024 * 1024),
         cost_estimate=cost(2 * cols * full.size, 2 * full.size + 4 * cols * d),
-    )(flipped, full)
-
-    qa[1], qa[3] = shift(qa[1], "dp", -1), shift(qa[3], "dp", -3)
-    part, *qa = lax.optimization_barrier((part, *qa))
-    qa[2] = shift(qa[2], "dp", -2)
+    )(at, *g_all, full)
+
+    qa[1] = shift(qa[1], "dp", -1)
+    part, qa[2], qa[3] = lax.optimization_barrier((part, qa[2], qa[3]))
+    qa[1], qa[2], qa[3] = lax.optimization_barrier((qa[1], qa[2], qa[3]))
+    qa[2], qa[3] = shift(qa[2], "dp", -2), shift(qa[3], "dp", -3)
 
     part = lax.all_to_all(part.reshape(nz, few, d), "z", 0, 0)
     part, grad_w_key, grad_w_value = lax.optimization_barrier((part, *grad_w))
-    part = jnp.sum(part.astype(F32), axis=0)
+    part = jnp.sum(part.astype(F32), axis=0).astype(BF16)
     parts = [part] + [shift(part, "dp", s) for s in range(1, dp)]
     parts = jnp.concatenate([parts[-1 - j % dp] for j in range(2 * dp - 1)], axis=0)
-    grad_memory = lax.dynamic_slice(parts, ((dp - 1 - here) * few, 0), (mine, d))
+    grad_memory = lax.dynamic_slice(parts, ((dp - 1 - here) * few, 0), (mine, d)).astype(F32)
     part, *qa = lax.optimization_barrier((part, *qa))
     qa = sum(a.astype(F32) for a in qa).astype(BF16)
     grad_queries, attended = qa[:, :width].swapaxes(1, 2), qa[:, width:].swapaxes(1, 2)

time: 134 us -> 134 us (level)
  blocking collectives: 19.2 us -> 0 us
  waiting for transfers between devices: 29.7 us -> 41.7 us
  starting transfers between devices: 37.8 us -> 44.8 us
    all_to_all x1 -> x0, blocking collectives: 19.2 us -> none  [shards(): lax.all_to_all(jnp.broadcast_to(quarter, (nz, few, d)), 'z', 0, 0)]
    all_to_all x0 -> x1, waiting for transfers between devices: none -> 10.2 us  [shards(): lax.all_to_all(jnp.broadcast_to(quarter, (nz, few, d)), 'z', 0, 0)]
    all_to_all x0 -> x1, starting transfers between devices: none -> 8.57 us  [shards(): lax.all_to_all(jnp.broadcast_to(quarter, (nz, few, d)), 'z', 0, 0)]
    all_to_all x1, starting transfers between devices: 9.2 us -> 7.1 us  [shards(): part = lax.all_to_all(part.reshape(nz, few, d), 'z', 0, 0)]
    ppermute x22, waiting for transfers between devices: 29 us -> 30.8 us  [shift(): return lax.ppermute(x, axis, [(a, (a + by) % n) for a in range(n)])]
    ppermute x22, starting transfers between devices: 25.5 us -> 27 us  [shift(): return lax.ppermute(x, axis, [(a, (a + by) % n) for a in range(n)])]
    pallas_call x2 -> x1, Pallas kernels: 9.59 us -> 9.69 us  [shards(): pl.pallas_call(weights_kernel, grid_spec=pltpu.PrefetchScalarGridSpec(num...]
  transfers between devices with their start and end apart: 26 -> 27, of which waited for: 12 -> 13; matrix products, arithmetic and copies ran while one was open for 4% -> 5% of each run, Pallas kernels for 17% -> 17%
where the time goes in v4:
time: 134 us; the launch traced here: 133 us
  starting transfers between devices  44.8 us (33%)
  waiting for transfers between devices  41.7 us (31%)
  Pallas kernels  22.7 us (17%)
  between operations  14.2 us (11%)
  local copies, waits for them, and re-layouts  6.57 us (5%)
  other arithmetic  2.91 us (2%)
    ppermute x22, waiting for transfers between devices, shift(): return lax.ppermute(x, axis, [(a, (a + by) % n) for a in range(n)])  30.8 us
    ppermute x22, starting transfers between devices, shift(): return lax.ppermute(x, axis, [(a, (a + by) % n) for a in range(n)])  27 us
    all_to_all x1, waiting for transfers between devices, shards(): lax.all_to_all(jnp.broadcast_to(quarter, (nz, few, d)), 'z', 0, 0)  10.2 us
    pallas_call x1, Pallas kernels, shards(): pl.pallas_call(weights_kernel, grid_spec=pltpu.PrefetchScalarGridSpec(num...  9.69 us
    all_to_all x1, starting transfers between devices, shards(): lax.all_to_all(jnp.broadcast_to(quarter, (nz, few, d)), 'z', 0, 0)  8.57 us
    all_to_all x1, starting transfers between devices, shards(): part = lax.all_to_all(part.reshape(nz, few, d), 'z', 0, 0)  7.1 us
    pallas_call x1, Pallas kernels, shards(): pl.pallas_call(grads_kernel, out_shape=[jax.ShapeDtypeStruct((2 * half, c...  5.27 us
    pallas_call x1, Pallas kernels, shards(): pl.pallas_call(project_kernel, out_shape=(jax.ShapeDtypeStruct((half, col...  3.27 us
  transfers between devices with their start and end apart: 27, of which 13 were waited for; matrix products, arithmetic and copies ran while one was open for 5% of the time, Pallas kernels for 17%

profile of v4, /device:TPU:32, one launch (start us, length us, event | category | flops | bytes accessed | tf_op | source)
XLA Modules:
  0.0 132.8 jit_solution(15123577602535008188)
XLA Ops:
  8.5 0.9 constant_dynamic-slice_fusion
  10.1 8.6 %all-to-all-start = ((bf16[8,4,4096]{2,1,0:T(4,128)(2,1)}), bf16[8,4,4096]{2,1,0:T(4,128)(2,1)}, u32[]{:S(2)}, u32[]{:S(2)}) async-start(bf16[8,4,4096]{2,1,0:T(4,128)(2,1)} %broadcast_in_dim.3), calls=%async_computation | async-start | bytes 524288 | tf_op jit(solution)/shard_map/all_to_all | solution.py:165
  19.3 10.2 %all-to-all-done = bf16[8,4,4096]{2,1,0:T(4,128)(2,1)} async-done(((bf16[8,4,4096]{2,1,0:T(4,128)(2,1)}), bf16[8,4,4096]{2,1,0:T(4,128)(2,1)}, u32[]{:S(2)}, u32[]{:S(2)}) %all-to-all-start) | async-done | bytes 262176 | tf_op jit(solution)/shard_map/all_to_all | solution.py:165
  29.5 1.0 reshape.16.refs_0_
  30.6 2.9 %collective-permute-start.4 = (bf16[32,4096]{1,0:T(8,128)(2,1)S(1)}, bf16[32,4096]{1,0:T(8,128)(2,1)S(1)}, u32[]{:S(2)}, u32[]{:S(2)}) collective-permute-start(bf16[32,4096]{1,0:T(8,128)(2,1)S(1)} %reshape.16.refs_0_), channel_id=1, source_target_pairs={{0,6},{2,0},{4,2},{6,4},{1,7},{3,1},{5,3},{7,5},{8,14},{10,8},{12,... | collective-permute-start | bytes 786440 | tf_op jit(solution)/shard_map/ppermute | solution.py:21
  34.2 0.9 collective-permute-start.2
  35.1 1.0 pad_maximum_fusion.refs_0_
  36.1 3.1 %collective-permute-start.8 = (bf16[3,128,512]{2,1,0:T(8,128)(2,1)S(1)}, bf16[3,128,512]{2,1,0:T(8,128)(2,1)S(1)}, u32[]{:S(2)}, u32[]{:S(2)}) collective-permute-start(bf16[3,128,512]{2,1,0:T(8,128)(2,1)S(1)} %pad_maximum_fusion.refs_0_), channel_id=1, source_target_pairs={{0,192},{64,0},{128,64},{192,128},{1,193},{65,1},{129,65},{193,129... | collective-permute-start | bytes 1179656 | tf_op jit(solution)/shard_map/ppermute | solution.py:21
  39.9 3.4 %collective-permute-done.4.refs_3_ = bf16[32,4096]{1,0:T(8,128)(2,1)S(1)} collective-permute-done((bf16[32,4096]{1,0:T(8,128)(2,1)S(1)}, bf16[32,4096]{1,0:T(8,128)(2,1)S(1)}, u32[]{:S(2)}, u32[]{:S(2)}) %collective-permute-start.4) | collective-permute-done | bytes 262176 | tf_op jit(solution)/shard_map/ppermute | solution.py:21
  43.3 1.6 %collective-permute-start.6 = (bf16[3,128,512]{2,1,0:T(8,128)(2,1)S(1)}, bf16[3,128,512]{2,1,0:T(8,128)(2,1)S(1)}, u32[]{:S(2)}, u32[]{:S(2)}) collective-permute-start(bf16[3,128,512]{2,1,0:T(8,128)(2,1)S(1)} %pad_maximum_fusion.refs_0_), channel_id=1, source_target_pairs={{0,64},{64,128},{128,192},{192,0},{1,65},{65,129},{129,193},{193,1... | collective-permute-start | bytes 1179656 | tf_op jit(solution)/shard_map/ppermute | solution.py:21
  44.8 1.7 %collective-permute-done.2.refs_1_ = bf16[32,4096]{1,0:T(8,128)(2,1)S(1)} collective-permute-done((bf16[32,4096]{1,0:T(8,128)(2,1)S(1)}, bf16[32,4096]{1,0:T(8,128)(2,1)S(1)}, u32[]{:S(2)}, u32[]{:S(2)}) %collective-permute-start.2) | collective-permute-done | bytes 262176 | tf_op jit(solution)/shard_map/ppermute | solution.py:21
  46.6 1.4 %copy-done.1 = bf16[3,64,4096]{2,1,0:T(8,128)(2,1)S(1)} copy-done((bf16[3,64,4096]{2,1,0:T(8,128)(2,1)S(1)}, bf16[3,64,4096]{2,1,0:T(8,128)(2,1)}, u32[]{:S(2)}) %copy-start.1) | copy-done | bytes 1572888
  48.0 3.3 %shard_map.92 = (bf16[128,384]{1,0:T(8,128)(2,1)S(1)}, bf16[128,384]{1,0:T(8,128)(2,1)S(1)}) custom-call(bf16[3,64,4096]{2,1,0:T(8,128)(2,1)S(1)} %copy-done, bf16[3,64,4096]{2,1,0:T(8,128)(2,1)S(1)} %copy-done.1, bf16[3,64,4096]{2,1,0:T(8,128)(2,1)S(1)} %collective-permute-done.other_key, bf16[3,64,4096]{2,1,0:T(8,128)(2,1)} %collective-permute-done.1.other_value, ...), custom_call_target="tpu_custom_call" | custom-call | flops 805306368 | bytes 7340032 | tf_op jit(solution)/shard_map/pallas_call | solution.py:175
  51.4 1.3 collective-permute-done.5.other_ref
  52.7 3.7 %collective-permute-done.6.refs_1_ = bf16[3,128,512]{2,1,0:T(8,128)(2,1)S(1)} collective-permute-done((bf16[3,128,512]{2,1,0:T(8,128)(2,1)S(1)}, bf16[3,128,512]{2,1,0:T(8,128)(2,1)S(1)}, u32[]{:S(2)}, u32[]{:S(2)}) %collective-permute-start.6) | collective-permute-done | bytes 393248 | tf_op jit(solution)/shard_map/ppermute | solution.py:21
  56.4 1.9 %shard_map.93.refs_4_ = f32[8,2048]{1,0:T(8,128)S(1)} custom-call(bf16[128,384]{1,0:T(8,128)(2,1)S(1)} %get-tuple-element.39.own_ref, bf16[128,384]{1,0:T(8,128)(2,1)S(1)} %collective-permute-done.5.other_ref, bf16[3,128,512]{2,1,0:T(8,128)(2,1)S(1)} %pad_maximum_fusion.refs_0_, bf16[3,128,512]{2,1,0:T(8,128)(2,1)S(1)} %collective-permute-done.6.refs_1_, ...), custom_call_target="tpu_custom_call" | custom-call | flops 1610612736 | bytes 3145728 | tf_op jit(solution)/shard_map/pallas_call | solution.py:185
  59.7 0.8 collective-permute-start.9
  60.5 2.2 %collective-permute-done.11.refs_7_ = f32[8,2048]{1,0:T(8,128)S(1)} collective-permute-done((f32[8,2048]{1,0:T(8,128)S(1)}, f32[8,2048]{1,0:T(8,128)S(1)}, u32[]{:S(2)}, u32[]{:S(2)}) %collective-permute-start.11) | collective-permute-done | bytes 65568 | tf_op jit(solution)/shard_map/ppermute | solution.py:21
  62.7 2.1 %collective-permute-done.10.refs_6_ = f32[8,2048]{1,0:T(8,128)S(1)} collective-permute-done((f32[8,2048]{1,0:T(8,128)S(1)}, f32[8,2048]{1,0:T(8,128)S(1)}, u32[]{:S(2)}, u32[]{:S(2)}) %collective-permute-start.10) | collective-permute-done | bytes 65568 | tf_op jit(solution)/shard_map/ppermute | solution.py:21
  65.5 5.3 %shard_map.94 = (bf16[256,384]{1,0:T(8,128)(2,1)S(1)}, bf16[3,128,512]{2,1,0:T(8,128)(2,1)S(1)}, bf16[3,128,512]{2,1,0:T(8,128)(2,1)}, bf16[3,128,512]{2,1,0:T(8,128)(2,1)S(1)}, bf16[3,128,512]{2,1,0:T(8,128)(2,1)S(1)}) custom-call(bf16[128,384]{1,0:T(8,128)(2,1)S(1)} %get-tuple-element.39.own_ref, bf16[128,384]{1,0:T(8,128)(2,1)S(1)} %collective-permute-done.5.other_ref, ...), custom_call_target="tpu_custom_call" | custom-call | flops 4831838208 | bytes 6291456 | tf_op jit(solution)/shard_map/pallas_call | solution.py:192
  72.2 2.5 %shard_map.95 = (bf16[32,4096]{1,0:T(8,128)(2,1)S(1)}, bf16[32,4096]{1,0:T(8,128)(2,1)S(1)}, bf16[32,4096]{1,0:T(8,128)(2,1)S(1)}, bf16[32,4096]{1,0:T(8,128)(2,1)S(1)}) custom-call(bf16[256,384]{1,0:T(8,128)(2,1)S(1)} %get-tuple-element.42.own_ref, bf16[128,384]{1,0:T(8,128)(2,1)S(1)} %collective-permute-done.12.other_ref, ...), custom_call_target="tpu_custom_call" | custom-call | flops 805306368 | bytes 7340032 | tf_op jit(solution)/shard_map/pallas_call | solution.py:200
  74.8 2.3 %collective-permute-start.13 = (bf16[32,4096]{1,0:T(8,128)(2,1)S(1)}, bf16[32,4096]{1,0:T(8,128)(2,1)S(1)}, u32[]{:S(2)}, u32[]{:S(2)}) collective-permute-start(bf16[32,4096]{1,0:T(8,128)(2,1)S(1)} %get-tuple-element.44), channel_id=1, source_target_pairs={{0,6},{2,0},{4,2},{6,4},{1,7},{3,1},{5,3},{7,5},{8,14},{10,8},{12,... | collective-permute-start | bytes 786440 | tf_op jit(solution)/shard_map/ppermute | solution.py:21
  77.1 1.8 %collective-permute-start.14 = (bf16[32,4096]{1,0:T(8,128)(2,1)S(1)}, bf16[32,4096]{1,0:T(8,128)(2,1)S(1)}, u32[]{:S(2)}, u32[]{:S(2)}) collective-permute-start(bf16[32,4096]{1,0:T(8,128)(2,1)S(1)} %get-tuple-element.45), channel_id=1, source_target_pairs={{0,4},{2,6},{4,0},{6,2},{1,5},{3,7},{5,1},{7,3},{8,12},{10,14},{12... | collective-permute-start | bytes 786440 | tf_op jit(solution)/shard_map/ppermute | solution.py:21
  78.9 1.7 %collective-permute-start.18 = (bf16[3,128,512]{2,1,0:T(8,128)(2,1)}, bf16[3,128,512]{2,1,0:T(8,128)(2,1)S(1)}, u32[]{:S(2)}, u32[]{:S(2)}) collective-permute-start(bf16[3,128,512]{2,1,0:T(8,128)(2,1)} %get-tuple-element.55), channel_id=1, source_target_pairs={{0,192},{64,0},{128,64},{192,128},{1,193},{65,1},{129,65},{193,129... | collective-permute-start | bytes 1179656 | tf_op jit(solution)/shard_map/ppermute | solution.py:21
  80.7 1.3 collective-permute-start.17
  81.9 10.8 %collective-permute-done.13 = bf16[32,4096]{1,0:T(8,128)(2,1)S(1)} collective-permute-done((bf16[32,4096]{1,0:T(8,128)(2,1)S(1)}, bf16[32,4096]{1,0:T(8,128)(2,1)S(1)}, u32[]{:S(2)}, u32[]{:S(2)}) %collective-permute-start.13) | collective-permute-done | bytes 262176 | tf_op jit(solution)/shard_map/ppermute | solution.py:21
  92.8 1.9 %collective-permute-done.15 = bf16[32,4096]{1,0:T(8,128)(2,1)S(1)} collective-permute-done((bf16[32,4096]{1,0:T(8,128)(2,1)S(1)}, bf16[32,4096]{1,0:T(8,128)(2,1)S(1)}, u32[]{:S(2)}, u32[]{:S(2)}) %collective-permute-start.15) | collective-permute-done | bytes 262176 | tf_op jit(solution)/shard_map/ppermute | solution.py:21
  95.6 7.1 %all-to-all-start.1 = ((bf16[8,4,4096]{2,1,0:T(4,128)(2,1)}), bf16[8,4,4096]{2,1,0:T(4,128)(2,1)S(1)}, u32[]{:S(2)}, u32[]{:S(2)}) async-start(bf16[8,4,4096]{2,1,0:T(4,128)(2,1)} %reshape.17), calls=%async_computation.1 | async-start | bytes 524288 | tf_op jit(solution)/shard_map/all_to_all | solution.py:232
  102.7 3.1 %collective-permute-start.19 = (bf16[3,128,512]{2,1,0:T(8,128)(2,1)S(1)}, bf16[3,128,512]{2,1,0:T(8,128)(2,1)S(1)}, u32[]{:S(2)}, u32[]{:S(2)}) collective-permute-start(bf16[3,128,512]{2,1,0:T(8,128)(2,1)S(1)} %copy-done.6), channel_id=1, source_target_pairs={{0,128},{64,192},{128,0},{192,64},{1,129},{65,193},{129,1},{193,65... | collective-permute-start | bytes 1179656 | tf_op jit(solution)/shard_map/ppermute | solution.py:21
  107.1 9.7 %shard_map.96 = (f32[3,64,4096]{2,1,0:T(8,128)}, f32[3,64,4096]{2,1,0:T(8,128)}) custom-call(s32[3]{0:T(128)} %pad_add_fusion.at_ref, bf16[2,256,384]{2,1,0:T(8,128)(2,1)} %copy-done.7, bf16[2,256,384]{2,1,0:T(8,128)(2,1)} %copy-done.8, bf16[1024,4096]{1,0:T(8,128)(2,1)} %all-gather.2.cloned.1.call-done.refs_2_), custom_call_target="tpu_custom_call" | custom-call | flops 3221225472 | bytes 14680064 | tf_op jit(solution)/shard_map/pallas_call | solution.py:213
  117.1 4.1 %collective-permute-start.22 = (bf16[4,4096]{1,0:T(4,128)(2,1)S(1)}, bf16[4,4096]{1,0:T(4,128)(2,1)S(1)}, u32[]{:S(2)}, u32[]{:S(2)}) collective-permute-start(bf16[4,4096]{1,0:T(4,128)(2,1)S(1)} %reduce_sum.12), channel_id=1, source_target_pairs={{0,128},{64,192},{128,0},{192,64},{1,129},{65,193},{129,1},{193,65... | collective-permute-start | bytes 98312 | tf_op jit(solution)/shard_map/ppermute | solution.py:21
  121.7 1.8 %collective-permute-done.20 = bf16[3,128,512]{2,1,0:T(8,128)(2,1)S(1)} collective-permute-done((bf16[3,128,512]{2,1,0:T(8,128)(2,1)S(1)}, bf16[3,128,512]{2,1,0:T(8,128)(2,1)S(1)}, u32[]{:S(2)}, u32[]{:S(2)}) %collective-permute-start.20) | collective-permute-done | bytes 393248 | tf_op jit(solution)/shard_map/ppermute | solution.py:21
  (60 shorter events, 13.1 us)
Async XLA Ops:
  7.2 39.4 %copy-start = (bf16[3,64,4096]{2,1,0:T(8,128)(2,1)S(1)}, bf16[3,64,4096]{2,1,0:T(8,128)(2,1)}, u32[]{:S(2)}) copy-start(bf16[3,64,4096]{2,1,0:T(8,128)(2,1)} %own_key.3) | copy-start | bytes 4718596
  7.2 99.2 %all-gather.2.cloned.1.call-start = ((), (), s32[]{:S(2)}) async-start(), calls=%async_computation.2 | async-start | bytes 8519680 | tf_op jit(solution)/shard_map/all_gather | solution.py:162
  7.9 22.6 %collective-permute-start = (bf16[3,64,4096]{2,1,0:T(8,128)(2,1)}, bf16[3,64,4096]{2,1,0:T(8,128)(2,1)S(1)}, u32[]{:S(2)}, u32[]{:S(2)}) collective-permute-start(bf16[3,64,4096]{2,1,0:T(8,128)(2,1)} %own_key.3), channel_id=1, source_target_pairs={{0,1},{1,0},{2,3},{3,2},{4,5},{5,4},{6,7},{7,6},{8,9},{9,8},{10,11... | collective-permute-start | bytes 4718600 | tf_op jit(solution)/shard_map/ppermute | solution.py:21
  8.0 22.6 %collective-permute-start.1 = (bf16[3,64,4096]{2,1,0:T(8,128)(2,1)}, bf16[3,64,4096]{2,1,0:T(8,128)(2,1)}, u32[]{:S(2)}, u32[]{:S(2)}) collective-permute-start(bf16[3,64,4096]{2,1,0:T(8,128)(2,1)} %own_value.3), channel_id=1, source_target_pairs={{0,1},{1,0},{2,3},{3,2},{4,5},{5,4},{6,7},{7,6},{8,9},{9,8},{10,11... | collective-permute-start | bytes 4718600 | tf_op jit(solution)/shard_map/ppermute | solution.py:21
  10.1 19.4 %all-to-all-start = ((bf16[8,4,4096]{2,1,0:T(4,128)(2,1)}), bf16[8,4,4096]{2,1,0:T(4,128)(2,1)}, u32[]{:S(2)}, u32[]{:S(2)}) async-start(bf16[8,4,4096]{2,1,0:T(4,128)(2,1)} %broadcast_in_dim.3), calls=%async_computation | async-start | bytes 524288 | tf_op jit(solution)/shard_map/all_to_all | solution.py:165
  30.6 12.7 %collective-permute-start.4 = (bf16[32,4096]{1,0:T(8,128)(2,1)S(1)}, bf16[32,4096]{1,0:T(8,128)(2,1)S(1)}, u32[]{:S(2)}, u32[]{:S(2)}) collective-permute-start(bf16[32,4096]{1,0:T(8,128)(2,1)S(1)} %reshape.16.refs_0_), channel_id=1, source_target_pairs={{0,6},{2,0},{4,2},{6,4},{1,7},{3,1},{5,3},{7,5},{8,14},{10,8},{12,... | collective-permute-start | bytes 786440 | tf_op jit(solution)/shard_map/ppermute | solution.py:21
  33.5 11.3 %collective-permute-start.3 = (bf16[32,4096]{1,0:T(8,128)(2,1)S(1)}, bf16[32,4096]{1,0:T(8,128)(2,1)S(1)}, u32[]{:S(2)}, u32[]{:S(2)}) collective-permute-start(bf16[32,4096]{1,0:T(8,128)(2,1)S(1)} %reshape.16.refs_0_), channel_id=1, source_target_pairs={{0,4},{2,6},{4,0},{6,2},{1,5},{3,7},{5,1},{7,3},{8,12},{10,14},{12... | collective-permute-start | bytes 786440 | tf_op jit(solution)/shard_map/ppermute | solution.py:21
  34.2 12.4 %collective-permute-start.2 = (bf16[32,4096]{1,0:T(8,128)(2,1)S(1)}, bf16[32,4096]{1,0:T(8,128)(2,1)S(1)}, u32[]{:S(2)}, u32[]{:S(2)}) collective-permute-start(bf16[32,4096]{1,0:T(8,128)(2,1)S(1)} %reshape.16.refs_0_), channel_id=1, source_target_pairs={{0,2},{2,4},{4,6},{6,0},{1,3},{3,5},{5,7},{7,1},{8,10},{10,12},{12... | collective-permute-start | bytes 786440 | tf_op jit(solution)/shard_map/ppermute | solution.py:21
  36.1 16.5 %collective-permute-start.8 = (bf16[3,128,512]{2,1,0:T(8,128)(2,1)S(1)}, bf16[3,128,512]{2,1,0:T(8,128)(2,1)S(1)}, u32[]{:S(2)}, u32[]{:S(2)}) collective-permute-start(bf16[3,128,512]{2,1,0:T(8,128)(2,1)S(1)} %pad_maximum_fusion.refs_0_), channel_id=1, source_target_pairs={{0,192},{64,0},{128,64},{192,128},{1,193},{65,1},{129,65},{193,129... | collective-permute-start | bytes 1179656 | tf_op jit(solution)/shard_map/ppermute | solution.py:21
  39.2 13.4 %collective-permute-start.7 = (bf16[3,128,512]{2,1,0:T(8,128)(2,1)S(1)}, bf16[3,128,512]{2,1,0:T(8,128)(2,1)S(1)}, u32[]{:S(2)}, u32[]{:S(2)}) collective-permute-start(bf16[3,128,512]{2,1,0:T(8,128)(2,1)S(1)} %pad_maximum_fusion.refs_0_), channel_id=1, source_target_pairs={{0,128},{64,192},{128,0},{192,64},{1,129},{65,193},{129,1},{193,65... | collective-permute-start | bytes 1179656 | tf_op jit(solution)/shard_map/ppermute | solution.py:21
  43.3 13.1 %collective-permute-start.6 = (bf16[3,128,512]{2,1,0:T(8,128)(2,1)S(1)}, bf16[3,128,512]{2,1,0:T(8,128)(2,1)S(1)}, u32[]{:S(2)}, u32[]{:S(2)}) collective-permute-start(bf16[3,128,512]{2,1,0:T(8,128)(2,1)S(1)} %pad_maximum_fusion.refs_0_), channel_id=1, source_target_pairs={{0,64},{64,128},{128,192},{192,0},{1,65},{65,129},{129,193},{193,1... | collective-permute-start | bytes 1179656 | tf_op jit(solution)/shard_map/ppermute | solution.py:21
  51.3 1.4 %collective-permute-start.5 = (bf16[128,384]{1,0:T(8,128)(2,1)S(1)}, bf16[128,384]{1,0:T(8,128)(2,1)S(1)}, u32[]{:S(2)}, u32[]{:S(2)}) collective-permute-start(bf16[128,384]{1,0:T(8,128)(2,1)S(1)} %get-tuple-element.40), channel_id=1, source_target_pairs={{0,1},{1,0},{2,3},{3,2},{4,5},{5,4},{6,7},{7,6},{8,9},{9,8},{10,11... | collective-permute-start | bytes 294920 | tf_op jit(solution)/shard_map/ppermute | solution.py:21
  58.3 13.9 %copy-start.2 = (bf16[3,64,4096]{2,1,0:T(8,128)(2,1)S(1)}, bf16[3,64,4096]{2,1,0:T(8,128)(2,1)}, u32[]{:S(2)}) copy-start(bf16[3,64,4096]{2,1,0:T(8,128)(2,1)} %own_value.3) | copy-start | bytes 4718596
  58.4 4.3 %collective-permute-start.11 = (f32[8,2048]{1,0:T(8,128)S(1)}, f32[8,2048]{1,0:T(8,128)S(1)}, u32[]{:S(2)}, u32[]{:S(2)}) collective-permute-start(f32[8,2048]{1,0:T(8,128)S(1)} %shard_map.93.refs_4_), channel_id=1, source_target_pairs={{0,192},{64,0},{128,64},{192,128},{1,193},{65,1},{129,65},{193,129... | collective-permute-start | bytes 196616 | tf_op jit(solution)/shard_map/ppermute | solution.py:21
  59.0 5.8 %collective-permute-start.10 = (f32[8,2048]{1,0:T(8,128)S(1)}, f32[8,2048]{1,0:T(8,128)S(1)}, u32[]{:S(2)}, u32[]{:S(2)}) collective-permute-start(f32[8,2048]{1,0:T(8,128)S(1)} %shard_map.93.refs_4_), channel_id=1, source_target_pairs={{0,128},{64,192},{128,0},{192,64},{1,129},{65,193},{129,1},{193,65... | collective-permute-start | bytes 196616 | tf_op jit(solution)/shard_map/ppermute | solution.py:21
  59.7 5.8 %collective-permute-start.9 = (f32[8,2048]{1,0:T(8,128)S(1)}, f32[8,2048]{1,0:T(8,128)S(1)}, u32[]{:S(2)}, u32[]{:S(2)}) collective-permute-start(f32[8,2048]{1,0:T(8,128)S(1)} %shard_map.93.refs_4_), channel_id=1, source_target_pairs={{0,64},{64,128},{128,192},{192,0},{1,65},{65,129},{129,193},{193,1... | collective-permute-start | bytes 196616 | tf_op jit(solution)/shard_map/ppermute | solution.py:21
  70.8 1.4 %collective-permute-start.12 = (bf16[128,384]{1,0:T(8,128)(2,1)S(1)}, bf16[128,384]{1,0:T(8,128)(2,1)S(1)}, u32[]{:S(2)}, u32[]{:S(2)}) collective-permute-start(bf16[128,384]{1,0:T(8,128)(2,1)S(1)} %slice.9), channel_id=1, source_target_pairs={{0,1},{1,0},{2,3},{3,2},{4,5},{5,4},{6,7},{7,6},{8,9},{9,8},{10,11... | collective-permute-start | bytes 294920 | tf_op jit(solution)/shard_map/ppermute | solution.py:21
  70.9 9.7 %collective-permute-start.16 = (bf16[256,384]{1,0:T(8,128)(2,1)S(1)}, bf16[256,384]{1,0:T(8,128)(2,1)S(1)}, u32[]{:S(2)}, u32[]{:S(2)}) collective-permute-start(bf16[256,384]{1,0:T(8,128)(2,1)S(1)} %get-tuple-element.42.own_ref), channel_id=1, source_target_pairs={{0,64},{64,0},{128,192},{192,128},{1,65},{65,1},{129,193},{193,129... | collective-permute-start | bytes 589832 | tf_op jit(solution)/shard_map/ppermute | solution.py:206
  74.8 18.0 %collective-permute-start.13 = (bf16[32,4096]{1,0:T(8,128)(2,1)S(1)}, bf16[32,4096]{1,0:T(8,128)(2,1)S(1)}, u32[]{:S(2)}, u32[]{:S(2)}) collective-permute-start(bf16[32,4096]{1,0:T(8,128)(2,1)S(1)} %get-tuple-element.44), channel_id=1, source_target_pairs={{0,6},{2,0},{4,2},{6,4},{1,7},{3,1},{5,3},{7,5},{8,14},{10,8},{12,... | collective-permute-start | bytes 786440 | tf_op jit(solution)/shard_map/ppermute | solution.py:21
  77.1 15.7 %collective-permute-start.14 = (bf16[32,4096]{1,0:T(8,128)(2,1)S(1)}, bf16[32,4096]{1,0:T(8,128)(2,1)S(1)}, u32[]{:S(2)}, u32[]{:S(2)}) collective-permute-start(bf16[32,4096]{1,0:T(8,128)(2,1)S(1)} %get-tuple-element.45), channel_id=1, source_target_pairs={{0,4},{2,6},{4,0},{6,2},{1,5},{3,7},{5,1},{7,3},{8,12},{10,14},{12... | collective-permute-start | bytes 786440 | tf_op jit(solution)/shard_map/ppermute | solution.py:21
  78.9 15.8 %collective-permute-start.15 = (bf16[32,4096]{1,0:T(8,128)(2,1)S(1)}, bf16[32,4096]{1,0:T(8,128)(2,1)S(1)}, u32[]{:S(2)}, u32[]{:S(2)}) collective-permute-start(bf16[32,4096]{1,0:T(8,128)(2,1)S(1)} %get-tuple-element.46), channel_id=1, source_target_pairs={{0,2},{2,4},{4,6},{6,0},{1,3},{3,5},{5,7},{7,1},{8,10},{10,12},{12... | collective-permute-start | bytes 786440 | tf_op jit(solution)/shard_map/ppermute | solution.py:21
  78.9 23.8 %collective-permute-start.18 = (bf16[3,128,512]{2,1,0:T(8,128)(2,1)}, bf16[3,128,512]{2,1,0:T(8,128)(2,1)S(1)}, u32[]{:S(2)}, u32[]{:S(2)}) collective-permute-start(bf16[3,128,512]{2,1,0:T(8,128)(2,1)} %get-tuple-element.55), channel_id=1, source_target_pairs={{0,192},{64,0},{128,64},{192,128},{1,193},{65,1},{129,65},{193,129... | collective-permute-start | bytes 1179656 | tf_op jit(solution)/shard_map/ppermute | solution.py:21
  80.6 22.1 %copy-start.6 = (bf16[3,128,512]{2,1,0:T(8,128)(2,1)S(1)}, bf16[3,128,512]{2,1,0:T(8,128)(2,1)}, u32[]{:S(2)}) copy-start(bf16[3,128,512]{2,1,0:T(8,128)(2,1)} %copy-done.5) | copy-start | bytes 1179652
  80.6 25.2 %copy-start.4 = (bf16[3,128,512]{2,1,0:T(8,128)(2,1)S(1)}, bf16[3,128,512]{2,1,0:T(8,128)(2,1)}, u32[]{:S(2)}) copy-start(bf16[3,128,512]{2,1,0:T(8,128)(2,1)} %copy-done.3) | copy-start | bytes 1179652
  80.7 25.8 %copy-start.7 = (bf16[2,256,384]{2,1,0:T(8,128)(2,1)}, bf16[2,256,384]{2,1,0:T(8,128)(2,1)S(1)}, u32[]{:S(2)}) copy-start(bf16[2,256,384]{2,1,0:T(8,128)(2,1)S(1)} %pad_maximum_fusion.1.refs_0_) | copy-start | bytes 1179652
  80.7 25.7 %collective-permute-start.17 = (bf16[2,256,384]{2,1,0:T(8,128)(2,1)S(1)}, bf16[2,256,384]{2,1,0:T(8,128)(2,1)S(1)}, u32[]{:S(2)}, u32[]{:S(2)}) collective-permute-start(bf16[2,256,384]{2,1,0:T(8,128)(2,1)S(1)} %pad_maximum_fusion.1.refs_0_), channel_id=1, source_target_pairs={{0,128},{64,192},{128,0},{192,64},{1,129},{65,193},{129,1},{193,65... | collective-permute-start | bytes 1179656 | tf_op jit(solution)/shard_map/ppermute | solution.py:207
  95.6 21.2 %all-to-all-start.1 = ((bf16[8,4,4096]{2,1,0:T(4,128)(2,1)}), bf16[8,4,4096]{2,1,0:T(4,128)(2,1)S(1)}, u32[]{:S(2)}, u32[]{:S(2)}) async-start(bf16[8,4,4096]{2,1,0:T(4,128)(2,1)} %reshape.17), calls=%async_computation.1 | async-start | bytes 524288 | tf_op jit(solution)/shard_map/all_to_all | solution.py:232
  102.7 19.0 %collective-permute-start.19 = (bf16[3,128,512]{2,1,0:T(8,128)(2,1)S(1)}, bf16[3,128,512]{2,1,0:T(8,128)(2,1)S(1)}, u32[]{:S(2)}, u32[]{:S(2)}) collective-permute-start(bf16[3,128,512]{2,1,0:T(8,128)(2,1)S(1)} %copy-done.6), channel_id=1, source_target_pairs={{0,128},{64,192},{128,0},{192,64},{1,129},{65,193},{129,1},{193,65... | collective-permute-start | bytes 1179656 | tf_op jit(solution)/shard_map/ppermute | solution.py:21
  105.8 17.7 %collective-permute-start.20 = (bf16[3,128,512]{2,1,0:T(8,128)(2,1)S(1)}, bf16[3,128,512]{2,1,0:T(8,128)(2,1)S(1)}, u32[]{:S(2)}, u32[]{:S(2)}) collective-permute-start(bf16[3,128,512]{2,1,0:T(8,128)(2,1)S(1)} %copy-done.4), channel_id=1, source_target_pairs={{0,64},{64,128},{128,192},{192,0},{1,65},{65,129},{129,193},{193,1... | collective-permute-start | bytes 1179656 | tf_op jit(solution)/shard_map/ppermute | solution.py:21
  117.0 7.5 %collective-permute-start.23 = (bf16[4,4096]{1,0:T(4,128)(2,1)S(1)}, bf16[4,4096]{1,0:T(4,128)(2,1)S(1)}, u32[]{:S(2)}, u32[]{:S(2)}) collective-permute-start(bf16[4,4096]{1,0:T(4,128)(2,1)S(1)} %reduce_sum.12), channel_id=1, source_target_pairs={{0,64},{64,128},{128,192},{192,0},{1,65},{65,129},{129,193},{193,1... | collective-permute-start | bytes 98312 | tf_op jit(solution)/shard_map/ppermute | solution.py:21
  117.1 7.5 %collective-permute-start.22 = (bf16[4,4096]{1,0:T(4,128)(2,1)S(1)}, bf16[4,4096]{1,0:T(4,128)(2,1)S(1)}, u32[]{:S(2)}, u32[]{:S(2)}) collective-permute-start(bf16[4,4096]{1,0:T(4,128)(2,1)S(1)} %reduce_sum.12), channel_id=1, source_target_pairs={{0,128},{64,192},{128,0},{192,64},{1,129},{65,193},{129,1},{193,65... | collective-permute-start | bytes 98312 | tf_op jit(solution)/shard_map/ppermute | solution.py:21
  121.2 3.9 %collective-permute-start.21 = (bf16[4,4096]{1,0:T(4,128)(2,1)S(1)}, bf16[4,4096]{1,0:T(4,128)(2,1)S(1)}, u32[]{:S(2)}, u32[]{:S(2)}) collective-permute-start(bf16[4,4096]{1,0:T(4,128)(2,1)S(1)} %reduce_sum.12), channel_id=1, source_target_pairs={{0,192},{64,0},{128,64},{192,128},{1,193},{65,1},{129,65},{193,129... | collective-permute-start | bytes 98312 | tf_op jit(solution)/shard_map/ppermute | solution.py:21
  (4 other events, 10.1 us)
Sparse Core Ops, SparseCore 0:
  10.8 91.3 all-gather.1

commit v5 on v4

--- a/solution.py
+++ b/solution.py
@@ -224,10 +224,10 @@
         cost_estimate=cost(2 * cols * full.size, 2 * full.size + 4 * cols * d),
     )(at, *g_all, full)
 
-    qa[1] = shift(qa[1], "dp", -1)
-    part, qa[2], qa[3] = lax.optimization_barrier((part, qa[2], qa[3]))
+    qa[2] = shift(qa[2], "dp", -2)
+    part, qa[1], qa[3] = lax.optimization_barrier((part, qa[1], qa[3]))
     qa[1], qa[2], qa[3] = lax.optimization_barrier((qa[1], qa[2], qa[3]))
-    qa[2], qa[3] = shift(qa[2], "dp", -2), shift(qa[3], "dp", -3)
+    qa[1], qa[3] = shift(qa[1], "dp", -1), shift(qa[3], "dp", -3)
 
     part = lax.all_to_all(part.reshape(nz, few, d), "z", 0, 0)
     part, grad_w_key, grad_w_value = lax.optimization_barrier((part, *grad_w))

time: 134 us -> 133 us (level)
  no operation moved by 1% of the time
where the time goes in v5:
time: 133 us
  starting transfers between devices  44.8 us (34%)
  waiting for transfers between devices  41.3 us (31%)
  Pallas kernels  22.8 us (17%)
  between operations  14.2 us (11%)
  local copies, waits for them, and re-layouts  6.53 us (5%)
  other arithmetic  2.91 us (2%)
    ppermute x22, waiting for transfers between devices, shift(): return lax.ppermute(x, axis, [(a, (a + by) % n) for a in range(n)])  30.4 us
    ppermute x22, starting transfers between devices, shift(): return lax.ppermute(x, axis, [(a, (a + by) % n) for a in range(n)])  26.5 us
    all_to_all x1, waiting for transfers between devices, shards(): lax.all_to_all(jnp.broadcast_to(quarter, (nz, few, d)), 'z', 0, 0)  10.2 us
    pallas_call x1, Pallas kernels, shards(): pl.pallas_call(weights_kernel, grid_spec=pltpu.PrefetchScalarGridSpec(num...  9.69 us
    all_to_all x1, starting transfers between devices, shards(): lax.all_to_all(jnp.broadcast_to(quarter, (nz, few, d)), 'z', 0, 0)  8.57 us
    all_to_all x1, starting transfers between devices, shards(): part = lax.all_to_all(part.reshape(nz, few, d), 'z', 0, 0)  7.1 us
    pallas_call x1, Pallas kernels, shards(): pl.pallas_call(grads_kernel, out_shape=[jax.ShapeDtypeStruct((2 * half, c...  5.37 us
    pallas_call x1, Pallas kernels, shards(): pl.pallas_call(project_kernel, out_shape=(jax.ShapeDtypeStruct((half, col...  3.27 us
  transfers between devices with their start and end apart: 27, of which 13 were waited for; matrix products, arithmetic and copies ran while one was open for 5% of the time, Pallas kernels for 17%

profile of v5, /device:TPU:32, one launch (start us, length us, event | category | flops | bytes accessed | tf_op | source)
XLA Modules:
  0.0 132.5 jit_solution(5797831020076213933)
XLA Ops:
  8.5 0.9 constant_dynamic-slice_fusion
  10.1 8.6 %all-to-all-start = ((bf16[8,4,4096]{2,1,0:T(4,128)(2,1)}), bf16[8,4,4096]{2,1,0:T(4,128)(2,1)}, u32[]{:S(2)}, u32[]{:S(2)}) async-start(bf16[8,4,4096]{2,1,0:T(4,128)(2,1)} %broadcast_in_dim.3), calls=%async_computation | async-start | bytes 524288 | tf_op jit(solution)/shard_map/all_to_all | solution.py:165
  19.3 10.2 %all-to-all-done = bf16[8,4,4096]{2,1,0:T(4,128)(2,1)} async-done(((bf16[8,4,4096]{2,1,0:T(4,128)(2,1)}), bf16[8,4,4096]{2,1,0:T(4,128)(2,1)}, u32[]{:S(2)}, u32[]{:S(2)}) %all-to-all-start) | async-done | bytes 262176 | tf_op jit(solution)/shard_map/all_to_all | solution.py:165
  29.5 1.0 reshape.16.refs_0_
  30.6 2.9 %collective-permute-start.4 = (bf16[32,4096]{1,0:T(8,128)(2,1)S(1)}, bf16[32,4096]{1,0:T(8,128)(2,1)S(1)}, u32[]{:S(2)}, u32[]{:S(2)}) collective-permute-start(bf16[32,4096]{1,0:T(8,128)(2,1)S(1)} %reshape.16.refs_0_), channel_id=1, source_target_pairs={{0,6},{2,0},{4,2},{6,4},{1,7},{3,1},{5,3},{7,5},{8,14},{10,8},{12,... | collective-permute-start | bytes 786440 | tf_op jit(solution)/shard_map/ppermute | solution.py:21
  34.2 0.9 collective-permute-start.2
  35.1 1.0 pad_maximum_fusion.refs_0_
  36.1 3.1 %collective-permute-start.8 = (bf16[3,128,512]{2,1,0:T(8,128)(2,1)S(1)}, bf16[3,128,512]{2,1,0:T(8,128)(2,1)S(1)}, u32[]{:S(2)}, u32[]{:S(2)}) collective-permute-start(bf16[3,128,512]{2,1,0:T(8,128)(2,1)S(1)} %pad_maximum_fusion.refs_0_), channel_id=1, source_target_pairs={{0,192},{64,0},{128,64},{192,128},{1,193},{65,1},{129,65},{193,129... | collective-permute-start | bytes 1179656 | tf_op jit(solution)/shard_map/ppermute | solution.py:21
  39.9 3.4 %collective-permute-done.4.refs_3_ = bf16[32,4096]{1,0:T(8,128)(2,1)S(1)} collective-permute-done((bf16[32,4096]{1,0:T(8,128)(2,1)S(1)}, bf16[32,4096]{1,0:T(8,128)(2,1)S(1)}, u32[]{:S(2)}, u32[]{:S(2)}) %collective-permute-start.4) | collective-permute-done | bytes 262176 | tf_op jit(solution)/shard_map/ppermute | solution.py:21
  43.3 1.6 %collective-permute-start.6 = (bf16[3,128,512]{2,1,0:T(8,128)(2,1)S(1)}, bf16[3,128,512]{2,1,0:T(8,128)(2,1)S(1)}, u32[]{:S(2)}, u32[]{:S(2)}) collective-permute-start(bf16[3,128,512]{2,1,0:T(8,128)(2,1)S(1)} %pad_maximum_fusion.refs_0_), channel_id=1, source_target_pairs={{0,64},{64,128},{128,192},{192,0},{1,65},{65,129},{129,193},{193,1... | collective-permute-start | bytes 1179656 | tf_op jit(solution)/shard_map/ppermute | solution.py:21
  44.8 1.7 %collective-permute-done.2.refs_1_ = bf16[32,4096]{1,0:T(8,128)(2,1)S(1)} collective-permute-done((bf16[32,4096]{1,0:T(8,128)(2,1)S(1)}, bf16[32,4096]{1,0:T(8,128)(2,1)S(1)}, u32[]{:S(2)}, u32[]{:S(2)}) %collective-permute-start.2) | collective-permute-done | bytes 262176 | tf_op jit(solution)/shard_map/ppermute | solution.py:21
  46.6 1.4 %copy-done.1 = bf16[3,64,4096]{2,1,0:T(8,128)(2,1)S(1)} copy-done((bf16[3,64,4096]{2,1,0:T(8,128)(2,1)S(1)}, bf16[3,64,4096]{2,1,0:T(8,128)(2,1)}, u32[]{:S(2)}) %copy-start.1) | copy-done | bytes 1572888
  48.0 3.3 %shard_map.92 = (bf16[128,384]{1,0:T(8,128)(2,1)S(1)}, bf16[128,384]{1,0:T(8,128)(2,1)S(1)}) custom-call(bf16[3,64,4096]{2,1,0:T(8,128)(2,1)S(1)} %copy-done, bf16[3,64,4096]{2,1,0:T(8,128)(2,1)S(1)} %copy-done.1, bf16[3,64,4096]{2,1,0:T(8,128)(2,1)S(1)} %collective-permute-done.other_key, bf16[3,64,4096]{2,1,0:T(8,128)(2,1)} %collective-permute-done.1.other_value, ...), custom_call_target="tpu_custom_call" | custom-call | flops 805306368 | bytes 7340032 | tf_op jit(solution)/shard_map/pallas_call | solution.py:175
  51.4 1.3 collective-permute-done.5.other_ref
  52.7 3.7 %collective-permute-done.6.refs_1_ = bf16[3,128,512]{2,1,0:T(8,128)(2,1)S(1)} collective-permute-done((bf16[3,128,512]{2,1,0:T(8,128)(2,1)S(1)}, bf16[3,128,512]{2,1,0:T(8,128)(2,1)S(1)}, u32[]{:S(2)}, u32[]{:S(2)}) %collective-permute-start.6) | collective-permute-done | bytes 393248 | tf_op jit(solution)/shard_map/ppermute | solution.py:21
  56.4 1.9 %shard_map.93.refs_4_ = f32[8,2048]{1,0:T(8,128)S(1)} custom-call(bf16[128,384]{1,0:T(8,128)(2,1)S(1)} %get-tuple-element.39.own_ref, bf16[128,384]{1,0:T(8,128)(2,1)S(1)} %collective-permute-done.5.other_ref, bf16[3,128,512]{2,1,0:T(8,128)(2,1)S(1)} %pad_maximum_fusion.refs_0_, bf16[3,128,512]{2,1,0:T(8,128)(2,1)S(1)} %collective-permute-done.6.refs_1_, ...), custom_call_target="tpu_custom_call" | custom-call | flops 1610612736 | bytes 3145728 | tf_op jit(solution)/shard_map/pallas_call | solution.py:185
  60.5 2.2 %collective-permute-done.11.refs_7_ = f32[8,2048]{1,0:T(8,128)S(1)} collective-permute-done((f32[8,2048]{1,0:T(8,128)S(1)}, f32[8,2048]{1,0:T(8,128)S(1)}, u32[]{:S(2)}, u32[]{:S(2)}) %collective-permute-start.11) | collective-permute-done | bytes 65568 | tf_op jit(solution)/shard_map/ppermute | solution.py:21
  62.7 2.1 %collective-permute-done.10.refs_6_ = f32[8,2048]{1,0:T(8,128)S(1)} collective-permute-done((f32[8,2048]{1,0:T(8,128)S(1)}, f32[8,2048]{1,0:T(8,128)S(1)}, u32[]{:S(2)}, u32[]{:S(2)}) %collective-permute-start.10) | collective-permute-done | bytes 65568 | tf_op jit(solution)/shard_map/ppermute | solution.py:21
  65.5 5.4 %shard_map.94 = (bf16[256,384]{1,0:T(8,128)(2,1)S(1)}, bf16[3,128,512]{2,1,0:T(8,128)(2,1)S(1)}, bf16[3,128,512]{2,1,0:T(8,128)(2,1)S(1)}, bf16[3,128,512]{2,1,0:T(8,128)(2,1)}, bf16[3,128,512]{2,1,0:T(8,128)(2,1)S(1)}) custom-call(bf16[128,384]{1,0:T(8,128)(2,1)S(1)} %get-tuple-element.39.own_ref, bf16[128,384]{1,0:T(8,128)(2,1)S(1)} %collective-permute-done.5.other_ref, ...), custom_call_target="tpu_custom_call" | custom-call | flops 4831838208 | bytes 6291456 | tf_op jit(solution)/shard_map/pallas_call | solution.py:192
  72.3 2.6 %shard_map.95 = (bf16[32,4096]{1,0:T(8,128)(2,1)S(1)}, bf16[32,4096]{1,0:T(8,128)(2,1)S(1)}, bf16[32,4096]{1,0:T(8,128)(2,1)S(1)}, bf16[32,4096]{1,0:T(8,128)(2,1)S(1)}) custom-call(bf16[256,384]{1,0:T(8,128)(2,1)S(1)} %get-tuple-element.42.own_ref, bf16[128,384]{1,0:T(8,128)(2,1)S(1)} %collective-permute-done.12.other_ref, ...), custom_call_target="tpu_custom_call" | custom-call | flops 805306368 | bytes 7340032 | tf_op jit(solution)/shard_map/pallas_call | solution.py:200
  74.9 2.3 %collective-permute-start.13 = (bf16[32,4096]{1,0:T(8,128)(2,1)S(1)}, bf16[32,4096]{1,0:T(8,128)(2,1)S(1)}, u32[]{:S(2)}, u32[]{:S(2)}) collective-permute-start(bf16[32,4096]{1,0:T(8,128)(2,1)S(1)} %get-tuple-element.44), channel_id=1, source_target_pairs={{0,6},{2,0},{4,2},{6,4},{1,7},{3,1},{5,3},{7,5},{8,14},{10,8},{12,... | collective-permute-start | bytes 786440 | tf_op jit(solution)/shard_map/ppermute | solution.py:21
  77.1 1.8 %collective-permute-start.14 = (bf16[32,4096]{1,0:T(8,128)(2,1)S(1)}, bf16[32,4096]{1,0:T(8,128)(2,1)S(1)}, u32[]{:S(2)}, u32[]{:S(2)}) collective-permute-start(bf16[32,4096]{1,0:T(8,128)(2,1)S(1)} %get-tuple-element.45), channel_id=1, source_target_pairs={{0,4},{2,6},{4,0},{6,2},{1,5},{3,7},{5,1},{7,3},{8,12},{10,14},{12... | collective-permute-start | bytes 786440 | tf_op jit(solution)/shard_map/ppermute | solution.py:21
  79.0 1.9 %collective-permute-start.18 = (bf16[3,128,512]{2,1,0:T(8,128)(2,1)}, bf16[3,128,512]{2,1,0:T(8,128)(2,1)S(1)}, u32[]{:S(2)}, u32[]{:S(2)}) collective-permute-start(bf16[3,128,512]{2,1,0:T(8,128)(2,1)} %get-tuple-element.56), channel_id=1, source_target_pairs={{0,128},{64,192},{128,0},{192,64},{1,129},{65,193},{129,1},{193,65... | collective-permute-start | bytes 1179656 | tf_op jit(solution)/shard_map/ppermute | solution.py:21
  80.9 1.8 %collective-permute-start.17 = (bf16[2,256,384]{2,1,0:T(8,128)(2,1)S(1)}, bf16[2,256,384]{2,1,0:T(8,128)(2,1)S(1)}, u32[]{:S(2)}, u32[]{:S(2)}) collective-permute-start(bf16[2,256,384]{2,1,0:T(8,128)(2,1)S(1)} %pad_maximum_fusion.1.refs_0_), channel_id=1, source_target_pairs={{0,128},{64,192},{128,0},{192,64},{1,129},{65,193},{129,1},{193,65... | collective-permute-start | bytes 1179656 | tf_op jit(solution)/shard_map/ppermute | solution.py:207
  82.7 10.2 %collective-permute-done.13 = bf16[32,4096]{1,0:T(8,128)(2,1)S(1)} collective-permute-done((bf16[32,4096]{1,0:T(8,128)(2,1)S(1)}, bf16[32,4096]{1,0:T(8,128)(2,1)S(1)}, u32[]{:S(2)}, u32[]{:S(2)}) %collective-permute-start.13) | collective-permute-done | bytes 262176 | tf_op jit(solution)/shard_map/ppermute | solution.py:21
  92.8 1.8 %collective-permute-done.15 = bf16[32,4096]{1,0:T(8,128)(2,1)S(1)} collective-permute-done((bf16[32,4096]{1,0:T(8,128)(2,1)S(1)}, bf16[32,4096]{1,0:T(8,128)(2,1)S(1)}, u32[]{:S(2)}, u32[]{:S(2)}) %collective-permute-start.15) | collective-permute-done | bytes 262176 | tf_op jit(solution)/shard_map/ppermute | solution.py:21
  95.6 7.1 %all-to-all-start.1 = ((bf16[8,4,4096]{2,1,0:T(4,128)(2,1)}), bf16[8,4,4096]{2,1,0:T(4,128)(2,1)S(1)}, u32[]{:S(2)}, u32[]{:S(2)}) async-start(bf16[8,4,4096]{2,1,0:T(4,128)(2,1)} %reshape.17), calls=%async_computation.1 | async-start | bytes 524288 | tf_op jit(solution)/shard_map/all_to_all | solution.py:232
  102.7 2.8 %collective-permute-start.19 = (bf16[3,128,512]{2,1,0:T(8,128)(2,1)S(1)}, bf16[3,128,512]{2,1,0:T(8,128)(2,1)S(1)}, u32[]{:S(2)}, u32[]{:S(2)}) collective-permute-start(bf16[3,128,512]{2,1,0:T(8,128)(2,1)S(1)} %copy-done.6), channel_id=1, source_target_pairs={{0,192},{64,0},{128,64},{192,128},{1,193},{65,1},{129,65},{193,129... | collective-permute-start | bytes 1179656 | tf_op jit(solution)/shard_map/ppermute | solution.py:21
  106.3 9.7 %shard_map.96 = (f32[3,64,4096]{2,1,0:T(8,128)}, f32[3,64,4096]{2,1,0:T(8,128)}) custom-call(s32[3]{0:T(128)} %pad_add_fusion.at_ref, bf16[2,256,384]{2,1,0:T(8,128)(2,1)} %copy-done.7, bf16[2,256,384]{2,1,0:T(8,128)(2,1)} %copy-done.8, bf16[1024,4096]{1,0:T(8,128)(2,1)} %all-gather.2.cloned.1.call-done.refs_2_), custom_call_target="tpu_custom_call" | custom-call | flops 3221225472 | bytes 14680064 | tf_op jit(solution)/shard_map/pallas_call | solution.py:213
  116.9 3.9 %collective-permute-start.22 = (bf16[4,4096]{1,0:T(4,128)(2,1)S(1)}, bf16[4,4096]{1,0:T(4,128)(2,1)S(1)}, u32[]{:S(2)}, u32[]{:S(2)}) collective-permute-start(bf16[4,4096]{1,0:T(4,128)(2,1)S(1)} %reduce_sum.12), channel_id=1, source_target_pairs={{0,128},{64,192},{128,0},{192,64},{1,129},{65,193},{129,1},{193,65... | collective-permute-start | bytes 98312 | tf_op jit(solution)/shard_map/ppermute | solution.py:21
  122.1 1.0 collective-permute-done.22
  123.1 1.7 %collective-permute-done.21 = bf16[4,4096]{1,0:T(4,128)(2,1)S(1)} collective-permute-done((bf16[4,4096]{1,0:T(4,128)(2,1)S(1)}, bf16[4,4096]{1,0:T(4,128)(2,1)S(1)}, u32[]{:S(2)}, u32[]{:S(2)}) %collective-permute-start.21) | collective-permute-done | bytes 32800 | tf_op jit(solution)/shard_map/ppermute | solution.py:21
  (60 shorter events, 13.2 us)
Async XLA Ops:
  7.2 39.4 %copy-start = (bf16[3,64,4096]{2,1,0:T(8,128)(2,1)S(1)}, bf16[3,64,4096]{2,1,0:T(8,128)(2,1)}, u32[]{:S(2)}) copy-start(bf16[3,64,4096]{2,1,0:T(8,128)(2,1)} %own_key.3) | copy-start | bytes 4718596
  7.2 98.4 %all-gather.2.cloned.1.call-start = ((), (), s32[]{:S(2)}) async-start(), calls=%async_computation.2 | async-start | bytes 8519680 | tf_op jit(solution)/shard_map/all_gather | solution.py:162
  7.9 22.6 %collective-permute-start = (bf16[3,64,4096]{2,1,0:T(8,128)(2,1)}, bf16[3,64,4096]{2,1,0:T(8,128)(2,1)S(1)}, u32[]{:S(2)}, u32[]{:S(2)}) collective-permute-start(bf16[3,64,4096]{2,1,0:T(8,128)(2,1)} %own_key.3), channel_id=1, source_target_pairs={{0,1},{1,0},{2,3},{3,2},{4,5},{5,4},{6,7},{7,6},{8,9},{9,8},{10,11... | collective-permute-start | bytes 4718600 | tf_op jit(solution)/shard_map/ppermute | solution.py:21
  8.0 22.6 %collective-permute-start.1 = (bf16[3,64,4096]{2,1,0:T(8,128)(2,1)}, bf16[3,64,4096]{2,1,0:T(8,128)(2,1)}, u32[]{:S(2)}, u32[]{:S(2)}) collective-permute-start(bf16[3,64,4096]{2,1,0:T(8,128)(2,1)} %own_value.3), channel_id=1, source_target_pairs={{0,1},{1,0},{2,3},{3,2},{4,5},{5,4},{6,7},{7,6},{8,9},{9,8},{10,11... | collective-permute-start | bytes 4718600 | tf_op jit(solution)/shard_map/ppermute | solution.py:21
  10.1 19.4 %all-to-all-start = ((bf16[8,4,4096]{2,1,0:T(4,128)(2,1)}), bf16[8,4,4096]{2,1,0:T(4,128)(2,1)}, u32[]{:S(2)}, u32[]{:S(2)}) async-start(bf16[8,4,4096]{2,1,0:T(4,128)(2,1)} %broadcast_in_dim.3), calls=%async_computation | async-start | bytes 524288 | tf_op jit(solution)/shard_map/all_to_all | solution.py:165
  30.6 12.7 %collective-permute-start.4 = (bf16[32,4096]{1,0:T(8,128)(2,1)S(1)}, bf16[32,4096]{1,0:T(8,128)(2,1)S(1)}, u32[]{:S(2)}, u32[]{:S(2)}) collective-permute-start(bf16[32,4096]{1,0:T(8,128)(2,1)S(1)} %reshape.16.refs_0_), channel_id=1, source_target_pairs={{0,6},{2,0},{4,2},{6,4},{1,7},{3,1},{5,3},{7,5},{8,14},{10,8},{12,... | collective-permute-start | bytes 786440 | tf_op jit(solution)/shard_map/ppermute | solution.py:21
  33.5 11.3 %collective-permute-start.3 = (bf16[32,4096]{1,0:T(8,128)(2,1)S(1)}, bf16[32,4096]{1,0:T(8,128)(2,1)S(1)}, u32[]{:S(2)}, u32[]{:S(2)}) collective-permute-start(bf16[32,4096]{1,0:T(8,128)(2,1)S(1)} %reshape.16.refs_0_), channel_id=1, source_target_pairs={{0,4},{2,6},{4,0},{6,2},{1,5},{3,7},{5,1},{7,3},{8,12},{10,14},{12... | collective-permute-start | bytes 786440 | tf_op jit(solution)/shard_map/ppermute | solution.py:21
  34.2 12.4 %collective-permute-start.2 = (bf16[32,4096]{1,0:T(8,128)(2,1)S(1)}, bf16[32,4096]{1,0:T(8,128)(2,1)S(1)}, u32[]{:S(2)}, u32[]{:S(2)}) collective-permute-start(bf16[32,4096]{1,0:T(8,128)(2,1)S(1)} %reshape.16.refs_0_), channel_id=1, source_target_pairs={{0,2},{2,4},{4,6},{6,0},{1,3},{3,5},{5,7},{7,1},{8,10},{10,12},{12... | collective-permute-start | bytes 786440 | tf_op jit(solution)/shard_map/ppermute | solution.py:21
  36.1 16.5 %collective-permute-start.8 = (bf16[3,128,512]{2,1,0:T(8,128)(2,1)S(1)}, bf16[3,128,512]{2,1,0:T(8,128)(2,1)S(1)}, u32[]{:S(2)}, u32[]{:S(2)}) collective-permute-start(bf16[3,128,512]{2,1,0:T(8,128)(2,1)S(1)} %pad_maximum_fusion.refs_0_), channel_id=1, source_target_pairs={{0,192},{64,0},{128,64},{192,128},{1,193},{65,1},{129,65},{193,129... | collective-permute-start | bytes 1179656 | tf_op jit(solution)/shard_map/ppermute | solution.py:21
  39.2 13.4 %collective-permute-start.7 = (bf16[3,128,512]{2,1,0:T(8,128)(2,1)S(1)}, bf16[3,128,512]{2,1,0:T(8,128)(2,1)S(1)}, u32[]{:S(2)}, u32[]{:S(2)}) collective-permute-start(bf16[3,128,512]{2,1,0:T(8,128)(2,1)S(1)} %pad_maximum_fusion.refs_0_), channel_id=1, source_target_pairs={{0,128},{64,192},{128,0},{192,64},{1,129},{65,193},{129,1},{193,65... | collective-permute-start | bytes 1179656 | tf_op jit(solution)/shard_map/ppermute | solution.py:21
  43.3 13.1 %collective-permute-start.6 = (bf16[3,128,512]{2,1,0:T(8,128)(2,1)S(1)}, bf16[3,128,512]{2,1,0:T(8,128)(2,1)S(1)}, u32[]{:S(2)}, u32[]{:S(2)}) collective-permute-start(bf16[3,128,512]{2,1,0:T(8,128)(2,1)S(1)} %pad_maximum_fusion.refs_0_), channel_id=1, source_target_pairs={{0,64},{64,128},{128,192},{192,0},{1,65},{65,129},{129,193},{193,1... | collective-permute-start | bytes 1179656 | tf_op jit(solution)/shard_map/ppermute | solution.py:21
  51.3 1.4 %collective-permute-start.5 = (bf16[128,384]{1,0:T(8,128)(2,1)S(1)}, bf16[128,384]{1,0:T(8,128)(2,1)S(1)}, u32[]{:S(2)}, u32[]{:S(2)}) collective-permute-start(bf16[128,384]{1,0:T(8,128)(2,1)S(1)} %get-tuple-element.40), channel_id=1, source_target_pairs={{0,1},{1,0},{2,3},{3,2},{4,5},{5,4},{6,7},{7,6},{8,9},{9,8},{10,11... | collective-permute-start | bytes 294920 | tf_op jit(solution)/shard_map/ppermute | solution.py:21
  58.3 13.9 %copy-start.2 = (bf16[3,64,4096]{2,1,0:T(8,128)(2,1)S(1)}, bf16[3,64,4096]{2,1,0:T(8,128)(2,1)}, u32[]{:S(2)}) copy-start(bf16[3,64,4096]{2,1,0:T(8,128)(2,1)} %own_value.3) | copy-start | bytes 4718596
  58.4 4.3 %collective-permute-start.11 = (f32[8,2048]{1,0:T(8,128)S(1)}, f32[8,2048]{1,0:T(8,128)S(1)}, u32[]{:S(2)}, u32[]{:S(2)}) collective-permute-start(f32[8,2048]{1,0:T(8,128)S(1)} %shard_map.93.refs_4_), channel_id=1, source_target_pairs={{0,192},{64,0},{128,64},{192,128},{1,193},{65,1},{129,65},{193,129... | collective-permute-start | bytes 196616 | tf_op jit(solution)/shard_map/ppermute | solution.py:21
  59.0 5.8 %collective-permute-start.10 = (f32[8,2048]{1,0:T(8,128)S(1)}, f32[8,2048]{1,0:T(8,128)S(1)}, u32[]{:S(2)}, u32[]{:S(2)}) collective-permute-start(f32[8,2048]{1,0:T(8,128)S(1)} %shard_map.93.refs_4_), channel_id=1, source_target_pairs={{0,128},{64,192},{128,0},{192,64},{1,129},{65,193},{129,1},{193,65... | collective-permute-start | bytes 196616 | tf_op jit(solution)/shard_map/ppermute | solution.py:21
  59.7 5.8 %collective-permute-start.9 = (f32[8,2048]{1,0:T(8,128)S(1)}, f32[8,2048]{1,0:T(8,128)S(1)}, u32[]{:S(2)}, u32[]{:S(2)}) collective-permute-start(f32[8,2048]{1,0:T(8,128)S(1)} %shard_map.93.refs_4_), channel_id=1, source_target_pairs={{0,64},{64,128},{128,192},{192,0},{1,65},{65,129},{129,193},{193,1... | collective-permute-start | bytes 196616 | tf_op jit(solution)/shard_map/ppermute | solution.py:21
  70.9 1.4 %collective-permute-start.12 = (bf16[128,384]{1,0:T(8,128)(2,1)S(1)}, bf16[128,384]{1,0:T(8,128)(2,1)S(1)}, u32[]{:S(2)}, u32[]{:S(2)}) collective-permute-start(bf16[128,384]{1,0:T(8,128)(2,1)S(1)} %slice.9), channel_id=1, source_target_pairs={{0,1},{1,0},{2,3},{3,2},{4,5},{5,4},{6,7},{7,6},{8,9},{9,8},{10,11... | collective-permute-start | bytes 294920 | tf_op jit(solution)/shard_map/ppermute | solution.py:21
  71.0 9.8 %collective-permute-start.16 = (bf16[256,384]{1,0:T(8,128)(2,1)S(1)}, bf16[256,384]{1,0:T(8,128)(2,1)S(1)}, u32[]{:S(2)}, u32[]{:S(2)}) collective-permute-start(bf16[256,384]{1,0:T(8,128)(2,1)S(1)} %get-tuple-element.42.own_ref), channel_id=1, source_target_pairs={{0,64},{64,0},{128,192},{192,128},{1,65},{65,1},{129,193},{193,129... | collective-permute-start | bytes 589832 | tf_op jit(solution)/shard_map/ppermute | solution.py:206
  74.9 17.9 %collective-permute-start.13 = (bf16[32,4096]{1,0:T(8,128)(2,1)S(1)}, bf16[32,4096]{1,0:T(8,128)(2,1)S(1)}, u32[]{:S(2)}, u32[]{:S(2)}) collective-permute-start(bf16[32,4096]{1,0:T(8,128)(2,1)S(1)} %get-tuple-element.44), channel_id=1, source_target_pairs={{0,6},{2,0},{4,2},{6,4},{1,7},{3,1},{5,3},{7,5},{8,14},{10,8},{12,... | collective-permute-start | bytes 786440 | tf_op jit(solution)/shard_map/ppermute | solution.py:21
  77.1 15.7 %collective-permute-start.14 = (bf16[32,4096]{1,0:T(8,128)(2,1)S(1)}, bf16[32,4096]{1,0:T(8,128)(2,1)S(1)}, u32[]{:S(2)}, u32[]{:S(2)}) collective-permute-start(bf16[32,4096]{1,0:T(8,128)(2,1)S(1)} %get-tuple-element.45), channel_id=1, source_target_pairs={{0,4},{2,6},{4,0},{6,2},{1,5},{3,7},{5,1},{7,3},{8,12},{10,14},{12... | collective-permute-start | bytes 786440 | tf_op jit(solution)/shard_map/ppermute | solution.py:21
  79.0 15.7 %collective-permute-start.15 = (bf16[32,4096]{1,0:T(8,128)(2,1)S(1)}, bf16[32,4096]{1,0:T(8,128)(2,1)S(1)}, u32[]{:S(2)}, u32[]{:S(2)}) collective-permute-start(bf16[32,4096]{1,0:T(8,128)(2,1)S(1)} %get-tuple-element.46), channel_id=1, source_target_pairs={{0,2},{2,4},{4,6},{6,0},{1,3},{3,5},{5,7},{7,1},{8,10},{10,12},{12... | collective-permute-start | bytes 786440 | tf_op jit(solution)/shard_map/ppermute | solution.py:21
  79.0 23.7 %collective-permute-start.18 = (bf16[3,128,512]{2,1,0:T(8,128)(2,1)}, bf16[3,128,512]{2,1,0:T(8,128)(2,1)S(1)}, u32[]{:S(2)}, u32[]{:S(2)}) collective-permute-start(bf16[3,128,512]{2,1,0:T(8,128)(2,1)} %get-tuple-element.56), channel_id=1, source_target_pairs={{0,128},{64,192},{128,0},{192,64},{1,129},{65,193},{129,1},{193,65... | collective-permute-start | bytes 1179656 | tf_op jit(solution)/shard_map/ppermute | solution.py:21
  80.8 21.9 %copy-start.6 = (bf16[3,128,512]{2,1,0:T(8,128)(2,1)S(1)}, bf16[3,128,512]{2,1,0:T(8,128)(2,1)}, u32[]{:S(2)}) copy-start(bf16[3,128,512]{2,1,0:T(8,128)(2,1)} %copy-done.5) | copy-start | bytes 1179652
  80.8 24.7 %copy-start.4 = (bf16[3,128,512]{2,1,0:T(8,128)(2,1)S(1)}, bf16[3,128,512]{2,1,0:T(8,128)(2,1)}, u32[]{:S(2)}) copy-start(bf16[3,128,512]{2,1,0:T(8,128)(2,1)} %copy-done.3) | copy-start | bytes 1179652
  80.9 24.7 %copy-start.7 = (bf16[2,256,384]{2,1,0:T(8,128)(2,1)}, bf16[2,256,384]{2,1,0:T(8,128)(2,1)S(1)}, u32[]{:S(2)}) copy-start(bf16[2,256,384]{2,1,0:T(8,128)(2,1)S(1)} %pad_maximum_fusion.1.refs_0_) | copy-start | bytes 1179652
  80.9 24.6 %collective-permute-start.17 = (bf16[2,256,384]{2,1,0:T(8,128)(2,1)S(1)}, bf16[2,256,384]{2,1,0:T(8,128)(2,1)S(1)}, u32[]{:S(2)}, u32[]{:S(2)}) collective-permute-start(bf16[2,256,384]{2,1,0:T(8,128)(2,1)S(1)} %pad_maximum_fusion.1.refs_0_), channel_id=1, source_target_pairs={{0,128},{64,192},{128,0},{192,64},{1,129},{65,193},{129,1},{193,65... | collective-permute-start | bytes 1179656 | tf_op jit(solution)/shard_map/ppermute | solution.py:207
  95.6 20.4 %all-to-all-start.1 = ((bf16[8,4,4096]{2,1,0:T(4,128)(2,1)}), bf16[8,4,4096]{2,1,0:T(4,128)(2,1)S(1)}, u32[]{:S(2)}, u32[]{:S(2)}) async-start(bf16[8,4,4096]{2,1,0:T(4,128)(2,1)} %reshape.17), calls=%async_computation.1 | async-start | bytes 524288 | tf_op jit(solution)/shard_map/all_to_all | solution.py:232
  102.7 18.4 %collective-permute-start.19 = (bf16[3,128,512]{2,1,0:T(8,128)(2,1)S(1)}, bf16[3,128,512]{2,1,0:T(8,128)(2,1)S(1)}, u32[]{:S(2)}, u32[]{:S(2)}) collective-permute-start(bf16[3,128,512]{2,1,0:T(8,128)(2,1)S(1)} %copy-done.6), channel_id=1, source_target_pairs={{0,192},{64,0},{128,64},{192,128},{1,193},{65,1},{129,65},{193,129... | collective-permute-start | bytes 1179656 | tf_op jit(solution)/shard_map/ppermute | solution.py:21
  105.5 15.6 %collective-permute-start.20 = (bf16[3,128,512]{2,1,0:T(8,128)(2,1)S(1)}, bf16[3,128,512]{2,1,0:T(8,128)(2,1)S(1)}, u32[]{:S(2)}, u32[]{:S(2)}) collective-permute-start(bf16[3,128,512]{2,1,0:T(8,128)(2,1)S(1)} %copy-done.4), channel_id=1, source_target_pairs={{0,64},{64,128},{128,192},{192,0},{1,65},{65,129},{129,193},{193,1... | collective-permute-start | bytes 1179656 | tf_op jit(solution)/shard_map/ppermute | solution.py:21
  116.1 6.0 %collective-permute-start.23 = (bf16[4,4096]{1,0:T(4,128)(2,1)S(1)}, bf16[4,4096]{1,0:T(4,128)(2,1)S(1)}, u32[]{:S(2)}, u32[]{:S(2)}) collective-permute-start(bf16[4,4096]{1,0:T(4,128)(2,1)S(1)} %reduce_sum.12), channel_id=1, source_target_pairs={{0,64},{64,128},{128,192},{192,0},{1,65},{65,129},{129,193},{193,1... | collective-permute-start | bytes 98312 | tf_op jit(solution)/shard_map/ppermute | solution.py:21
  116.9 6.2 %collective-permute-start.22 = (bf16[4,4096]{1,0:T(4,128)(2,1)S(1)}, bf16[4,4096]{1,0:T(4,128)(2,1)S(1)}, u32[]{:S(2)}, u32[]{:S(2)}) collective-permute-start(bf16[4,4096]{1,0:T(4,128)(2,1)S(1)} %reduce_sum.12), channel_id=1, source_target_pairs={{0,128},{64,192},{128,0},{192,64},{1,129},{65,193},{129,1},{193,65... | collective-permute-start | bytes 98312 | tf_op jit(solution)/shard_map/ppermute | solution.py:21
  120.9 3.9 %collective-permute-start.21 = (bf16[4,4096]{1,0:T(4,128)(2,1)S(1)}, bf16[4,4096]{1,0:T(4,128)(2,1)S(1)}, u32[]{:S(2)}, u32[]{:S(2)}) collective-permute-start(bf16[4,4096]{1,0:T(4,128)(2,1)S(1)} %reduce_sum.12), channel_id=1, source_target_pairs={{0,192},{64,0},{128,64},{192,128},{1,193},{65,1},{129,65},{193,129... | collective-permute-start | bytes 98312 | tf_op jit(solution)/shard_map/ppermute | solution.py:21
  (4 other events, 10.1 us)
Sparse Core Ops, SparseCore 0:
  10.8 91.3 all-gather.1

commit v6 on v5

--- a/solution.py
+++ b/solution.py
@@ -207,7 +207,7 @@
     g_all = (g_all, lax.ppermute(g_all, "dp", [(a, a ^ 2) for a in range(dp)]))
     part = sum([part[0].astype(F32)] + [shift(part[s], "x", -s).astype(F32) for s in range(1, nx)]).astype(BF16)
 
-    block = 1024
+    block = 2048
     gw_shape = jax.ShapeDtypeStruct((layers, width, d), F32)
     gw_spec = pl.BlockSpec((layers, width, block), lambda n, at: (0, 0, n))
     grad_w = pl.pallas_call(

time: 133 us -> 132 us (level)
  no operation moved by 1% of the time
where the time goes in v6:
time: 132 us
  starting transfers between devices  44.8 us (34%)
  waiting for transfers between devices  41.3 us (31%)
  Pallas kernels  22 us (17%)
  between operations  14.2 us (11%)
  local copies, waits for them, and re-layouts  6.53 us (5%)
  other arithmetic  2.91 us (2%)
    ppermute x22, waiting for transfers between devices, shift(): return lax.ppermute(x, axis, [(a, (a + by) % n) for a in range(n)])  30.4 us
    ppermute x22, starting transfers between devices, shift(): return lax.ppermute(x, axis, [(a, (a + by) % n) for a in range(n)])  26.5 us
    all_to_all x1, waiting for transfers between devices, shards(): lax.all_to_all(jnp.broadcast_to(quarter, (nz, few, d)), 'z', 0, 0)  10.2 us
    pallas_call x1, Pallas kernels, shards(): pl.pallas_call(weights_kernel, grid_spec=pltpu.PrefetchScalarGridSpec(num...  8.83 us
    all_to_all x1, starting transfers between devices, shards(): lax.all_to_all(jnp.broadcast_to(quarter, (nz, few, d)), 'z', 0, 0)  8.57 us
    all_to_all x1, starting transfers between devices, shards(): part = lax.all_to_all(part.reshape(nz, few, d), 'z', 0, 0)  7.1 us
    pallas_call x1, Pallas kernels, shards(): pl.pallas_call(grads_kernel, out_shape=[jax.ShapeDtypeStruct((2 * half, c...  5.37 us
    pallas_call x1, Pallas kernels, shards(): pl.pallas_call(project_kernel, out_shape=(jax.ShapeDtypeStruct((half, col...  3.27 us
  transfers between devices with their start and end apart: 27, of which 13 were waited for; matrix products, arithmetic and copies ran while one was open for 5% of the time, Pallas kernels for 17%

profile of v6, /device:TPU:32, one launch (start us, length us, event | category | flops | bytes accessed | tf_op | source)
XLA Modules:
  0.0 131.7 jit_solution(3598775067850388627)
XLA Ops:
  8.5 0.9 constant_dynamic-slice_fusion
  10.1 8.6 %all-to-all-start = ((bf16[8,4,4096]{2,1,0:T(4,128)(2,1)}), bf16[8,4,4096]{2,1,0:T(4,128)(2,1)}, u32[]{:S(2)}, u32[]{:S(2)}) async-start(bf16[8,4,4096]{2,1,0:T(4,128)(2,1)} %broadcast_in_dim.3), calls=%async_computation | async-start | bytes 524288 | tf_op jit(solution)/shard_map/all_to_all | solution.py:165
  19.3 10.2 %all-to-all-done = bf16[8,4,4096]{2,1,0:T(4,128)(2,1)} async-done(((bf16[8,4,4096]{2,1,0:T(4,128)(2,1)}), bf16[8,4,4096]{2,1,0:T(4,128)(2,1)}, u32[]{:S(2)}, u32[]{:S(2)}) %all-to-all-start) | async-done | bytes 262176 | tf_op jit(solution)/shard_map/all_to_all | solution.py:165
  29.5 1.0 reshape.16.refs_0_
  30.6 2.9 %collective-permute-start.4 = (bf16[32,4096]{1,0:T(8,128)(2,1)S(1)}, bf16[32,4096]{1,0:T(8,128)(2,1)S(1)}, u32[]{:S(2)}, u32[]{:S(2)}) collective-permute-start(bf16[32,4096]{1,0:T(8,128)(2,1)S(1)} %reshape.16.refs_0_), channel_id=1, source_target_pairs={{0,6},{2,0},{4,2},{6,4},{1,7},{3,1},{5,3},{7,5},{8,14},{10,8},{12,... | collective-permute-start | bytes 786440 | tf_op jit(solution)/shard_map/ppermute | solution.py:21
  34.2 0.9 collective-permute-start.2
  35.1 1.0 pad_maximum_fusion.refs_0_
  36.1 3.1 %collective-permute-start.8 = (bf16[3,128,512]{2,1,0:T(8,128)(2,1)S(1)}, bf16[3,128,512]{2,1,0:T(8,128)(2,1)S(1)}, u32[]{:S(2)}, u32[]{:S(2)}) collective-permute-start(bf16[3,128,512]{2,1,0:T(8,128)(2,1)S(1)} %pad_maximum_fusion.refs_0_), channel_id=1, source_target_pairs={{0,192},{64,0},{128,64},{192,128},{1,193},{65,1},{129,65},{193,129... | collective-permute-start | bytes 1179656 | tf_op jit(solution)/shard_map/ppermute | solution.py:21
  39.9 3.4 %collective-permute-done.4.refs_3_ = bf16[32,4096]{1,0:T(8,128)(2,1)S(1)} collective-permute-done((bf16[32,4096]{1,0:T(8,128)(2,1)S(1)}, bf16[32,4096]{1,0:T(8,128)(2,1)S(1)}, u32[]{:S(2)}, u32[]{:S(2)}) %collective-permute-start.4) | collective-permute-done | bytes 262176 | tf_op jit(solution)/shard_map/ppermute | solution.py:21
  43.3 1.6 %collective-permute-start.6 = (bf16[3,128,512]{2,1,0:T(8,128)(2,1)S(1)}, bf16[3,128,512]{2,1,0:T(8,128)(2,1)S(1)}, u32[]{:S(2)}, u32[]{:S(2)}) collective-permute-start(bf16[3,128,512]{2,1,0:T(8,128)(2,1)S(1)} %pad_maximum_fusion.refs_0_), channel_id=1, source_target_pairs={{0,64},{64,128},{128,192},{192,0},{1,65},{65,129},{129,193},{193,1... | collective-permute-start | bytes 1179656 | tf_op jit(solution)/shard_map/ppermute | solution.py:21
  44.8 1.7 %collective-permute-done.2.refs_1_ = bf16[32,4096]{1,0:T(8,128)(2,1)S(1)} collective-permute-done((bf16[32,4096]{1,0:T(8,128)(2,1)S(1)}, bf16[32,4096]{1,0:T(8,128)(2,1)S(1)}, u32[]{:S(2)}, u32[]{:S(2)}) %collective-permute-start.2) | collective-permute-done | bytes 262176 | tf_op jit(solution)/shard_map/ppermute | solution.py:21
  46.6 1.4 %copy-done.1 = bf16[3,64,4096]{2,1,0:T(8,128)(2,1)S(1)} copy-done((bf16[3,64,4096]{2,1,0:T(8,128)(2,1)S(1)}, bf16[3,64,4096]{2,1,0:T(8,128)(2,1)}, u32[]{:S(2)}) %copy-start.1) | copy-done | bytes 1572888
  48.0 3.3 %shard_map.92 = (bf16[128,384]{1,0:T(8,128)(2,1)S(1)}, bf16[128,384]{1,0:T(8,128)(2,1)S(1)}) custom-call(bf16[3,64,4096]{2,1,0:T(8,128)(2,1)S(1)} %copy-done, bf16[3,64,4096]{2,1,0:T(8,128)(2,1)S(1)} %copy-done.1, bf16[3,64,4096]{2,1,0:T(8,128)(2,1)S(1)} %collective-permute-done.other_key, bf16[3,64,4096]{2,1,0:T(8,128)(2,1)} %collective-permute-done.1.other_value, ...), custom_call_target="tpu_custom_call" | custom-call | flops 805306368 | bytes 7340032 | tf_op jit(solution)/shard_map/pallas_call | solution.py:175
  51.4 1.3 collective-permute-done.5.other_ref
  52.7 3.7 %collective-permute-done.6.refs_1_ = bf16[3,128,512]{2,1,0:T(8,128)(2,1)S(1)} collective-permute-done((bf16[3,128,512]{2,1,0:T(8,128)(2,1)S(1)}, bf16[3,128,512]{2,1,0:T(8,128)(2,1)S(1)}, u32[]{:S(2)}, u32[]{:S(2)}) %collective-permute-start.6) | collective-permute-done | bytes 393248 | tf_op jit(solution)/shard_map/ppermute | solution.py:21
  56.4 1.9 %shard_map.93.refs_4_ = f32[8,2048]{1,0:T(8,128)S(1)} custom-call(bf16[128,384]{1,0:T(8,128)(2,1)S(1)} %get-tuple-element.39.own_ref, bf16[128,384]{1,0:T(8,128)(2,1)S(1)} %collective-permute-done.5.other_ref, bf16[3,128,512]{2,1,0:T(8,128)(2,1)S(1)} %pad_maximum_fusion.refs_0_, bf16[3,128,512]{2,1,0:T(8,128)(2,1)S(1)} %collective-permute-done.6.refs_1_, ...), custom_call_target="tpu_custom_call" | custom-call | flops 1610612736 | bytes 3145728 | tf_op jit(solution)/shard_map/pallas_call | solution.py:185
  60.5 2.2 %collective-permute-done.11.refs_7_ = f32[8,2048]{1,0:T(8,128)S(1)} collective-permute-done((f32[8,2048]{1,0:T(8,128)S(1)}, f32[8,2048]{1,0:T(8,128)S(1)}, u32[]{:S(2)}, u32[]{:S(2)}) %collective-permute-start.11) | collective-permute-done | bytes 65568 | tf_op jit(solution)/shard_map/ppermute | solution.py:21
  62.7 2.1 %collective-permute-done.10.refs_6_ = f32[8,2048]{1,0:T(8,128)S(1)} collective-permute-done((f32[8,2048]{1,0:T(8,128)S(1)}, f32[8,2048]{1,0:T(8,128)S(1)}, u32[]{:S(2)}, u32[]{:S(2)}) %collective-permute-start.10) | collective-permute-done | bytes 65568 | tf_op jit(solution)/shard_map/ppermute | solution.py:21
  65.5 5.4 %shard_map.94 = (bf16[256,384]{1,0:T(8,128)(2,1)S(1)}, bf16[3,128,512]{2,1,0:T(8,128)(2,1)S(1)}, bf16[3,128,512]{2,1,0:T(8,128)(2,1)S(1)}, bf16[3,128,512]{2,1,0:T(8,128)(2,1)}, bf16[3,128,512]{2,1,0:T(8,128)(2,1)S(1)}) custom-call(bf16[128,384]{1,0:T(8,128)(2,1)S(1)} %get-tuple-element.39.own_ref, bf16[128,384]{1,0:T(8,128)(2,1)S(1)} %collective-permute-done.5.other_ref, ...), custom_call_target="tpu_custom_call" | custom-call | flops 4831838208 | bytes 6291456 | tf_op jit(solution)/shard_map/pallas_call | solution.py:192
  72.3 2.6 %shard_map.95 = (bf16[32,4096]{1,0:T(8,128)(2,1)S(1)}, bf16[32,4096]{1,0:T(8,128)(2,1)S(1)}, bf16[32,4096]{1,0:T(8,128)(2,1)S(1)}, bf16[32,4096]{1,0:T(8,128)(2,1)S(1)}) custom-call(bf16[256,384]{1,0:T(8,128)(2,1)S(1)} %get-tuple-element.42.own_ref, bf16[128,384]{1,0:T(8,128)(2,1)S(1)} %collective-permute-done.12.other_ref, ...), custom_call_target="tpu_custom_call" | custom-call | flops 805306368 | bytes 7340032 | tf_op jit(solution)/shard_map/pallas_call | solution.py:200
  74.9 2.3 %collective-permute-start.13 = (bf16[32,4096]{1,0:T(8,128)(2,1)S(1)}, bf16[32,4096]{1,0:T(8,128)(2,1)S(1)}, u32[]{:S(2)}, u32[]{:S(2)}) collective-permute-start(bf16[32,4096]{1,0:T(8,128)(2,1)S(1)} %get-tuple-element.44), channel_id=1, source_target_pairs={{0,6},{2,0},{4,2},{6,4},{1,7},{3,1},{5,3},{7,5},{8,14},{10,8},{12,... | collective-permute-start | bytes 786440 | tf_op jit(solution)/shard_map/ppermute | solution.py:21
  77.1 1.8 %collective-permute-start.14 = (bf16[32,4096]{1,0:T(8,128)(2,1)S(1)}, bf16[32,4096]{1,0:T(8,128)(2,1)S(1)}, u32[]{:S(2)}, u32[]{:S(2)}) collective-permute-start(bf16[32,4096]{1,0:T(8,128)(2,1)S(1)} %get-tuple-element.45), channel_id=1, source_target_pairs={{0,4},{2,6},{4,0},{6,2},{1,5},{3,7},{5,1},{7,3},{8,12},{10,14},{12... | collective-permute-start | bytes 786440 | tf_op jit(solution)/shard_map/ppermute | solution.py:21
  79.0 1.9 %collective-permute-start.18 = (bf16[3,128,512]{2,1,0:T(8,128)(2,1)}, bf16[3,128,512]{2,1,0:T(8,128)(2,1)S(1)}, u32[]{:S(2)}, u32[]{:S(2)}) collective-permute-start(bf16[3,128,512]{2,1,0:T(8,128)(2,1)} %get-tuple-element.56), channel_id=1, source_target_pairs={{0,128},{64,192},{128,0},{192,64},{1,129},{65,193},{129,1},{193,65... | collective-permute-start | bytes 1179656 | tf_op jit(solution)/shard_map/ppermute | solution.py:21
  80.9 1.8 %collective-permute-start.17 = (bf16[2,256,384]{2,1,0:T(8,128)(2,1)S(1)}, bf16[2,256,384]{2,1,0:T(8,128)(2,1)S(1)}, u32[]{:S(2)}, u32[]{:S(2)}) collective-permute-start(bf16[2,256,384]{2,1,0:T(8,128)(2,1)S(1)} %pad_maximum_fusion.1.refs_0_), channel_id=1, source_target_pairs={{0,128},{64,192},{128,0},{192,64},{1,129},{65,193},{129,1},{193,65... | collective-permute-start | bytes 1179656 | tf_op jit(solution)/shard_map/ppermute | solution.py:207
  82.7 10.2 %collective-permute-done.13 = bf16[32,4096]{1,0:T(8,128)(2,1)S(1)} collective-permute-done((bf16[32,4096]{1,0:T(8,128)(2,1)S(1)}, bf16[32,4096]{1,0:T(8,128)(2,1)S(1)}, u32[]{:S(2)}, u32[]{:S(2)}) %collective-permute-start.13) | collective-permute-done | bytes 262176 | tf_op jit(solution)/shard_map/ppermute | solution.py:21
  92.8 1.8 %collective-permute-done.15 = bf16[32,4096]{1,0:T(8,128)(2,1)S(1)} collective-permute-done((bf16[32,4096]{1,0:T(8,128)(2,1)S(1)}, bf16[32,4096]{1,0:T(8,128)(2,1)S(1)}, u32[]{:S(2)}, u32[]{:S(2)}) %collective-permute-start.15) | collective-permute-done | bytes 262176 | tf_op jit(solution)/shard_map/ppermute | solution.py:21
  95.6 7.1 %all-to-all-start.1 = ((bf16[8,4,4096]{2,1,0:T(4,128)(2,1)}), bf16[8,4,4096]{2,1,0:T(4,128)(2,1)S(1)}, u32[]{:S(2)}, u32[]{:S(2)}) async-start(bf16[8,4,4096]{2,1,0:T(4,128)(2,1)} %reshape.17), calls=%async_computation.1 | async-start | bytes 524288 | tf_op jit(solution)/shard_map/all_to_all | solution.py:232
  102.7 2.8 %collective-permute-start.19 = (bf16[3,128,512]{2,1,0:T(8,128)(2,1)S(1)}, bf16[3,128,512]{2,1,0:T(8,128)(2,1)S(1)}, u32[]{:S(2)}, u32[]{:S(2)}) collective-permute-start(bf16[3,128,512]{2,1,0:T(8,128)(2,1)S(1)} %copy-done.6), channel_id=1, source_target_pairs={{0,192},{64,0},{128,64},{192,128},{1,193},{65,1},{129,65},{193,129... | collective-permute-start | bytes 1179656 | tf_op jit(solution)/shard_map/ppermute | solution.py:21
  106.3 8.8 %shard_map.96 = (f32[3,64,4096]{2,1,0:T(8,128)}, f32[3,64,4096]{2,1,0:T(8,128)}) custom-call(s32[3]{0:T(128)} %pad_add_fusion.at_ref, bf16[2,256,384]{2,1,0:T(8,128)(2,1)} %copy-done.7, bf16[2,256,384]{2,1,0:T(8,128)(2,1)} %copy-done.8, bf16[1024,4096]{1,0:T(8,128)(2,1)} %all-gather.2.cloned.1.call-done.refs_2_), custom_call_target="tpu_custom_call" | custom-call | flops 3221225472 | bytes 14680064 | tf_op jit(solution)/shard_map/pallas_call | solution.py:213
  116.1 3.9 %collective-permute-start.22 = (bf16[4,4096]{1,0:T(4,128)(2,1)S(1)}, bf16[4,4096]{1,0:T(4,128)(2,1)S(1)}, u32[]{:S(2)}, u32[]{:S(2)}) collective-permute-start(bf16[4,4096]{1,0:T(4,128)(2,1)S(1)} %reduce_sum.12), channel_id=1, source_target_pairs={{0,128},{64,192},{128,0},{192,64},{1,129},{65,193},{129,1},{193,65... | collective-permute-start | bytes 98312 | tf_op jit(solution)/shard_map/ppermute | solution.py:21
  121.2 1.0 collective-permute-done.22
  122.3 1.7 %collective-permute-done.21 = bf16[4,4096]{1,0:T(4,128)(2,1)S(1)} collective-permute-done((bf16[4,4096]{1,0:T(4,128)(2,1)S(1)}, bf16[4,4096]{1,0:T(4,128)(2,1)S(1)}, u32[]{:S(2)}, u32[]{:S(2)}) %collective-permute-start.21) | collective-permute-done | bytes 32800 | tf_op jit(solution)/shard_map/ppermute | solution.py:21
  (60 shorter events, 13.2 us)
Async XLA Ops:
  7.2 39.4 %copy-start = (bf16[3,64,4096]{2,1,0:T(8,128)(2,1)S(1)}, bf16[3,64,4096]{2,1,0:T(8,128)(2,1)}, u32[]{:S(2)}) copy-start(bf16[3,64,4096]{2,1,0:T(8,128)(2,1)} %own_key.3) | copy-start | bytes 4718596
  7.2 98.4 %all-gather.2.cloned.1.call-start = ((), (), s32[]{:S(2)}) async-start(), calls=%async_computation.2 | async-start | bytes 8519680 | tf_op jit(solution)/shard_map/all_gather | solution.py:162
  7.9 22.6 %collective-permute-start = (bf16[3,64,4096]{2,1,0:T(8,128)(2,1)}, bf16[3,64,4096]{2,1,0:T(8,128)(2,1)S(1)}, u32[]{:S(2)}, u32[]{:S(2)}) collective-permute-start(bf16[3,64,4096]{2,1,0:T(8,128)(2,1)} %own_key.3), channel_id=1, source_target_pairs={{0,1},{1,0},{2,3},{3,2},{4,5},{5,4},{6,7},{7,6},{8,9},{9,8},{10,11... | collective-permute-start | bytes 4718600 | tf_op jit(solution)/shard_map/ppermute | solution.py:21
  8.0 22.6 %collective-permute-start.1 = (bf16[3,64,4096]{2,1,0:T(8,128)(2,1)}, bf16[3,64,4096]{2,1,0:T(8,128)(2,1)}, u32[]{:S(2)}, u32[]{:S(2)}) collective-permute-start(bf16[3,64,4096]{2,1,0:T(8,128)(2,1)} %own_value.3), channel_id=1, source_target_pairs={{0,1},{1,0},{2,3},{3,2},{4,5},{5,4},{6,7},{7,6},{8,9},{9,8},{10,11... | collective-permute-start | bytes 4718600 | tf_op jit(solution)/shard_map/ppermute | solution.py:21
  10.1 19.4 %all-to-all-start = ((bf16[8,4,4096]{2,1,0:T(4,128)(2,1)}), bf16[8,4,4096]{2,1,0:T(4,128)(2,1)}, u32[]{:S(2)}, u32[]{:S(2)}) async-start(bf16[8,4,4096]{2,1,0:T(4,128)(2,1)} %broadcast_in_dim.3), calls=%async_computation | async-start | bytes 524288 | tf_op jit(solution)/shard_map/all_to_all | solution.py:165
  30.6 12.7 %collective-permute-start.4 = (bf16[32,4096]{1,0:T(8,128)(2,1)S(1)}, bf16[32,4096]{1,0:T(8,128)(2,1)S(1)}, u32[]{:S(2)}, u32[]{:S(2)}) collective-permute-start(bf16[32,4096]{1,0:T(8,128)(2,1)S(1)} %reshape.16.refs_0_), channel_id=1, source_target_pairs={{0,6},{2,0},{4,2},{6,4},{1,7},{3,1},{5,3},{7,5},{8,14},{10,8},{12,... | collective-permute-start | bytes 786440 | tf_op jit(solution)/shard_map/ppermute | solution.py:21
  33.5 11.3 %collective-permute-start.3 = (bf16[32,4096]{1,0:T(8,128)(2,1)S(1)}, bf16[32,4096]{1,0:T(8,128)(2,1)S(1)}, u32[]{:S(2)}, u32[]{:S(2)}) collective-permute-start(bf16[32,4096]{1,0:T(8,128)(2,1)S(1)} %reshape.16.refs_0_), channel_id=1, source_target_pairs={{0,4},{2,6},{4,0},{6,2},{1,5},{3,7},{5,1},{7,3},{8,12},{10,14},{12... | collective-permute-start | bytes 786440 | tf_op jit(solution)/shard_map/ppermute | solution.py:21
  34.2 12.4 %collective-permute-start.2 = (bf16[32,4096]{1,0:T(8,128)(2,1)S(1)}, bf16[32,4096]{1,0:T(8,128)(2,1)S(1)}, u32[]{:S(2)}, u32[]{:S(2)}) collective-permute-start(bf16[32,4096]{1,0:T(8,128)(2,1)S(1)} %reshape.16.refs_0_), channel_id=1, source_target_pairs={{0,2},{2,4},{4,6},{6,0},{1,3},{3,5},{5,7},{7,1},{8,10},{10,12},{12... | collective-permute-start | bytes 786440 | tf_op jit(solution)/shard_map/ppermute | solution.py:21
  36.1 16.5 %collective-permute-start.8 = (bf16[3,128,512]{2,1,0:T(8,128)(2,1)S(1)}, bf16[3,128,512]{2,1,0:T(8,128)(2,1)S(1)}, u32[]{:S(2)}, u32[]{:S(2)}) collective-permute-start(bf16[3,128,512]{2,1,0:T(8,128)(2,1)S(1)} %pad_maximum_fusion.refs_0_), channel_id=1, source_target_pairs={{0,192},{64,0},{128,64},{192,128},{1,193},{65,1},{129,65},{193,129... | collective-permute-start | bytes 1179656 | tf_op jit(solution)/shard_map/ppermute | solution.py:21
  39.2 13.4 %collective-permute-start.7 = (bf16[3,128,512]{2,1,0:T(8,128)(2,1)S(1)}, bf16[3,128,512]{2,1,0:T(8,128)(2,1)S(1)}, u32[]{:S(2)}, u32[]{:S(2)}) collective-permute-start(bf16[3,128,512]{2,1,0:T(8,128)(2,1)S(1)} %pad_maximum_fusion.refs_0_), channel_id=1, source_target_pairs={{0,128},{64,192},{128,0},{192,64},{1,129},{65,193},{129,1},{193,65... | collective-permute-start | bytes 1179656 | tf_op jit(solution)/shard_map/ppermute | solution.py:21
  43.3 13.1 %collective-permute-start.6 = (bf16[3,128,512]{2,1,0:T(8,128)(2,1)S(1)}, bf16[3,128,512]{2,1,0:T(8,128)(2,1)S(1)}, u32[]{:S(2)}, u32[]{:S(2)}) collective-permute-start(bf16[3,128,512]{2,1,0:T(8,128)(2,1)S(1)} %pad_maximum_fusion.refs_0_), channel_id=1, source_target_pairs={{0,64},{64,128},{128,192},{192,0},{1,65},{65,129},{129,193},{193,1... | collective-permute-start | bytes 1179656 | tf_op jit(solution)/shard_map/ppermute | solution.py:21
  51.3 1.4 %collective-permute-start.5 = (bf16[128,384]{1,0:T(8,128)(2,1)S(1)}, bf16[128,384]{1,0:T(8,128)(2,1)S(1)}, u32[]{:S(2)}, u32[]{:S(2)}) collective-permute-start(bf16[128,384]{1,0:T(8,128)(2,1)S(1)} %get-tuple-element.40), channel_id=1, source_target_pairs={{0,1},{1,0},{2,3},{3,2},{4,5},{5,4},{6,7},{7,6},{8,9},{9,8},{10,11... | collective-permute-start | bytes 294920 | tf_op jit(solution)/shard_map/ppermute | solution.py:21
  58.3 13.9 %copy-start.2 = (bf16[3,64,4096]{2,1,0:T(8,128)(2,1)S(1)}, bf16[3,64,4096]{2,1,0:T(8,128)(2,1)}, u32[]{:S(2)}) copy-start(bf16[3,64,4096]{2,1,0:T(8,128)(2,1)} %own_value.3) | copy-start | bytes 4718596
  58.4 4.3 %collective-permute-start.11 = (f32[8,2048]{1,0:T(8,128)S(1)}, f32[8,2048]{1,0:T(8,128)S(1)}, u32[]{:S(2)}, u32[]{:S(2)}) collective-permute-start(f32[8,2048]{1,0:T(8,128)S(1)} %shard_map.93.refs_4_), channel_id=1, source_target_pairs={{0,192},{64,0},{128,64},{192,128},{1,193},{65,1},{129,65},{193,129... | collective-permute-start | bytes 196616 | tf_op jit(solution)/shard_map/ppermute | solution.py:21
  59.0 5.8 %collective-permute-start.10 = (f32[8,2048]{1,0:T(8,128)S(1)}, f32[8,2048]{1,0:T(8,128)S(1)}, u32[]{:S(2)}, u32[]{:S(2)}) collective-permute-start(f32[8,2048]{1,0:T(8,128)S(1)} %shard_map.93.refs_4_), channel_id=1, source_target_pairs={{0,128},{64,192},{128,0},{192,64},{1,129},{65,193},{129,1},{193,65... | collective-permute-start | bytes 196616 | tf_op jit(solution)/shard_map/ppermute | solution.py:21
  59.7 5.8 %collective-permute-start.9 = (f32[8,2048]{1,0:T(8,128)S(1)}, f32[8,2048]{1,0:T(8,128)S(1)}, u32[]{:S(2)}, u32[]{:S(2)}) collective-permute-start(f32[8,2048]{1,0:T(8,128)S(1)} %shard_map.93.refs_4_), channel_id=1, source_target_pairs={{0,64},{64,128},{128,192},{192,0},{1,65},{65,129},{129,193},{193,1... | collective-permute-start | bytes 196616 | tf_op jit(solution)/shard_map/ppermute | solution.py:21
  70.9 1.4 %collective-permute-start.12 = (bf16[128,384]{1,0:T(8,128)(2,1)S(1)}, bf16[128,384]{1,0:T(8,128)(2,1)S(1)}, u32[]{:S(2)}, u32[]{:S(2)}) collective-permute-start(bf16[128,384]{1,0:T(8,128)(2,1)S(1)} %slice.9), channel_id=1, source_target_pairs={{0,1},{1,0},{2,3},{3,2},{4,5},{5,4},{6,7},{7,6},{8,9},{9,8},{10,11... | collective-permute-start | bytes 294920 | tf_op jit(solution)/shard_map/ppermute | solution.py:21
  71.0 9.8 %collective-permute-start.16 = (bf16[256,384]{1,0:T(8,128)(2,1)S(1)}, bf16[256,384]{1,0:T(8,128)(2,1)S(1)}, u32[]{:S(2)}, u32[]{:S(2)}) collective-permute-start(bf16[256,384]{1,0:T(8,128)(2,1)S(1)} %get-tuple-element.42.own_ref), channel_id=1, source_target_pairs={{0,64},{64,0},{128,192},{192,128},{1,65},{65,1},{129,193},{193,129... | collective-permute-start | bytes 589832 | tf_op jit(solution)/shard_map/ppermute | solution.py:206
  74.9 17.9 %collective-permute-start.13 = (bf16[32,4096]{1,0:T(8,128)(2,1)S(1)}, bf16[32,4096]{1,0:T(8,128)(2,1)S(1)}, u32[]{:S(2)}, u32[]{:S(2)}) collective-permute-start(bf16[32,4096]{1,0:T(8,128)(2,1)S(1)} %get-tuple-element.44), channel_id=1, source_target_pairs={{0,6},{2,0},{4,2},{6,4},{1,7},{3,1},{5,3},{7,5},{8,14},{10,8},{12,... | collective-permute-start | bytes 786440 | tf_op jit(solution)/shard_map/ppermute | solution.py:21
  77.1 15.7 %collective-permute-start.14 = (bf16[32,4096]{1,0:T(8,128)(2,1)S(1)}, bf16[32,4096]{1,0:T(8,128)(2,1)S(1)}, u32[]{:S(2)}, u32[]{:S(2)}) collective-permute-start(bf16[32,4096]{1,0:T(8,128)(2,1)S(1)} %get-tuple-element.45), channel_id=1, source_target_pairs={{0,4},{2,6},{4,0},{6,2},{1,5},{3,7},{5,1},{7,3},{8,12},{10,14},{12... | collective-permute-start | bytes 786440 | tf_op jit(solution)/shard_map/ppermute | solution.py:21
  79.0 15.7 %collective-permute-start.15 = (bf16[32,4096]{1,0:T(8,128)(2,1)S(1)}, bf16[32,4096]{1,0:T(8,128)(2,1)S(1)}, u32[]{:S(2)}, u32[]{:S(2)}) collective-permute-start(bf16[32,4096]{1,0:T(8,128)(2,1)S(1)} %get-tuple-element.46), channel_id=1, source_target_pairs={{0,2},{2,4},{4,6},{6,0},{1,3},{3,5},{5,7},{7,1},{8,10},{10,12},{12... | collective-permute-start | bytes 786440 | tf_op jit(solution)/shard_map/ppermute | solution.py:21
  79.0 23.7 %collective-permute-start.18 = (bf16[3,128,512]{2,1,0:T(8,128)(2,1)}, bf16[3,128,512]{2,1,0:T(8,128)(2,1)S(1)}, u32[]{:S(2)}, u32[]{:S(2)}) collective-permute-start(bf16[3,128,512]{2,1,0:T(8,128)(2,1)} %get-tuple-element.56), channel_id=1, source_target_pairs={{0,128},{64,192},{128,0},{192,64},{1,129},{65,193},{129,1},{193,65... | collective-permute-start | bytes 1179656 | tf_op jit(solution)/shard_map/ppermute | solution.py:21
  80.8 21.9 %copy-start.6 = (bf16[3,128,512]{2,1,0:T(8,128)(2,1)S(1)}, bf16[3,128,512]{2,1,0:T(8,128)(2,1)}, u32[]{:S(2)}) copy-start(bf16[3,128,512]{2,1,0:T(8,128)(2,1)} %copy-done.5) | copy-start | bytes 1179652
  80.8 24.7 %copy-start.4 = (bf16[3,128,512]{2,1,0:T(8,128)(2,1)S(1)}, bf16[3,128,512]{2,1,0:T(8,128)(2,1)}, u32[]{:S(2)}) copy-start(bf16[3,128,512]{2,1,0:T(8,128)(2,1)} %copy-done.3) | copy-start | bytes 1179652
  80.9 24.7 %copy-start.7 = (bf16[2,256,384]{2,1,0:T(8,128)(2,1)}, bf16[2,256,384]{2,1,0:T(8,128)(2,1)S(1)}, u32[]{:S(2)}) copy-start(bf16[2,256,384]{2,1,0:T(8,128)(2,1)S(1)} %pad_maximum_fusion.1.refs_0_) | copy-start | bytes 1179652
  80.9 24.6 %collective-permute-start.17 = (bf16[2,256,384]{2,1,0:T(8,128)(2,1)S(1)}, bf16[2,256,384]{2,1,0:T(8,128)(2,1)S(1)}, u32[]{:S(2)}, u32[]{:S(2)}) collective-permute-start(bf16[2,256,384]{2,1,0:T(8,128)(2,1)S(1)} %pad_maximum_fusion.1.refs_0_), channel_id=1, source_target_pairs={{0,128},{64,192},{128,0},{192,64},{1,129},{65,193},{129,1},{193,65... | collective-permute-start | bytes 1179656 | tf_op jit(solution)/shard_map/ppermute | solution.py:207
  95.6 19.5 %all-to-all-start.1 = ((bf16[8,4,4096]{2,1,0:T(4,128)(2,1)}), bf16[8,4,4096]{2,1,0:T(4,128)(2,1)S(1)}, u32[]{:S(2)}, u32[]{:S(2)}) async-start(bf16[8,4,4096]{2,1,0:T(4,128)(2,1)} %reshape.17), calls=%async_computation.1 | async-start | bytes 524288 | tf_op jit(solution)/shard_map/all_to_all | solution.py:232
  102.7 17.5 %collective-permute-start.19 = (bf16[3,128,512]{2,1,0:T(8,128)(2,1)S(1)}, bf16[3,128,512]{2,1,0:T(8,128)(2,1)S(1)}, u32[]{:S(2)}, u32[]{:S(2)}) collective-permute-start(bf16[3,128,512]{2,1,0:T(8,128)(2,1)S(1)} %copy-done.6), channel_id=1, source_target_pairs={{0,192},{64,0},{128,64},{192,128},{1,193},{65,1},{129,65},{193,129... | collective-permute-start | bytes 1179656 | tf_op jit(solution)/shard_map/ppermute | solution.py:21
  105.5 14.7 %collective-permute-start.20 = (bf16[3,128,512]{2,1,0:T(8,128)(2,1)S(1)}, bf16[3,128,512]{2,1,0:T(8,128)(2,1)S(1)}, u32[]{:S(2)}, u32[]{:S(2)}) collective-permute-start(bf16[3,128,512]{2,1,0:T(8,128)(2,1)S(1)} %copy-done.4), channel_id=1, source_target_pairs={{0,64},{64,128},{128,192},{192,0},{1,65},{65,129},{129,193},{193,1... | collective-permute-start | bytes 1179656 | tf_op jit(solution)/shard_map/ppermute | solution.py:21
  115.2 6.0 %collective-permute-start.23 = (bf16[4,4096]{1,0:T(4,128)(2,1)S(1)}, bf16[4,4096]{1,0:T(4,128)(2,1)S(1)}, u32[]{:S(2)}, u32[]{:S(2)}) collective-permute-start(bf16[4,4096]{1,0:T(4,128)(2,1)S(1)} %reduce_sum.12), channel_id=1, source_target_pairs={{0,64},{64,128},{128,192},{192,0},{1,65},{65,129},{129,193},{193,1... | collective-permute-start | bytes 98312 | tf_op jit(solution)/shard_map/ppermute | solution.py:21
  116.1 6.2 %collective-permute-start.22 = (bf16[4,4096]{1,0:T(4,128)(2,1)S(1)}, bf16[4,4096]{1,0:T(4,128)(2,1)S(1)}, u32[]{:S(2)}, u32[]{:S(2)}) collective-permute-start(bf16[4,4096]{1,0:T(4,128)(2,1)S(1)} %reduce_sum.12), channel_id=1, source_target_pairs={{0,128},{64,192},{128,0},{192,64},{1,129},{65,193},{129,1},{193,65... | collective-permute-start | bytes 98312 | tf_op jit(solution)/shard_map/ppermute | solution.py:21
  120.0 3.9 %collective-permute-start.21 = (bf16[4,4096]{1,0:T(4,128)(2,1)S(1)}, bf16[4,4096]{1,0:T(4,128)(2,1)S(1)}, u32[]{:S(2)}, u32[]{:S(2)}) collective-permute-start(bf16[4,4096]{1,0:T(4,128)(2,1)S(1)} %reduce_sum.12), channel_id=1, source_target_pairs={{0,192},{64,0},{128,64},{192,128},{1,193},{65,1},{129,65},{193,129... | collective-permute-start | bytes 98312 | tf_op jit(solution)/shard_map/ppermute | solution.py:21
  (4 other events, 10.1 us)
Sparse Core Ops, SparseCore 0:
  10.8 91.3 all-gather.1
